TPU v7x, 256 devices: a whole 4x4x8 slice. The times are simulated.
256 devices in a mesh: scan: 32 (over z_hi, x, core), band: 8 (over z_lo, y).
Axes of the slice: x: 4, y: 4, z: 8 (z_hi: 4, z_lo: 2; z = z_hi * 2 + z_lo), core: 2. Of those that a mesh axis runs over, the one named last changes fastest.
Arguments:
- frame_codes: bfloat16 [2048, 576, 576], P('scan', 'band'), may hold values from 0.049804688 to 1
- row_scales: float32 [2048, 576], P('scan', 'band'), may hold values from 0.3 to 9
- row_shift: int32 [2048], P('scan'), may hold values from -9 to 9
- col_shift: int32 [2048], P('scan'), may hold values from -72 to 72
- segment_labels: int32 [576, 576], P('band'), may hold values from 0 to 127, as said below
- mask_coeffs: float32 [3, 128, 512], replicated, may hold values from -72 to 72
Outputs:
- virtual: float32 [2048, 512], P('scan', 'band')
Inputs may be any that keep to these rules, and one draw needn't show every extreme that they name: `segment_labels`: every segment number occurs.
All inputs are finite; a program needn't handle non-finite values.
Results may differ from a plain program's by a relative error of at most 0.0003.
Values may be sent and summed in bfloat16 or wider, within the bound.
No kernel may reach another device: no remote copies, remote signals or barrier semaphores. Data moves between devices by JAX's collectives and lax.ppermute only.
A program may use at most 192 MiB of HBM per device.

v0:
```python
import math

import jax
import jax.numpy as jnp
from jax import lax
from jax.sharding import PartitionSpec as P

MASKS = 512
SEGS = 128


def extended(block, sides, width):
    for axis, dim in sides:
        count = lax.axis_size(axis)
        forward = [(i, i + 1) for i in range(count - 1)]
        backward = [(target, source) for source, target in forward]
        low = lax.ppermute(
            lax.slice_in_dim(block, block.shape[dim] - width, None, axis=dim), axis, forward
        )
        high = lax.ppermute(lax.slice_in_dim(block, 0, width, axis=dim), axis, backward)
        block = jnp.concatenate([low, block, high], axis=dim)
    return block


def basis_table(labels, first_row, det_size):
    row_total, col_total = labels.shape
    global_rows = first_row + jnp.arange(row_total, dtype=jnp.int32)
    inside = ((global_rows >= 0) & (global_rows < det_size)).astype(jnp.float32)
    ycoord = (global_rows.astype(jnp.float32) + 0.5) / det_size - 0.5
    xcoord = (jnp.arange(col_total, dtype=jnp.int32).astype(jnp.float32) + 0.5) / det_size - 0.5
    plane = jnp.ones((row_total, col_total), jnp.float32) * inside[:, None]
    basis = jnp.stack([plane, plane * ycoord[:, None], plane * xcoord[None, :]], axis=-1).astype(
        jnp.bfloat16
    )
    onehot = (labels[:, :, None] == jnp.arange(SEGS, dtype=jnp.int32)).astype(jnp.bfloat16)
    table = basis[:, :, :, None] * onehot[:, :, None, :]
    return table.reshape(row_total * col_total, 3 * SEGS)


def shift_frames(frames, row_offset, col_step, out_rows):
    frame_count, src_rows, det_cols = frames.shape
    group = math.gcd(frame_count, 16)
    turns = frame_count // group

    def shift_group(items):
        block, offsets, steps = items
        src_index = jnp.arange(src_rows, dtype=jnp.int32)
        dst_index = jnp.arange(out_rows, dtype=jnp.int32)
        row_pick = (
            src_index[None, None, :] == dst_index[None, :, None] + offsets[:, None, None]
        ).astype(jnp.bfloat16)
        rowed = jnp.einsum(
            "fst,ftc->fsc", row_pick, block, preferred_element_type=jnp.float32
        ).astype(jnp.bfloat16)
        col_index = jnp.arange(det_cols, dtype=jnp.int32)
        col_pick = (
            col_index[None, None, :] == col_index[None, :, None] + steps[:, None, None]
        ).astype(jnp.bfloat16)
        return jnp.einsum(
            "fsc,fcd->fsd", rowed, col_pick, preferred_element_type=jnp.float32
        ).astype(jnp.bfloat16)

    shifted = lax.map(
        shift_group,
        (
            frames.reshape(turns, group, src_rows, det_cols),
            row_offset.reshape(turns, group),
            col_step.reshape(turns, group),
        ),
    )
    return shifted.reshape(frame_count, out_rows, det_cols)


def body(frame_codes, row_scales, row_shift, col_shift, segment_labels, mask_coeffs):
    frame_count, band_height, det_cols = frame_codes.shape
    band_index = lax.axis_index("band")
    first_row = band_index * band_height
    row_reach = band_height // 8
    dequant = (frame_codes.astype(jnp.float32) * row_scales[:, :, None]).astype(jnp.bfloat16)
    padded = extended(dequant, (("band", 1),), row_reach)
    moved = shift_frames(padded, row_reach - row_shift, col_shift, band_height)
    table = basis_table(segment_labels, first_row, det_cols)
    flat = moved.reshape(frame_count, band_height * det_cols)
    partials = jnp.dot(flat, table, preferred_element_type=jnp.float32)
    intensity_sum = lax.psum(jnp.sum(partials[:, :SEGS]), ("scan", "band"))
    mean_total = intensity_sum / (frame_count * lax.axis_size("scan"))
    coeff_table = mask_coeffs.reshape(3 * SEGS, MASKS)
    summed = lax.psum(partials, "band")
    mask_width = MASKS // lax.axis_size("band")
    own_cols = lax.dynamic_slice_in_dim(coeff_table, band_index * mask_width, mask_width, 1)
    virtual = (
        jnp.dot(
            summed, own_cols, precision=lax.Precision.HIGHEST, preferred_element_type=jnp.float32
        )
        / mean_total
    )
    return virtual


def solution(mesh):
    return jax.shard_map(
        body,
        mesh=mesh,
        in_specs=(
            P("scan", "band", None),
            P("scan", "band"),
            P("scan"),
            P("scan"),
            P("band", None),
            P(),
        ),
        out_specs=P("scan", "band"),
        check_vma=False,
    )
```

profile of v0, /device:TPU:6, one launch (start us, length us, event | category | flops | bytes accessed | tf_op | source)
XLA Modules:
  0.0 251.9 jit_solution(11607539573301819624)
XLA Ops:
  6.5 0.0 copy-start
  6.5 0.9 copy.8
  7.4 0.0 copy-start.3
  7.5 5.6 %multiply_convert_fusion = bf16[64,72,576]{2,0,1:T(8,128)(2,1)S(1)} fusion(bf16[64,72,576]{2,1,0:T(8,128)(2,1)} %param.8, f32[64,72]{0,1:T(8,128)S(1)} %copy.8), kind=kLoop, calls=%fused_computation.20 | loop fusion | flops 7962624 | bytes 10635264 | tf_op jit(solution)/shard_map/convert_element_type | solution.py:79
  13.1 0.0 copy-start.1
  13.1 2.6 %copy-done.1 = bf16[64,72,576]{2,0,1:T(8,128)(2,1)} copy-done((bf16[64,72,576]{2,0,1:T(8,128)(2,1)}, bf16[64,72,576]{2,0,1:T(8,128)(2,1)S(1)}, u32[]{:S(2)}) %copy-start.1) | copy-done | bytes 5308440
  15.6 1.0 fusion.14
  16.7 3.5 %collective-permute-start = (bf16[64,9,576]{2,0,1:T(8,128)(2,1)}, bf16[64,9,576]{2,0,1:T(8,128)(2,1)S(1)}, u32[]{:S(2)}, u32[]{:S(2)}) collective-permute-start(bf16[64,9,576]{2,0,1:T(8,128)(2,1)} %get-tuple-element.50), channel_id=1, source_target_pairs={{0,1},{1,2},{2,3},{3,4},{4,5},{5,6},{6,7},{8,9},{9,10},{10,11},{11... | collective-permute-start | bytes 1990664 | tf_op jit(solution)/shard_map/ppermute | solution.py:17
  20.2 1.3 collective-permute-start.1
  21.6 0.0 copy-done.3
  21.6 7.0 %fusion.9 = bf16[72,576,128]{1,0,2:T(8,128)(2,1)} fusion(s32[72,576]{1,0:T(8,128)S(1)} %copy-done.3), kind=kLoop, calls=%fused_computation.18 | loop fusion | flops 10616832 | bytes 10782720 | tf_op jit(solution)/shard_map/convert_element_type | solution.py:35
  28.5 0.1 multiply_convert_fusion.1
  28.6 0.1 stack.12
  28.7 0.1 stack.13
  28.8 15.1 %broadcast_multiply_fusion = bf16[72,576,3,128]{1,0,3,2:T(8,128)(2,1)} fusion(bf16[72,576,128]{1,0,2:T(8,128)(2,1)} %fusion.9, bf16[72,576,3]{1,0,2:T(8,128)(2,1)S(1)} %pad_maximum_fusion.1), kind=kLoop, calls=%fused_computation.19 | loop fusion | flops 15925248 | bytes 42716160 | tf_op jit(solution)/shard_map/mul | solution.py:36
  43.9 0.0 copy-start.4
  43.9 47.7 %mul.73 = bf16[41472,384]{0,1:T(8,128)(2,1)} reshape(bf16[72,576,3,128]{1,0,3,2:T(8,128)(2,1)} %broadcast_multiply_fusion) | data formatting | bytes 63700992 | tf_op jit(solution)/shard_map/mul | solution.py:36
  91.7 0.1 reshape.174
  91.8 0.1 reshape.176
  91.8 0.0 collective-permute-done
  91.8 0.0 collective-permute-done.1
  91.8 6.5 %pad_maximum_fusion = bf16[64,90,576]{2,0,1:T(8,128)(2,1)} fusion(bf16[64,9,576]{2,0,1:T(8,128)(2,1)S(1)} %collective-permute-done.1, bf16[64,72,576]{2,0,1:T(8,128)(2,1)} %copy-done.1, bf16[64,9,576]{2,0,1:T(8,128)(2,1)S(1)} %collective-permute-done), kind=kLoop, calls=%fused_computation.21 | loop fusion | flops 6635520 | bytes 13271040 | tf_op jit(solution)/shard_map/concatenate | solution.py:21
  98.4 34.5 %while.10 = (s32[]{:T(128)}, bf16[4,16,72,576]{3,2,1,0:T(8,128)(2,1)}, s32[4,16]{1,0:T(4,128)S(1)}, bf16[4,16,90,576]{3,1,0,2:T(8,128)(2,1)}, s32[4,16]{1,0:T(4,128)S(1)}, /*index=5*/s32[]{:T(128)}) while((s32[]{:T(128)}, bf16[4,16,72,576]{3,2,1,0:T(8,128)(2,1)}, s32[4,16]{1,0:T(4,128)S(1)}, bf16[4,16,90,576]{3,1,0,2:T(8,128)(2,1)}, ...), condition=%wide.region_1.2_spmd, body=%wide.region_0.1_spmd.sunk | while | flops 890600832 | bytes 6535117 | solution.py:63
  98.4 0.1 iota_add_fusion.5
  98.5 0.1 iota_add_fusion.6
  98.5 1.7 constant_dynamic-slice_fusion.4
  100.2 6.8 %bitcast_dynamic-update-slice_fusion.2 = bf16[4,16,72,576]{3,2,1,0:T(8,128)(2,1)} fusion(bf16[4,16,72,576]{3,2,1,0:T(8,128)(2,1)} %get-tuple-element.96, s32[]{:T(128)} %get-tuple-element.95, s32[16,576]{1,0:T(8,128)S(1)} %iota_add_fusion.5, bf16[1,16,90,576]{3,1,0,2:T(8,128)(2,1)S(1)} %constant_dynamic-slice_fusion.4, s32[16,72]{1,0:T(8,128)S(1)} %iota_add_fusion.6), kind=kOutput, calls=%fused_computation.7.clone.1 | convolution fusion | flops 890590464 | bytes 3175424 | tf_op jit(solution)/shard_map/while/body/eval_jaxpr/fsc,fcd->fsd/dot_general | solution.py:59
  107.0 0.1 iota_add_fusion.5
  107.1 0.1 iota_add_fusion.6
  107.1 1.7 constant_dynamic-slice_fusion.4
  108.8 6.8 %bitcast_dynamic-update-slice_fusion.2 = bf16[4,16,72,576]{3,2,1,0:T(8,128)(2,1)} fusion(bf16[4,16,72,576]{3,2,1,0:T(8,128)(2,1)} %get-tuple-element.96, s32[]{:T(128)} %get-tuple-element.95, s32[16,576]{1,0:T(8,128)S(1)} %iota_add_fusion.5, bf16[1,16,90,576]{3,1,0,2:T(8,128)(2,1)S(1)} %constant_dynamic-slice_fusion.4, s32[16,72]{1,0:T(8,128)S(1)} %iota_add_fusion.6), kind=kOutput, calls=%fused_computation.7.clone.1 | convolution fusion | flops 890590464 | bytes 3175424 | tf_op jit(solution)/shard_map/while/body/eval_jaxpr/fsc,fcd->fsd/dot_general | solution.py:59
  115.6 0.1 iota_add_fusion.5
  115.7 0.1 iota_add_fusion.6
  115.8 1.7 constant_dynamic-slice_fusion.4
  117.5 6.8 %bitcast_dynamic-update-slice_fusion.2 = bf16[4,16,72,576]{3,2,1,0:T(8,128)(2,1)} fusion(bf16[4,16,72,576]{3,2,1,0:T(8,128)(2,1)} %get-tuple-element.96, s32[]{:T(128)} %get-tuple-element.95, s32[16,576]{1,0:T(8,128)S(1)} %iota_add_fusion.5, bf16[1,16,90,576]{3,1,0,2:T(8,128)(2,1)S(1)} %constant_dynamic-slice_fusion.4, s32[16,72]{1,0:T(8,128)S(1)} %iota_add_fusion.6), kind=kOutput, calls=%fused_computation.7.clone.1 | convolution fusion | flops 890590464 | bytes 3175424 | tf_op jit(solution)/shard_map/while/body/eval_jaxpr/fsc,fcd->fsd/dot_general | solution.py:59
  124.2 0.1 iota_add_fusion.5
  124.3 0.1 iota_add_fusion.6
  124.4 1.7 constant_dynamic-slice_fusion.4
  126.1 6.8 %bitcast_dynamic-update-slice_fusion.2 = bf16[4,16,72,576]{3,2,1,0:T(8,128)(2,1)} fusion(bf16[4,16,72,576]{3,2,1,0:T(8,128)(2,1)} %get-tuple-element.96, s32[]{:T(128)} %get-tuple-element.95, s32[16,576]{1,0:T(8,128)S(1)} %iota_add_fusion.5, bf16[1,16,90,576]{3,1,0,2:T(8,128)(2,1)S(1)} %constant_dynamic-slice_fusion.4, s32[16,72]{1,0:T(8,128)S(1)} %iota_add_fusion.6), kind=kOutput, calls=%fused_computation.7.clone.1 | convolution fusion | flops 890590464 | bytes 3175424 | tf_op jit(solution)/shard_map/while/body/eval_jaxpr/fsc,fcd->fsd/dot_general | solution.py:59
  132.9 8.9 %reshape_reshape.3 = bf16[64,41472]{1,0:T(8,128)(2,1)} reshape(bf16[4,16,72,576]{3,2,1,0:T(8,128)(2,1)} %get-tuple-element.32) | data formatting | bytes 10616832 | tf_op jit(solution)/shard_map/reshape;reshape | solution.py:83
  141.7 16.9 %fusion.15 = f32[64,384]{1,0:T(8,128)S(1)} fusion(bf16[64,41472]{1,0:T(8,128)(2,1)} %reshape_reshape.3, bf16[41472,384]{0,1:T(8,128)(2,1)} %mul.73), kind=kOutput, calls=%fused_computation.36 | convolution fusion | flops 2038431744 | bytes 37257216 | tf_op jit(solution)/shard_map/dot_general | solution.py:84
  158.7 0.6 slice_reduce_fusion
  159.3 0.0 copy-done.2
  159.3 0.7 all-reduce.2.cloned.1.call-update
  160.0 81.4 %psum.15 = f32[]{:T(128)} all-reduce(f32[]{:T(128)} %slice_reduce_fusion), channel_id=1, replica_groups=mesh['scan'=32,'band'=8] {'scan','band'}, use_global_device_ids=true, to_apply=%region_4.5 | all-reduce | flops 1 | bytes 8 | tf_op jit(solution)/shard_map/psum | solution.py:85
  242.1 1.1 all-reduce.2.cloned.1.call-done
  243.2 0.0 copy-done
  243.2 1.8 convolution_divide_fusion
  (15 shorter events, 0.1 us)
Async XLA Ops:
  6.5 236.7 %copy-start = (f32[3,128,512]{2,1,0:T(8,128)S(1)}, f32[3,128,512]{2,1,0:T(8,128)}, u32[]{:S(2)}) copy-start(f32[3,128,512]{2,1,0:T(8,128)} %param.13) | copy-start | bytes 2359300
  7.4 14.1 %copy-start.3 = (s32[72,576]{1,0:T(8,128)S(1)}, s32[72,576]{1,0:T(8,128)}, u32[]{:S(2)}) copy-start(s32[72,576]{1,0:T(8,128)} %param.12) | copy-start | bytes 497668
  13.1 2.6 %copy-start.1 = (bf16[64,72,576]{2,0,1:T(8,128)(2,1)}, bf16[64,72,576]{2,0,1:T(8,128)(2,1)S(1)}, u32[]{:S(2)}) copy-start(bf16[64,72,576]{2,0,1:T(8,128)(2,1)S(1)} %multiply_convert_fusion) | copy-start | bytes 15925252
  16.7 75.2 %collective-permute-start = (bf16[64,9,576]{2,0,1:T(8,128)(2,1)}, bf16[64,9,576]{2,0,1:T(8,128)(2,1)S(1)}, u32[]{:S(2)}, u32[]{:S(2)}) collective-permute-start(bf16[64,9,576]{2,0,1:T(8,128)(2,1)} %get-tuple-element.50), channel_id=1, source_target_pairs={{0,1},{1,2},{2,3},{3,4},{4,5},{5,6},{6,7},{8,9},{9,10},{10,11},{11... | collective-permute-start | bytes 1990664 | tf_op jit(solution)/shard_map/ppermute | solution.py:17
  20.2 71.6 %collective-permute-start.1 = (bf16[64,9,576]{2,0,1:T(8,128)(2,1)S(1)}, bf16[64,9,576]{2,0,1:T(8,128)(2,1)S(1)}, u32[]{:S(2)}, u32[]{:S(2)}) collective-permute-start(bf16[64,9,576]{2,0,1:T(8,128)(2,1)S(1)} %get-tuple-element.51), channel_id=1, source_target_pairs={{1,0},{2,1},{3,2},{4,3},{5,4},{6,5},{7,6},{9,8},{10,9},{11,10},{12... | collective-permute-start | bytes 1990664 | tf_op jit(solution)/shard_map/ppermute | solution.py:20
  43.9 47.7 %copy-start.5 = (s32[64]{0:T(128)S(1)}, s32[64]{0:T(128)}, u32[]{:S(2)}) copy-start(s32[64]{0:T(128)} %param.10) | copy-start | bytes 772
  43.9 47.8 %copy-start.4 = (s32[64]{0:T(128)S(1)}, s32[64]{0:T(128)}, u32[]{:S(2)}) copy-start(s32[64]{0:T(128)} %param.11) | copy-start | bytes 772
  158.7 0.6 copy-start.2
  159.3 83.9 %all-reduce.2.cloned.1.call-start = ((), (), s32[]{:S(2)}) async-start(), calls=%async_computation | async-start | bytes 196608 | tf_op jit(solution)/shard_map/psum | solution.py:88
Sparse Core Ops, SparseCore 0:
  162.7 80.4 all-reduce.1
where the time goes:
time: 254 us; the launch traced here: 252 us
  blocking collectives  81.4 us (32%)
  local copies, waits for them, and re-layouts  68.2 us (27%)
  matrix products  45.9 us (18%)
  other arithmetic  35.5 us (14%)
  between operations  14.2 us (6%)
  starting transfers between devices  4.81 us (2%)
    psum x1, blocking collectives, body(): intensity_sum = lax.psum(jnp.sum(partials[:, :SEGS]), ('scan', 'band'))  81.4 us
    mul x1, local copies, waits for them, and re-layouts, basis_table(): table = basis[:, :, :, None] * onehot[:, :, None, :]  47.7 us
    dot_general x4, matrix products, shift_group(): jnp.einsum('fsc,fcd->fsd', rowed, col_pick, preferred_element_type=jnp.fl...  27.2 us
    dot_general x1, matrix products, body(): partials = jnp.dot(flat, table, preferred_element_type=jnp.float32)  16.9 us
    mul x1, other arithmetic, basis_table(): table = basis[:, :, :, None] * onehot[:, :, None, :]  15.1 us
    another operation x1, local copies, waits for them, and re-layouts, body(): flat = moved.reshape(frame_count, band_height * det_cols)  8.89 us
    convert_element_type x1, other arithmetic, basis_table(): (labels[:, :, None] == jnp.arange(SEGS, dtype=jnp.int32)).astype(jnp.bflo...  6.97 us
    dynamic_slice x4, local copies, waits for them, and re-layouts, shift_frames(): lax.map(shift_group, (frames.reshape(turns, group, src_rows, det_cols), r...  6.7 us
  transfers between devices with their start and end apart: 3, of which 1 were waited for; matrix products, arithmetic and copies ran while one was open for 28% of the time, Pallas kernels for 0%

commit v1 on v0

v1 whole, which is shorter than its diff:
```python
import functools

import jax
import jax.numpy as jnp
from jax import lax
from jax.experimental import pallas as pl
from jax.experimental.pallas import tpu as pltpu
from jax.sharding import PartitionSpec as P

MASKS = 512
SEGS = 128
LANES = 128
MIB = 2**20
VMEM = pl.BlockSpec(memory_space=pltpu.VMEM)
SMEM = pl.BlockSpec(memory_space=pltpu.SMEM)


class Sizes:
    def __init__(self, frame_count, band_height, det_cols):
        self.frames = frame_count
        self.rows = band_height
        self.cols = det_cols
        self.reach = band_height // 8
        self.ext = band_height + 2 * self.reach
        self.tiles = -(-det_cols // LANES)
        self.width = self.tiles * LANES
        self.pitch = frame_count + 8


def shift_kernel(size, row_shift, col_shift, scales, codes, moved, total, split, spread, acc):
    frames, rows, cols, tiles = size.frames, size.rows, size.cols, size.tiles
    empty = jnp.zeros((frames, LANES), jnp.float32)

    def clear(e, carry):
        for t in range(tiles):
            moved[t, pl.ds(pl.multiple_of(e * size.pitch, 8), frames), :] = empty
            moved[t, pl.ds(pl.multiple_of((e + rows) * size.pitch, 8), frames), :] = empty
        return carry

    lax.fori_loop(0, 2 * size.reach, clear, 0, unroll=3)

    scale = jnp.concatenate(
        [scales[...], jnp.zeros((frames, LANES - rows), jnp.float32)], axis=1
    )
    high = scale.astype(jnp.bfloat16).astype(jnp.float32)
    middle = (scale - high).astype(jnp.bfloat16).astype(jnp.float32)
    split[0:frames, :] = high
    split[frames : 2 * frames, :] = middle
    split[2 * frames : 3 * frames, :] = scale - high - middle
    acc[...] = jnp.zeros((rows, LANES), jnp.float32)

    lane = lax.broadcasted_iota(jnp.int32, (rows, LANES), 1)
    row = lax.broadcasted_iota(jnp.int32, (rows, LANES), 0)
    diagonal = lane == row
    ones = jnp.ones((3 * LANES, LANES), jnp.bfloat16)
    zero = jnp.zeros((rows, LANES), jnp.float32)
    first_row = lax.axis_index("band") * rows

    def spread_frame(f, carry):
        parts = [
            jnp.where(
                diagonal,
                jnp.broadcast_to(split[pl.ds(f + k * frames, 1), :], (rows, LANES)),
                0.0,
            ).astype(jnp.bfloat16)
            for k in range(3)
        ]
        spread[pl.ds(pl.multiple_of(f * rows, 8), rows), :] = jnp.dot(
            jnp.concatenate(parts, axis=1), ones, preferred_element_type=jnp.float32
        )
        return carry

    lax.fori_loop(0, frames, spread_frame, 0, unroll=16)

    def shift_frame(f, carry):
        down, right = row_shift[f], col_shift[f]
        turn = jnp.where(right < 0, right + LANES, right)
        positive = right >= 0
        below = lane < turn
        from_left = below & positive
        from_right = jnp.logical_not(below | positive)
        scale_f = spread[pl.ds(pl.multiple_of(f * rows, 8), rows), :]
        turned = [zero]
        for t in range(tiles):
            upper = min(cols, (t + 1) * LANES)
            value = codes[f, :, t * LANES : upper].astype(jnp.float32)
            if upper < (t + 1) * LANES:
                fill = jnp.zeros((rows, (t + 1) * LANES - upper), jnp.float32)
                value = jnp.concatenate([value, fill], axis=1)
            dequant = (value * scale_f).astype(jnp.bfloat16).astype(jnp.float32)
            turned.append(pltpu.roll(dequant, turn, 1))
        turned.append(zero)
        start = (size.reach + down) * size.pitch + f
        row_sum = zero
        for t in range(tiles):
            out = jnp.where(
                from_left, turned[t], jnp.where(from_right, turned[t + 2], turned[t + 1])
            )
            if (t + 1) * LANES > cols:
                out = jnp.where(lane < cols - t * LANES, out, 0.0)
            moved[t, pl.ds(start, rows, stride=size.pitch), :] = out
            row_sum = row_sum + out
        target = row + (first_row + down)
        acc[...] += jnp.where((target >= 0) & (target < cols), row_sum, 0.0)
        return carry

    lax.fori_loop(0, frames, shift_frame, 0, unroll=4)
    total[...] = jnp.sum(acc[...].reshape(rows // 8, 8, LANES), axis=0)


def shift_frames(size, row_shift, col_shift, scales, codes):
    return pl.pallas_call(
        functools.partial(shift_kernel, size),
        out_shape=[
            jax.ShapeDtypeStruct((size.tiles, size.ext * size.pitch, LANES), jnp.float32),
            jax.ShapeDtypeStruct((8, LANES), jnp.float32),
        ],
        in_specs=[SMEM, SMEM, VMEM, VMEM],
        out_specs=[VMEM, VMEM],
        scratch_shapes=[
            pltpu.VMEM((3 * size.frames, LANES), jnp.float32),
            pltpu.VMEM((size.frames * size.rows, LANES), jnp.float32),
            pltpu.VMEM((size.rows, LANES), jnp.float32),
        ],
        compiler_params=pltpu.CompilerParams(vmem_limit_bytes=16 * MIB),
        cost_estimate=pl.CostEstimate(flops=4 * 10**9, bytes_accessed=10**6, transcendentals=0),
        name="shift",
    )(row_shift, col_shift, scales, codes)


def table_consts(size):
    segment = lax.broadcasted_iota(jnp.int32, (16, size.width), 0)
    column = lax.broadcasted_iota(jnp.int32, (16, size.width), 1).astype(jnp.float32)
    xcoord = ((column + 0.5) / size.cols - 0.5).astype(jnp.bfloat16)
    ids = [
        (segment + 16 * k).astype(jnp.float32).astype(jnp.bfloat16) for k in range(SEGS // 16)
    ]
    return ids, xcoord


def add_row(size, consts, label_row, moved, moments, e):
    ids, xcoord = consts
    frames = size.frames
    zero = jnp.zeros((16, size.width), jnp.bfloat16)
    one = jnp.ones((16, size.width), jnp.bfloat16)
    label = jnp.broadcast_to(label_row, (16, size.width)).astype(jnp.bfloat16)
    plain, by_x = [], []
    for k in range(SEGS // 16):
        same = label == ids[k]
        plain.append(jnp.where(same, one, zero))
        by_x.append(jnp.where(same, xcoord, zero))
    table = jnp.concatenate(plain + by_x, axis=0)
    base = pl.multiple_of(e * size.pitch, 8)
    values = jnp.concatenate(
        [moved[t, pl.ds(base, frames), :].astype(jnp.bfloat16) for t in range(size.tiles)], axis=1
    )
    sums = lax.dot_general(
        table, values, (((1,), (1,)), ((), ())), preferred_element_type=jnp.float32
    )
    first_row = lax.axis_index("band") * size.rows
    offset = (first_row + e - size.reach).astype(jnp.float32)
    ycoord = ((offset + 0.5) / size.cols - 0.5).astype(jnp.bfloat16).astype(jnp.float32)
    moments[0:SEGS, :] += sums[0:SEGS]
    moments[SEGS : 2 * SEGS, :] += sums[0:SEGS] * ycoord
    moments[2 * SEGS : 3 * SEGS, :] += sums[SEGS : 2 * SEGS]


def widen(size, labels, out, at, count, start):
    rows = labels[pl.ds(start, count), :].astype(jnp.float32)
    fill = jnp.full((count, size.width - size.cols), -1.0, jnp.float32)
    out[pl.ds(at, count), :] = jnp.concatenate([rows, fill], axis=1)


def core_kernel(size, first, last, started, *refs):
    if started:
        labels, moved, before, moments, wide = refs
        moments[...] = before[...]
    else:
        labels, moved, moments, wide = refs
        moments[...] = jnp.zeros(moments.shape, jnp.float32)
    widen(size, labels, wide, 0, size.rows, 0)
    consts = table_consts(size)

    def step(r, carry):
        add_row(size, consts, wide[pl.ds(r, 1), :], moved, moments, r + size.reach)
        return carry

    lax.fori_loop(first, last, step, 0, unroll=12)


def core_rows(size, labels, moved, before, first, last):
    args = [labels, moved] + ([] if before is None else [before])
    return pl.pallas_call(
        functools.partial(core_kernel, size, first, last, before is not None),
        out_shape=jax.ShapeDtypeStruct((3 * SEGS, size.frames), jnp.float32),
        in_specs=[VMEM] * len(args),
        out_specs=VMEM,
        scratch_shapes=[pltpu.VMEM((size.rows, size.width), jnp.float32)],
        compiler_params=pltpu.CompilerParams(vmem_limit_bytes=8 * MIB),
        cost_estimate=pl.CostEstimate(flops=3 * 10**9, bytes_accessed=10**6, transcendentals=0),
        name="core",
    )(*args)


def edge_kernel(size, above, under, moved, before, coeffs, intensity, out, wide, moments):
    reach, frames = size.reach, size.frames
    moments[...] = before[...]
    widen(size, above, wide, 0, reach, size.rows - reach)
    widen(size, under, wide, reach, reach, 0)
    band, bands = lax.axis_index("band"), lax.axis_size("band")

    @pl.when(band == 0)
    def _():
        wide[0:reach, :] = jnp.full((reach, size.width), -1.0, jnp.float32)

    @pl.when(band == bands - 1)
    def _():
        wide[reach : 2 * reach, :] = jnp.full((reach, size.width), -1.0, jnp.float32)

    consts = table_consts(size)

    def step(r, carry):
        e = jnp.where(r < reach, r, r + size.rows)
        add_row(size, consts, wide[pl.ds(r, 1), :], moved, moments, e)
        return carry

    lax.fori_loop(0, 2 * reach, step, 0, unroll=9)
    partial = jnp.dot(
        moments[...].T,
        coeffs[...],
        precision=lax.Precision.HIGHEST,
        preferred_element_type=jnp.float32,
    )
    half = frames // 2
    width = MASKS // bands
    per = LANES // width
    lane = lax.broadcasted_iota(jnp.int32, (half, LANES), 1)
    for b in range(bands):
        at = (b // per) * LANES
        low = partial[:half, at : at + LANES]
        high = partial[half:, at : at + LANES]
        if b % per == 0:
            high = pltpu.roll(high, width, 1)
        else:
            low = pltpu.roll(low, width, 1)
        out[b, 0:half, :] = jnp.where(lane < width, low, high)
        out[b, half : half + 8, :] = intensity[...]


def edge_rows(size, above, under, moved, before, coeffs, intensity):
    bands = lax.axis_size("band")
    return pl.pallas_call(
        functools.partial(edge_kernel, size),
        out_shape=jax.ShapeDtypeStruct((bands, size.frames // 2 + 8, LANES), jnp.float32),
        in_specs=[VMEM] * 6,
        out_specs=VMEM,
        scratch_shapes=[
            pltpu.VMEM((2 * size.reach, size.width), jnp.float32),
            pltpu.VMEM((3 * SEGS, size.frames), jnp.float32),
        ],
        compiler_params=pltpu.CompilerParams(vmem_limit_bytes=12 * MIB),
        cost_estimate=pl.CostEstimate(flops=3 * 10**9, bytes_accessed=10**6, transcendentals=0),
        name="edge",
    )(above, under, moved, before, coeffs, intensity)


def finish_kernel(frame_total, blocks, out):
    bands, height, _ = blocks.shape
    half = height - 8
    summed = blocks[0]
    for b in range(1, bands):
        summed = summed + blocks[b]
    mean_total = jnp.sum(summed[half:, :]) / frame_total
    scaled = summed[:half] / mean_total
    width = out.shape[1]
    out[0:half, :] = scaled[:, :width]
    out[half:, :] = scaled[:, width:]


def finish(blocks, frame_count):
    half = frame_count // 2
    return pl.pallas_call(
        functools.partial(finish_kernel, float(frame_count * lax.axis_size("scan"))),
        out_shape=jax.ShapeDtypeStruct((2 * half, LANES // 2), jnp.float32),
        in_specs=[VMEM],
        out_specs=VMEM,
        compiler_params=pltpu.CompilerParams(vmem_limit_bytes=8 * MIB),
        name="finish",
    )(blocks)


def scan_pairs():
    count = lax.axis_size("scan")
    around = {0: 3, 1: 2, 2: 1, 3: 0}

    def z_around(i):
        return around[i // 8] * 8 + i % 8

    def x_around(i):
        return (i // 8) * 8 + around[i // 2 % 4] * 2 + i % 2

    moves = [lambda i: i ^ 8, z_around, lambda i: i ^ 2, x_around, lambda i: i ^ 1]
    return [[(i, move(i)) for i in range(count)] for move in moves]


def body(frame_codes, row_scales, row_shift, col_shift, segment_labels, mask_coeffs):
    frame_count, band_height, det_cols = frame_codes.shape
    size = Sizes(frame_count, band_height, det_cols)
    bands = lax.axis_size("band")
    down = [(i, i + 1) for i in range(bands - 1)]
    up = [(i + 1, i) for i in range(bands - 1)]
    above = lax.ppermute(segment_labels, "band", down)
    under = lax.ppermute(segment_labels, "band", up)
    moved, intensity = shift_frames(size, row_shift, col_shift, row_scales, frame_codes)
    moments = None
    third = band_height // 3
    pieces = [(0, third), (third, 2 * third), (2 * third, band_height)]
    for pairs in scan_pairs():
        intensity = intensity + lax.ppermute(intensity, "scan", pairs)
    for first, last in pieces:
        moments = core_rows(size, segment_labels, moved, moments, first, last)
    coeffs = mask_coeffs.reshape(3 * SEGS, MASKS)
    send = edge_rows(size, above, under, moved, moments, coeffs, intensity)
    blocks = lax.all_to_all(send, "band", 0, 0)
    return finish(blocks, frame_count)


def solution(mesh):
    return jax.shard_map(
        body,
        mesh=mesh,
        in_specs=(
            P("scan", "band", None),
            P("scan", "band"),
            P("scan"),
            P("scan"),
            P("band", None),
            P(),
        ),
        out_specs=P("scan", "band"),
        check_vma=False,
    )
```

time: 254 us -> 56.9 us (0.22)
  blocking collectives: 81.4 us -> 12.7 us
  local copies, waits for them, and re-layouts: 68.2 us -> 5.71 us
  matrix products: 45.9 us -> 0 us
  other arithmetic: 35.5 us -> 0.02 us
  Pallas kernels: 0 us -> 18.4 us
  between operations: 14.2 us -> 0.14 us
  starting transfers between devices: 4.81 us -> 16.2 us
    psum x1 -> x0, blocking collectives: 81.4 us -> none  [body(): intensity_sum = lax.psum(jnp.sum(partials[:, :SEGS]), ('scan', 'band'))]
    mul x1 -> x0, local copies, waits for them, and re-layouts: 47.7 us -> none  [basis_table(): table = basis[:, :, :, None] * onehot[:, :, None, :]]
    dot_general x6 -> x0, matrix products: 45.9 us -> none  [the longest x4 27.2 us: shift_group(): jnp.einsum('fsc,fcd->fsd', rowed, col_pick, preferred_element_type=jnp.fl...]
    pallas_call x0 -> x6, Pallas kernels: none -> 18.4 us  [the longest x1 7.85 us: shift_frames(): pl.pallas_call(functools.partial(shift_kernel, size), out_shape=[jax.Shap...]
    mul x1 -> x0, other arithmetic: 15.1 us -> none  [basis_table(): table = basis[:, :, :, None] * onehot[:, :, None, :]]
    all_to_all x0 -> x1, blocking collectives: none -> 12.7 us  [body(): blocks = lax.all_to_all(send, 'band', 0, 0)]
    convert_element_type x3 -> x0, other arithmetic: 12.6 us -> none  [the longest x1 6.97 us: basis_table(): (labels[:, :, None] == jnp.arange(SEGS, dtype=jnp.int32)).astype(jnp.bflo...]
    ppermute x2 -> x7, starting transfers between devices: 4.81 us -> 16.2 us  [the longest x5 11.4 us: body(): intensity = intensity + lax.ppermute(intensity, 'scan', pairs)]
  transfers between devices with their start and end apart: 3 -> 7, of which waited for: 1 -> 2; matrix products, arithmetic and copies ran while one was open for 28% -> 0% of each run, Pallas kernels for 0% -> 13%
where the time goes in v1:
time: 56.9 us; the launch traced here: 56 us
  Pallas kernels  18.4 us (32%)
  starting transfers between devices  16.2 us (28%)
  blocking collectives  12.7 us (22%)
  local copies, waits for them, and re-layouts  5.71 us (10%)
  waiting for transfers between devices  2.89 us (5%)
    all_to_all x1, blocking collectives, body(): blocks = lax.all_to_all(send, 'band', 0, 0)  12.7 us
    ppermute x5, starting transfers between devices, body(): intensity = intensity + lax.ppermute(intensity, 'scan', pairs)  11.4 us
    pallas_call x1, Pallas kernels, shift_frames(): pl.pallas_call(functools.partial(shift_kernel, size), out_shape=[jax.Shap...  7.85 us
    pallas_call x3, Pallas kernels, core_rows(): pl.pallas_call(functools.partial(core_kernel, size, first, last, before i...  7.16 us
    unnamed x14, local copies, waits for them, and re-layouts  5.71 us
    ppermute x1, starting transfers between devices, body(): above = lax.ppermute(segment_labels, 'band', down)  3.48 us
    ppermute x5, waiting for transfers between devices, body(): intensity = intensity + lax.ppermute(intensity, 'scan', pairs)  2.88 us
    pallas_call x1, Pallas kernels, edge_rows(): pl.pallas_call(functools.partial(edge_kernel, size), out_shape=jax.ShapeD...  2.55 us
  transfers between devices with their start and end apart: 7, of which 2 were waited for; matrix products, arithmetic and copies ran while one was open for 0% of the time, Pallas kernels for 13%

profile of v1, /device:TPU:6, one launch (start us, length us, event | category | flops | bytes accessed | tf_op | source)
XLA Modules:
  0.0 56.0 jit_solution(13325897755231311325)
XLA Ops:
  0.0 0.0 copy-start.1
  0.0 0.0 copy-start.3
  0.0 2.7 %copy-done.3 = bf16[64,72,576]{2,1,0:T(8,128)(2,1)S(1)} copy-done((bf16[64,72,576]{2,1,0:T(8,128)(2,1)S(1)}, bf16[64,72,576]{2,1,0:T(8,128)(2,1)}, u32[]{:S(2)}) %copy-start.3) | copy-done | bytes 5308440
  2.7 0.0 copy-start.4
  2.7 0.8 %copy-done.4 = f32[64,72]{1,0:T(8,128)S(1)} copy-done((f32[64,72]{1,0:T(8,128)S(1)}, f32[64,72]{1,0:T(8,128)}, u32[]{:S(2)}) %copy-start.4) | copy-done | bytes 18456
  3.5 0.0 copy-start.5
  3.5 0.7 %copy-done.5 = s32[64]{0:T(128)S(1)} copy-done((s32[64]{0:T(128)S(1)}, s32[64]{0:T(128)}, u32[]{:S(2)}) %copy-start.5) | copy-done | bytes 280
  4.1 0.0 copy-start.6
  4.1 0.7 %copy-done.6 = s32[64]{0:T(128)S(1)} copy-done((s32[64]{0:T(128)S(1)}, s32[64]{0:T(128)}, u32[]{:S(2)}) %copy-start.6) | copy-done | bytes 280
  4.8 7.8 %shift.1 = (f32[5,6480,128]{2,1,0:T(8,128)S(1)}, f32[8,128]{1,0:T(8,128)S(1)}) custom-call(s32[64]{0:T(128)S(1)} %copy-done.5, s32[64]{0:T(128)S(1)} %copy-done.6, f32[64,72]{1,0:T(8,128)S(1)} %copy-done.4, bf16[64,72,576]{2,1,0:T(8,128)(2,1)S(1)} %copy-done.3), custom_call_target="tpu_custom_call" | custom-call | flops 4000000000 | bytes 1000000 | tf_op jit(solution)/shard_map/shift/pallas_call | solution.py:112
  12.6 3.4 %collective-permute-start.2 = (f32[8,128]{1,0:T(8,128)S(1)}, f32[8,128]{1,0:T(8,128)S(1)}, u32[]{:S(2)}, u32[]{:S(2)}) collective-permute-start(f32[8,128]{1,0:T(8,128)S(1)} %get-tuple-element.8), channel_id=1, source_target_pairs={{0,64},{8,72},{16,80},{24,88},{32,96},{40,104},{48,112},{56,120},{... | collective-permute-start | bytes 12296 | tf_op jit(solution)/shard_map/ppermute | solution.py:319
  16.0 1.6 %collective-permute-done.2 = f32[8,128]{1,0:T(8,128)S(1)} collective-permute-done((f32[8,128]{1,0:T(8,128)S(1)}, f32[8,128]{1,0:T(8,128)S(1)}, u32[]{:S(2)}, u32[]{:S(2)}) %collective-permute-start.2) | collective-permute-done | bytes 4128 | tf_op jit(solution)/shard_map/ppermute | solution.py:319
  17.6 6.0 %collective-permute-start.3 = (f32[8,128]{1,0:T(8,128)S(1)}, f32[8,128]{1,0:T(8,128)S(1)}, u32[]{:S(2)}, u32[]{:S(2)}) collective-permute-start(f32[8,128]{1,0:T(8,128)S(1)} %add.15), channel_id=1, source_target_pairs={{0,192},{8,200},{16,208},{24,216},{32,224},{40,232},{48,240},{56,2... | collective-permute-start | bytes 12296 | tf_op jit(solution)/shard_map/ppermute | solution.py:319
  23.5 3.5 %collective-permute-start = (s32[72,576]{1,0:T(8,128)}, s32[72,576]{1,0:T(8,128)S(1)}, u32[]{:S(2)}, u32[]{:S(2)}) collective-permute-start(s32[72,576]{1,0:T(8,128)} %refs_0_.5), channel_id=1, source_target_pairs={{0,1},{1,2},{2,3},{3,4},{4,5},{5,6},{6,7},{8,9},{9,10},{10,11},{11... | collective-permute-start | bytes 497672 | tf_op jit(solution)/shard_map/ppermute | solution.py:312
  27.0 1.3 %collective-permute-start.1 = (s32[72,576]{1,0:T(8,128)}, s32[72,576]{1,0:T(8,128)S(1)}, u32[]{:S(2)}, u32[]{:S(2)}) collective-permute-start(s32[72,576]{1,0:T(8,128)} %refs_0_.5), channel_id=1, source_target_pairs={{1,0},{2,1},{3,2},{4,3},{5,4},{6,5},{7,6},{9,8},{10,9},{11,10},{12... | collective-permute-start | bytes 497672 | tf_op jit(solution)/shard_map/ppermute | solution.py:313
  28.3 0.0 collective-permute-done.3
  28.3 0.9 %collective-permute-start.4 = (f32[8,128]{1,0:T(8,128)S(1)}, f32[8,128]{1,0:T(8,128)S(1)}, u32[]{:S(2)}, u32[]{:S(2)}) collective-permute-start(f32[8,128]{1,0:T(8,128)S(1)} %add.16), channel_id=1, source_target_pairs={{0,16},{8,24},{16,0},{24,8},{32,48},{40,56},{48,32},{56,40},{64,80... | collective-permute-start | bytes 12296 | tf_op jit(solution)/shard_map/ppermute | solution.py:319
  29.3 0.0 copy-start
  29.3 0.9 %copy-done = s32[72,576]{1,0:T(8,128)S(1)} copy-done((s32[72,576]{1,0:T(8,128)S(1)}, s32[72,576]{1,0:T(8,128)}, u32[]{:S(2)}) %copy-start) | copy-done | bytes 165912
  30.2 2.4 %core.3.refs_2_ = f32[384,64]{1,0:T(8,128)S(1)} custom-call(s32[72,576]{1,0:T(8,128)S(1)} %copy-done, f32[5,6480,128]{2,1,0:T(8,128)S(1)} %get-tuple-element.7.refs_1_.moved), custom_call_target="tpu_custom_call" | custom-call | flops 3000000000 | bytes 1000000 | tf_op jit(solution)/shard_map/core/pallas_call | solution.py:193
  32.6 0.0 collective-permute-done.4
  32.6 0.0 copy-start.2
  32.6 1.2 %collective-permute-start.5 = (f32[8,128]{1,0:T(8,128)S(1)}, f32[8,128]{1,0:T(8,128)S(1)}, u32[]{:S(2)}, u32[]{:S(2)}) collective-permute-start(f32[8,128]{1,0:T(8,128)S(1)} %add.17), channel_id=1, source_target_pairs={{0,48},{8,56},{16,32},{24,40},{32,16},{40,24},{48,0},{56,8},{64,11... | collective-permute-start | bytes 12296 | tf_op jit(solution)/shard_map/ppermute | solution.py:319
  33.8 0.0 copy-done.1
  33.8 2.4 %core.4.refs_2_ = f32[384,64]{1,0:T(8,128)S(1)} custom-call(s32[72,576]{1,0:T(8,128)S(1)} %copy-done.1, f32[5,6480,128]{2,1,0:T(8,128)S(1)} %get-tuple-element.7.refs_1_.moved, f32[384,64]{1,0:T(8,128)S(1)} %core.3.refs_2_), custom_call_target="tpu_custom_call" | custom-call | flops 3000000000 | bytes 1000000 | tf_op jit(solution)/shard_map/core/pallas_call | solution.py:193
  36.2 1.3 %collective-permute-done.5 = f32[8,128]{1,0:T(8,128)S(1)} collective-permute-done((f32[8,128]{1,0:T(8,128)S(1)}, f32[8,128]{1,0:T(8,128)S(1)}, u32[]{:S(2)}, u32[]{:S(2)}) %collective-permute-start.5) | collective-permute-done | bytes 4128 | tf_op jit(solution)/shard_map/ppermute | solution.py:319
  37.5 0.0 collective-permute-start.6
  37.5 2.4 %core.5.before = f32[384,64]{1,0:T(8,128)S(1)} custom-call(s32[72,576]{1,0:T(8,128)S(1)} %copy-done.1, f32[5,6480,128]{2,1,0:T(8,128)S(1)} %get-tuple-element.7.refs_1_.moved, f32[384,64]{1,0:T(8,128)S(1)} %core.4.refs_2_), custom_call_target="tpu_custom_call" | custom-call | flops 3000000000 | bytes 1000000 | tf_op jit(solution)/shard_map/core/pallas_call | solution.py:193
  39.9 0.0 collective-permute-done.6
  39.9 0.0 collective-permute-done.above
  40.0 0.0 collective-permute-done.1.under
  40.0 0.0 copy-done.2
  40.0 2.5 %edge.1 = f32[8,40,128]{2,1,0:T(8,128)S(1)} custom-call(s32[72,576]{1,0:T(8,128)S(1)} %collective-permute-done.above, s32[72,576]{1,0:T(8,128)S(1)} %collective-permute-done.1.under, f32[5,6480,128]{2,1,0:T(8,128)S(1)} %get-tuple-element.7.refs_1_.moved, f32[384,64]{1,0:T(8,128)S(1)} %core.5.before, f32[384,512]{1,0:T(8,128)S(1)} %bitcast.1, ...), custom_call_target="tpu_custom_call" | custom-call | flops 3000000000 | bytes 1000000 | tf_op jit(solution)/shard_map/edge/pallas_call | solution.py:252
  42.5 12.7 %all_to_all.5.blocks = f32[8,40,128]{2,1,0:T(8,128)S(1)} all-to-all(f32[8,40,128]{2,1,0:T(8,128)S(1)} %edge.1), channel_id=1, replica_groups=mesh['scan'=32,'band'=8] {'band'}, dimensions={0} | all-to-all | bytes 327680 | tf_op jit(solution)/shard_map/all_to_all | solution.py:324
  55.2 0.8 %finish.1 = f32[64,64]{1,0:T(8,128)} custom-call(f32[8,40,128]{2,1,0:T(8,128)S(1)} %all_to_all.5.blocks), custom_call_target="tpu_custom_call" | custom-call | tf_op jit(solution)/shard_map/finish/pallas_call | solution.py:282
  (5 shorter events, 0.0 us)
Async XLA Ops:
  0.0 33.8 %copy-start.1 = (s32[72,576]{1,0:T(8,128)S(1)}, s32[72,576]{1,0:T(8,128)}, u32[]{:S(2)}) copy-start(s32[72,576]{1,0:T(8,128)} %refs_0_.5) | copy-start | bytes 497668
  0.0 2.7 %copy-start.3 = (bf16[64,72,576]{2,1,0:T(8,128)(2,1)S(1)}, bf16[64,72,576]{2,1,0:T(8,128)(2,1)}, u32[]{:S(2)}) copy-start(bf16[64,72,576]{2,1,0:T(8,128)(2,1)} %codes.1) | copy-start | bytes 15925252
  2.7 0.8 %copy-start.4 = (f32[64,72]{1,0:T(8,128)S(1)}, f32[64,72]{1,0:T(8,128)}, u32[]{:S(2)}) copy-start(f32[64,72]{1,0:T(8,128)} %scales.1) | copy-start | bytes 55300
  3.5 0.7 %copy-start.5 = (s32[64]{0:T(128)S(1)}, s32[64]{0:T(128)}, u32[]{:S(2)}) copy-start(s32[64]{0:T(128)} %row_shift.1) | copy-start | bytes 772
  4.1 0.7 %copy-start.6 = (s32[64]{0:T(128)S(1)}, s32[64]{0:T(128)}, u32[]{:S(2)}) copy-start(s32[64]{0:T(128)} %col_shift.1) | copy-start | bytes 772
  12.6 4.9 %collective-permute-start.2 = (f32[8,128]{1,0:T(8,128)S(1)}, f32[8,128]{1,0:T(8,128)S(1)}, u32[]{:S(2)}, u32[]{:S(2)}) collective-permute-start(f32[8,128]{1,0:T(8,128)S(1)} %get-tuple-element.8), channel_id=1, source_target_pairs={{0,64},{8,72},{16,80},{24,88},{32,96},{40,104},{48,112},{56,120},{... | collective-permute-start | bytes 12296 | tf_op jit(solution)/shard_map/ppermute | solution.py:319
  17.6 10.7 %collective-permute-start.3 = (f32[8,128]{1,0:T(8,128)S(1)}, f32[8,128]{1,0:T(8,128)S(1)}, u32[]{:S(2)}, u32[]{:S(2)}) collective-permute-start(f32[8,128]{1,0:T(8,128)S(1)} %add.15), channel_id=1, source_target_pairs={{0,192},{8,200},{16,208},{24,216},{32,224},{40,232},{48,240},{56,2... | collective-permute-start | bytes 12296 | tf_op jit(solution)/shard_map/ppermute | solution.py:319
  23.5 16.4 %collective-permute-start = (s32[72,576]{1,0:T(8,128)}, s32[72,576]{1,0:T(8,128)S(1)}, u32[]{:S(2)}, u32[]{:S(2)}) collective-permute-start(s32[72,576]{1,0:T(8,128)} %refs_0_.5), channel_id=1, source_target_pairs={{0,1},{1,2},{2,3},{3,4},{4,5},{5,6},{6,7},{8,9},{9,10},{10,11},{11... | collective-permute-start | bytes 497672 | tf_op jit(solution)/shard_map/ppermute | solution.py:312
  27.0 12.9 %collective-permute-start.1 = (s32[72,576]{1,0:T(8,128)}, s32[72,576]{1,0:T(8,128)S(1)}, u32[]{:S(2)}, u32[]{:S(2)}) collective-permute-start(s32[72,576]{1,0:T(8,128)} %refs_0_.5), channel_id=1, source_target_pairs={{1,0},{2,1},{3,2},{4,3},{5,4},{6,5},{7,6},{9,8},{10,9},{11,10},{12... | collective-permute-start | bytes 497672 | tf_op jit(solution)/shard_map/ppermute | solution.py:313
  28.3 4.2 %collective-permute-start.4 = (f32[8,128]{1,0:T(8,128)S(1)}, f32[8,128]{1,0:T(8,128)S(1)}, u32[]{:S(2)}, u32[]{:S(2)}) collective-permute-start(f32[8,128]{1,0:T(8,128)S(1)} %add.16), channel_id=1, source_target_pairs={{0,16},{8,24},{16,0},{24,8},{32,48},{40,56},{48,32},{56,40},{64,80... | collective-permute-start | bytes 12296 | tf_op jit(solution)/shard_map/ppermute | solution.py:319
  29.3 0.9 %copy-start = (s32[72,576]{1,0:T(8,128)S(1)}, s32[72,576]{1,0:T(8,128)}, u32[]{:S(2)}) copy-start(s32[72,576]{1,0:T(8,128)} %refs_0_.5) | copy-start | bytes 497668
  32.6 7.4 %copy-start.2 = (f32[3,128,512]{2,1,0:T(8,128)S(1)}, f32[3,128,512]{2,1,0:T(8,128)}, u32[]{:S(2)}) copy-start(f32[3,128,512]{2,1,0:T(8,128)} %param.11) | copy-start | bytes 2359300
  32.6 4.9 %collective-permute-start.5 = (f32[8,128]{1,0:T(8,128)S(1)}, f32[8,128]{1,0:T(8,128)S(1)}, u32[]{:S(2)}, u32[]{:S(2)}) collective-permute-start(f32[8,128]{1,0:T(8,128)S(1)} %add.17), channel_id=1, source_target_pairs={{0,48},{8,56},{16,32},{24,40},{32,16},{40,24},{48,0},{56,8},{64,11... | collective-permute-start | bytes 12296 | tf_op jit(solution)/shard_map/ppermute | solution.py:319
  37.5 2.4 %collective-permute-start.6 = (f32[8,128]{1,0:T(8,128)S(1)}, f32[8,128]{1,0:T(8,128)S(1)}, u32[]{:S(2)}, u32[]{:S(2)}) collective-permute-start(f32[8,128]{1,0:T(8,128)S(1)} %add.18), channel_id=1, source_target_pairs={{0,8},{8,0},{16,24},{24,16},{32,40},{40,32},{48,56},{56,48},{64,72... | collective-permute-start | bytes 12296 | tf_op jit(solution)/shard_map/ppermute | solution.py:319

commit v2 on v1

v2 whole, which is shorter than its diff:
```python
import functools

import jax
import jax.numpy as jnp
from jax import lax
from jax.experimental import pallas as pl
from jax.experimental.pallas import tpu as pltpu
from jax.sharding import PartitionSpec as P

MASKS = 512
SEGS = 128
LANES = 128
MIB = 2**20
VMEM = pl.BlockSpec(memory_space=pltpu.VMEM)
SMEM = pl.BlockSpec(memory_space=pltpu.SMEM)


class Sizes:
    def __init__(self, frame_count, band_height, det_cols):
        self.frames = frame_count
        self.rows = band_height
        self.cols = det_cols
        self.reach = band_height // 8
        self.ext = band_height + 2 * self.reach
        self.tiles = -(-det_cols // LANES)
        self.width = self.tiles * LANES
        self.pitch = frame_count + 1
        self.tall = -(-band_height // 16) * 16
        self.packed = 8 + -(-self.reach // 8) * 8


def widened(size, labels):
    fill = jnp.full((labels.shape[0], size.width - size.cols), -1.0, jnp.float32)
    return jnp.concatenate([labels.astype(jnp.float32), fill], axis=1)


def diagonal_kernel(size, out):
    place = lax.broadcasted_iota(jnp.int32, out.shape, 1)
    row = lax.broadcasted_iota(jnp.int32, out.shape, 0)
    chosen = (place == row) | (place == row + size.rows) | (place == row + 2 * size.rows)
    out[...] = jnp.where(chosen & (row < size.rows), 1.0, 0.0).astype(jnp.bfloat16)


def diagonals(size):
    return pl.pallas_call(
        functools.partial(diagonal_kernel, size),
        out_shape=jax.ShapeDtypeStruct((size.tall, 2 * LANES), jnp.bfloat16),
        out_specs=VMEM,
        compiler_params=pltpu.CompilerParams(vmem_limit_bytes=2 * MIB),
        cost_estimate=pl.CostEstimate(flops=10**10, bytes_accessed=10**6, transcendentals=0),
        name="diagonals",
    )()


def prepare_kernel(size, diagonal, scales, labels, moved, spread, wide, split):
    frames, rows = size.frames, size.rows
    empty = jnp.zeros((frames, LANES), jnp.float32)

    def clear(e, carry):
        for t in range(size.tiles):
            moved[t, pl.ds(e * size.pitch, frames), :] = empty
            moved[t, pl.ds((e + rows) * size.pitch, frames), :] = empty
        return carry

    lax.fori_loop(0, 2 * size.reach, clear, 0, unroll=3)

    whole = scales[...]
    high = whole.astype(jnp.bfloat16).astype(jnp.float32)
    middle = (whole - high).astype(jnp.bfloat16).astype(jnp.float32)
    rest = jnp.zeros((frames, 2 * LANES - rows), jnp.float32)
    parts = [
        pltpu.roll(jnp.concatenate([part, rest], axis=1), k * rows, 1)
        for k, part in enumerate([high, middle, whole - high - middle])
    ]
    split[...] = parts[0] + parts[1] + parts[2]
    tall = size.tall
    group = 8
    ones = jnp.ones((2 * LANES, LANES), jnp.bfloat16)

    def spread_group(i, carry):
        chosen = []
        for j in range(group):
            line = split[pl.ds(i * group + j, 1), :]
            line = jnp.broadcast_to(line, (16, 2 * LANES)).astype(jnp.bfloat16)
            chosen.append(jnp.concatenate([line] * (tall // 16), axis=0) * diagonal[...])
        at = pl.multiple_of(i * (group * tall), 8)
        spread[pl.ds(at, group * tall), :] = jnp.dot(
            jnp.concatenate(chosen, axis=0), ones, preferred_element_type=jnp.float32
        )
        return carry

    lax.fori_loop(0, frames // group, spread_group, 0, unroll=8)
    wide[...] = widened(size, labels[...])


def prepare(size, diagonal, scales, labels):
    return pl.pallas_call(
        functools.partial(prepare_kernel, size),
        out_shape=[
            jax.ShapeDtypeStruct((size.tiles, size.ext * size.pitch, LANES), jnp.float32),
            jax.ShapeDtypeStruct((size.frames * size.tall, LANES), jnp.float32),
            jax.ShapeDtypeStruct((size.rows, size.width), jnp.float32),
        ],
        in_specs=[VMEM] * 3,
        out_specs=[VMEM] * 3,
        scratch_shapes=[pltpu.VMEM((size.frames, 2 * LANES), jnp.float32)],
        compiler_params=pltpu.CompilerParams(vmem_limit_bytes=8 * MIB),
        cost_estimate=pl.CostEstimate(flops=5 * 10**8, bytes_accessed=10**6, transcendentals=0),
        name="prepare",
    )(diagonal, scales, labels)


def shift_kernel(size, row_shift, col_shift, spread, codes, wide, cleared, moved, payload, total):
    frames, rows, cols, tiles, reach = size.frames, size.rows, size.cols, size.tiles, size.reach
    total[...] = jnp.zeros((rows, LANES), jnp.float32)
    whole_lane = lax.broadcasted_iota(jnp.int32, (rows, LANES), 1)
    lane = whole_lane.astype(jnp.float32).astype(jnp.bfloat16)
    source = lax.broadcasted_iota(jnp.int32, (rows, LANES), 0)
    band = lax.axis_index("band")
    zero = jnp.zeros((rows, LANES), jnp.bfloat16)

    def shift_frame(f, carry):
        down, right = row_shift[f], col_shift[f]
        turn = jnp.where(right < 0, right + LANES, right)
        left_end = jnp.where(right < 0, 0, turn).astype(jnp.float32).astype(jnp.bfloat16)
        right_start = jnp.where(right < 0, turn, LANES).astype(jnp.float32).astype(jnp.bfloat16)
        from_left = lane < left_end
        from_right = lane >= right_start
        scale_f = spread[pl.ds(pl.multiple_of(f * size.tall, 8), rows), :]
        turned = [zero]
        for t in range(tiles):
            upper = min(cols, (t + 1) * LANES)
            value = codes[f, :, t * LANES : upper].astype(jnp.float32)
            if upper < (t + 1) * LANES:
                fill = jnp.zeros((rows, (t + 1) * LANES - upper), jnp.float32)
                value = jnp.concatenate([value, fill], axis=1)
            turned.append(pltpu.roll((value * scale_f).astype(jnp.bfloat16), turn, 1))
        turned.append(zero)
        start = (reach + down) * size.pitch + f
        row_sum = jnp.zeros((rows, LANES), jnp.float32)
        for t in range(tiles):
            out = jnp.where(
                from_left, turned[t], jnp.where(from_right, turned[t + 2], turned[t + 1])
            ).astype(jnp.float32)
            moved[t, pl.ds(start, rows, stride=size.pitch), :] = out
            if (t + 1) * LANES > cols:
                out = jnp.where(whole_lane < cols - t * LANES, out, 0.0)
            row_sum = row_sum + out
        target = source + (band * rows + down)
        total[...] += jnp.where((target >= 0) & (target < cols), row_sum, 0.0)
        return carry

    lax.fori_loop(0, frames, shift_frame, 0, unroll=4)
    payload[0:8, 0:LANES] = jnp.sum(total[...].reshape(rows // 8, 8, LANES), axis=0)
    top, bottom = wide[0:reach, :], wide[rows - reach : rows, :]
    payload[8 : 8 + reach, :] = jnp.where(band % 2 == 0, bottom, top)


def shift_frames(size, row_shift, col_shift, spread, codes, wide, cleared):
    return pl.pallas_call(
        functools.partial(shift_kernel, size),
        out_shape=[
            jax.ShapeDtypeStruct(cleared.shape, jnp.float32),
            jax.ShapeDtypeStruct((size.packed, size.width), jnp.float32),
        ],
        in_specs=[SMEM] * 2 + [VMEM] * 4,
        out_specs=[VMEM] * 2,
        scratch_shapes=[pltpu.VMEM((size.rows, LANES), jnp.float32)],
        input_output_aliases={5: 0},
        compiler_params=pltpu.CompilerParams(vmem_limit_bytes=12 * MIB),
        cost_estimate=pl.CostEstimate(flops=6 * 10**9, bytes_accessed=10**6, transcendentals=0),
        name="shift",
    )(row_shift, col_shift, spread, codes, wide, cleared)


def table_consts(size):
    segment = lax.broadcasted_iota(jnp.int32, (16, size.width), 0)
    column = lax.broadcasted_iota(jnp.int32, (16, size.width), 1).astype(jnp.float32)
    xcoord = ((column + 0.5) / size.cols - 0.5).astype(jnp.bfloat16)
    ids = [
        (segment + 16 * k).astype(jnp.float32).astype(jnp.bfloat16) for k in range(SEGS // 16)
    ]
    return ids, xcoord


def add_row(size, consts, label_row, values, moments, e):
    ids, xcoord = consts
    zero = jnp.zeros((16, size.width), jnp.bfloat16)
    one = jnp.ones((16, size.width), jnp.bfloat16)
    label = jnp.broadcast_to(label_row, (16, size.width)).astype(jnp.bfloat16)
    plain, by_x = [], []
    for k in range(SEGS // 16):
        same = label == ids[k]
        plain.append(jnp.where(same, one, zero))
        by_x.append(jnp.where(same, xcoord, zero))
    table = jnp.concatenate(plain + by_x, axis=0)
    sums = lax.dot_general(
        table, values, (((1,), (1,)), ((), ())), preferred_element_type=jnp.float32
    )
    first_row = lax.axis_index("band") * size.rows
    offset = (first_row + e - size.reach).astype(jnp.float32)
    ycoord = ((offset + 0.5) / size.cols - 0.5).astype(jnp.bfloat16).astype(jnp.float32)
    moments[0:SEGS, :] += sums[0:SEGS]
    moments[SEGS : 2 * SEGS, :] += sums[0:SEGS] * ycoord
    moments[2 * SEGS : 3 * SEGS, :] += sums[SEGS : 2 * SEGS]


def values_of(size, moved, e):
    base = e * size.pitch
    tiles = [
        moved[t, pl.ds(base, size.frames), :].astype(jnp.bfloat16) for t in range(size.tiles)
    ]
    return jnp.concatenate(tiles, axis=1)


def core_kernel(size, first, last, started, moved, wide, token, *refs):
    if started:
        before, moments = refs
        moments[...] = before[...]
    else:
        (moments,) = refs
        moments[...] = jnp.zeros(moments.shape, jnp.float32)
    consts = table_consts(size)

    def step(r, carry):
        e = r + size.reach
        add_row(size, consts, wide[pl.ds(r, 1), :], values_of(size, moved, e), moments, e)
        return carry

    lax.fori_loop(first, last, step, 0, unroll=9)


def core_rows(size, moved, wide, token, before, first, last):
    args = [moved, wide, token] + ([] if before is None else [before])
    specs = [VMEM, VMEM, pl.BlockSpec(memory_space=pl.ANY)] + [VMEM] * (len(args) - 3)
    return pl.pallas_call(
        functools.partial(core_kernel, size, first, last, before is not None),
        out_shape=jax.ShapeDtypeStruct((3 * SEGS, size.frames), jnp.float32),
        in_specs=specs,
        out_specs=VMEM,
        compiler_params=pltpu.CompilerParams(vmem_limit_bytes=8 * MIB),
        cost_estimate=pl.CostEstimate(flops=4 * 10**9, bytes_accessed=10**6, transcendentals=0),
        name="core",
    )(*args)


def edge_kernel(size, moved, first_got, second_got, token, before, coeffs, send, wide, moments):
    frames, rows, reach = size.frames, size.rows, size.reach
    moments[...] = before[...]
    band, bands = lax.axis_index("band"), lax.axis_size("band")
    even = band % 2 == 0
    first, second = first_got[8 : 8 + reach, :], second_got[8 : 8 + reach, :]
    wide[0:reach, :] = jnp.where(even, second, first)
    wide[reach : 2 * reach, :] = jnp.where(even, first, second)
    nothing = jnp.full((reach, size.width), -1.0, jnp.float32)

    @pl.when(band == 0)
    def _():
        wide[0:reach, :] = nothing

    @pl.when(band == bands - 1)
    def _():
        wide[reach : 2 * reach, :] = nothing

    consts = table_consts(size)

    def step(r, carry):
        e = jnp.where(r < reach, r, r + rows)
        add_row(size, consts, wide[pl.ds(r, 1), :], values_of(size, moved, e), moments, e)
        return carry

    lax.fori_loop(0, 2 * reach, step, 0, unroll=9)
    partial = jnp.dot(
        moments[...].T,
        coeffs[...],
        precision=lax.Precision.HIGHEST,
        preferred_element_type=jnp.float32,
    )
    half = frames // 2
    width = MASKS // bands
    per = LANES // width
    lane = lax.broadcasted_iota(jnp.int32, (half, LANES), 1)
    for b in range(bands):
        at = (b // per) * LANES
        low = partial[:half, at : at + LANES]
        high = partial[half:, at : at + LANES]
        if b % per == 0:
            high = pltpu.roll(high, width, 1)
        else:
            low = pltpu.roll(low, width, 1)
        send[b, 0:half, :] = jnp.where(lane < width, low, high)


def edge_rows(size, moved, first_got, second_got, token, before, coeffs):
    return pl.pallas_call(
        functools.partial(edge_kernel, size),
        out_shape=jax.ShapeDtypeStruct(
            (lax.axis_size("band"), size.frames // 2 + 8, LANES), jnp.float32
        ),
        in_specs=[VMEM, VMEM, VMEM, pl.BlockSpec(memory_space=pl.ANY), VMEM, VMEM],
        out_specs=VMEM,
        scratch_shapes=[
            pltpu.VMEM((2 * size.reach, size.width), jnp.float32),
            pltpu.VMEM((3 * SEGS, size.frames), jnp.float32),
        ],
        compiler_params=pltpu.CompilerParams(vmem_limit_bytes=12 * MIB),
        cost_estimate=pl.CostEstimate(flops=4 * 10**9, bytes_accessed=10**6, transcendentals=0),
        name="edge",
    )(moved, first_got, second_got, token, before, coeffs)


def join_kernel(size, own, other, wide, token, out):
    out[0:8, 0:LANES] = own[0:8, 0:LANES] + other[0:8, 0:LANES]
    if out.shape[0] > 8:
        top, bottom = wide[0 : size.reach, :], wide[size.rows - size.reach : size.rows, :]
        out[8 : 8 + size.reach, :] = jnp.where(lax.axis_index("band") % 2 == 0, top, bottom)


def join(size, own, other, wide, token, with_labels):
    shape = (size.packed, size.width) if with_labels else (8, LANES)
    return pl.pallas_call(
        functools.partial(join_kernel, size),
        out_shape=jax.ShapeDtypeStruct(shape, jnp.float32),
        in_specs=[VMEM, VMEM, VMEM, pl.BlockSpec(memory_space=pl.ANY)],
        out_specs=VMEM,
        compiler_params=pltpu.CompilerParams(vmem_limit_bytes=2 * MIB),
        name="join",
    )(own, other, wide, token)


def put_kernel(send, own, other, out):
    bands, height, _ = out.shape
    for b in range(bands):
        out[b, height - 8 : height, :] = own[0:8, 0:LANES] + other[0:8, 0:LANES]


def put_total(send, own, other):
    return pl.pallas_call(
        put_kernel,
        out_shape=jax.ShapeDtypeStruct(send.shape, jnp.float32),
        in_specs=[VMEM] * 3,
        out_specs=VMEM,
        input_output_aliases={0: 0},
        compiler_params=pltpu.CompilerParams(vmem_limit_bytes=2 * MIB),
        name="put",
    )(send, own, other)


def finish_kernel(frame_total, blocks, out):
    bands, height, _ = blocks.shape
    half = height - 8
    summed = blocks[0]
    for b in range(1, bands):
        summed = summed + blocks[b]
    mean_total = jnp.sum(summed[half:, :]) / frame_total
    scaled = summed[:half] / mean_total
    width = out.shape[1]
    out[0:half, :] = scaled[:, :width]
    out[half:, :] = scaled[:, width:]


def finish(blocks, frame_count):
    half = frame_count // 2
    return pl.pallas_call(
        functools.partial(finish_kernel, float(frame_count * lax.axis_size("scan"))),
        out_shape=jax.ShapeDtypeStruct((2 * half, LANES // 2), jnp.float32),
        in_specs=[VMEM],
        out_specs=VMEM,
        compiler_params=pltpu.CompilerParams(vmem_limit_bytes=8 * MIB),
        name="finish",
    )(blocks)


def partner_steps():
    scans, bands = lax.axis_size("scan"), lax.axis_size("band")
    around = {0: 3, 1: 2, 2: 1, 3: 0}

    def x_around(s):
        return (s // 8) * 8 + around[s // 2 % 4] * 2 + s % 2

    def z_around(s):
        return around[s // 8] * 8 + s % 8

    def same(b):
        return b

    def upper_pair(b):
        return b ^ 1

    def lower_pair(b):
        return (((b + 1) % bands) ^ 1) - 1 if ((b + 1) % bands) ^ 1 else bands - 1

    moves = [
        (lambda s: s ^ 1, upper_pair),
        (lambda s: s ^ 2, lower_pair),
        (x_around, same),
        (lambda s: s ^ 8, same),
        (z_around, same),
    ]
    return [
        [(s * bands + b, move(s) * bands + turn(b)) for s in range(scans) for b in range(bands)]
        for move, turn in moves
    ]


def body(frame_codes, row_scales, row_shift, col_shift, segment_labels, mask_coeffs):
    frame_count, band_height, det_cols = frame_codes.shape
    size = Sizes(frame_count, band_height, det_cols)
    cleared, spread, wide = prepare(size, diagonals(size), row_scales, segment_labels)
    moved, total = shift_frames(size, row_shift, col_shift, spread, frame_codes, wide, cleared)
    coeffs = mask_coeffs.reshape(3 * SEGS, MASKS)
    steps = partner_steps()
    cuts = [band_height * i // (len(steps) - 1) for i in range(len(steps))]
    moments, got = None, []
    for i, pairs in enumerate(steps):
        got.append(lax.ppermute(total, ("scan", "band"), pairs))
        if i < len(steps) - 1:
            moments = core_rows(size, moved, wide, total, moments, cuts[i], cuts[i + 1])
            total = join(size, total, got[i], wide, moments, i == 0)
    send = edge_rows(size, moved, got[0], got[1], total, moments, coeffs)
    send = put_total(send, total, got[-1])
    blocks = lax.all_to_all(send, "band", 0, 0)
    return finish(blocks, frame_count)


def solution(mesh):
    return jax.shard_map(
        body,
        mesh=mesh,
        in_specs=(
            P("scan", "band", None),
            P("scan", "band"),
            P("scan"),
            P("scan"),
            P("band", None),
            P(),
        ),
        out_specs=P("scan", "band"),
        check_vma=False,
    )
```

time: 56.9 us -> 48.8 us (0.86); the launches traced: 56 us -> 48.7 us
  local copies, waits for them, and re-layouts: 5.71 us -> 1.52 us
  Pallas kernels: 18.4 us -> 15.9 us
  blocking collectives: 12.7 us -> 11.4 us
    unnamed x14 -> x12, local copies, waits for them, and re-layouts: 5.71 us -> 1.52 us
    pallas_call x1, Pallas kernels: 7.85 us -> 3.81 us  [shift_frames(): pl.pallas_call(functools.partial(shift_kernel, size), out_shape=[jax.Shap...]
    pallas_call x0 -> x7, Pallas kernels: none -> 1.29 us  [the longest x1 1.25 us: prepare(): pl.pallas_call(functools.partial(prepare_kernel, size), out_shape=[jax.Sh...]
    all_to_all x1, blocking collectives: 12.7 us -> 11.4 us  [body(): blocks = lax.all_to_all(send, 'band', 0, 0)]
    ppermute x7 -> x5, starting transfers between devices: 16.2 us -> 16.5 us  [body(): got.append(lax.ppermute(total, ('scan', 'band'), pairs))]
    pallas_call x3 -> x4, Pallas kernels: 7.16 us -> 7.47 us  [core_rows(): pl.pallas_call(functools.partial(core_kernel, size, first, last, before i...]
    ppermute x7 -> x5, waiting for transfers between devices: 2.89 us -> 3.15 us  [body(): got.append(lax.ppermute(total, ('scan', 'band'), pairs))]
  transfers between devices with their start and end apart: 7 -> 5, of which waited for: 2 -> 3; matrix products, arithmetic and copies ran while one was open for 0% -> 0% of each run, Pallas kernels for 13% -> 21%
where the time goes in v2:
time: 48.8 us; the launch traced here: 48.7 us
  starting transfers between devices  16.5 us (34%)
  Pallas kernels  15.9 us (33%)
  blocking collectives  11.4 us (23%)
  waiting for transfers between devices  3.15 us (6%)
  local copies, waits for them, and re-layouts  1.52 us (3%)
    ppermute x5, starting transfers between devices, body(): got.append(lax.ppermute(total, ('scan', 'band'), pairs))  16.5 us
    all_to_all x1, blocking collectives, body(): blocks = lax.all_to_all(send, 'band', 0, 0)  11.4 us
    pallas_call x4, Pallas kernels, core_rows(): pl.pallas_call(functools.partial(core_kernel, size, first, last, before i...  7.47 us
    pallas_call x1, Pallas kernels, shift_frames(): pl.pallas_call(functools.partial(shift_kernel, size), out_shape=[jax.Shap...  3.81 us
    ppermute x5, waiting for transfers between devices, body(): got.append(lax.ppermute(total, ('scan', 'band'), pairs))  3.15 us
    pallas_call x1, Pallas kernels, edge_rows(): pl.pallas_call(functools.partial(edge_kernel, size), out_shape=jax.ShapeD...  2.56 us
    unnamed x12, local copies, waits for them, and re-layouts  1.52 us
    pallas_call x1, Pallas kernels, prepare(): pl.pallas_call(functools.partial(prepare_kernel, size), out_shape=[jax.Sh...  1.25 us
  transfers between devices with their start and end apart: 5, of which 3 were waited for; matrix products, arithmetic and copies ran while one was open for 0% of the time, Pallas kernels for 21%

profile of v2, /device:TPU:6, one launch (start us, length us, event | category | flops | bytes accessed | tf_op | source)
XLA Modules:
  0.0 48.7 jit_solution(10317596917483742302)
XLA Ops:
  0.0 0.0 copy-start.4
  0.0 0.0 copy-start.5
  0.0 0.0 copy-start.3
  0.0 0.0 copy-start.2
  0.0 0.0 copy-start
  0.1 0.9 %copy-done.4 = s32[72,576]{1,0:T(8,128)S(1)} copy-done((s32[72,576]{1,0:T(8,128)S(1)}, s32[72,576]{1,0:T(8,128)}, u32[]{:S(2)}) %copy-start.4) | copy-done | bytes 165912
  0.9 0.0 copy-done.5
  0.9 1.2 %prepare.1 = (f32[5,5850,128]{2,1,0:T(8,128)S(1)}, f32[5120,128]{1,0:T(8,128)S(1)}, f32[72,640]{1,0:T(8,128)S(1)}) custom-call(bf16[80,256]{1,0:T(8,128)(2,1)S(1)} %diagonals.1.diagonal, f32[64,72]{1,0:T(8,128)S(1)} %copy-done.5, s32[72,576]{1,0:T(8,128)S(1)} %copy-done.4), custom_call_target="tpu_custom_call" | custom-call | flops 500000000 | bytes 1000000 | tf_op jit(solution)/shard_map/prepare/pallas_call | solution.py:97
  2.2 0.0 copy-done.3
  2.2 0.0 copy-done.2
  2.2 0.6 %copy-done = bf16[64,72,576]{2,1,0:T(8,128)(2,1)S(1)} copy-done((bf16[64,72,576]{2,1,0:T(8,128)(2,1)S(1)}, bf16[64,72,576]{2,1,0:T(8,128)(2,1)}, u32[]{:S(2)}) %copy-start) | copy-done | bytes 5308440
  2.8 3.8 %shift.1 = (f32[5,5850,128]{2,1,0:T(8,128)S(1)}, f32[24,640]{1,0:T(8,128)S(1)}) custom-call(s32[64]{0:T(128)S(1)} %copy-done.2, s32[64]{0:T(128)S(1)} %copy-done.3, f32[5120,128]{1,0:T(8,128)S(1)} %get-tuple-element.10.spread, bf16[64,72,576]{2,1,0:T(8,128)(2,1)S(1)} %copy-done, ...), custom_call_target="tpu_custom_call", output_to_operand_aliasing={{0}: (5, {})} | custom-call | flops 6000000000 | bytes 1000000 | tf_op jit(solution)/shard_map/shift/pallas_call | solution.py:160
  6.7 1.1 %collective-permute-start = (f32[24,640]{1,0:T(8,128)S(1)}, f32[24,640]{1,0:T(8,128)S(1)}, u32[]{:S(2)}, u32[]{:S(2)}) collective-permute-start(f32[24,640]{1,0:T(8,128)S(1)} %get-tuple-element.14.token.own), channel_id=1, source_target_pairs={{0,9},{1,8},{2,11},{3,10},{4,13},{5,12},{6,15},{7,14},{8,1},{9,0},... | collective-permute-start | bytes 184328 | tf_op jit(solution)/shard_map/ppermute | solution.py:416
  7.8 1.9 %core.4.token.refs_0_ = f32[384,64]{1,0:T(8,128)S(1)} custom-call(f32[5,5850,128]{2,1,0:T(8,128)S(1)} %get-tuple-element.13.moved, f32[72,640]{1,0:T(8,128)S(1)} %get-tuple-element.11.wide, f32[24,640]{1,0:T(8,128)S(1)} %get-tuple-element.14.token.own), custom_call_target="tpu_custom_call" | custom-call | flops 4000000000 | bytes 1000000 | tf_op jit(solution)/shard_map/core/pallas_call | solution.py:236
  9.6 1.3 %collective-permute-done.other.first_got = f32[24,640]{1,0:T(8,128)S(1)} collective-permute-done((f32[24,640]{1,0:T(8,128)S(1)}, f32[24,640]{1,0:T(8,128)S(1)}, u32[]{:S(2)}, u32[]{:S(2)}) %collective-permute-start) | collective-permute-done | bytes 61472 | tf_op jit(solution)/shard_map/ppermute | solution.py:416
  10.9 4.8 %collective-permute-start.1 = (f32[24,640]{1,0:T(8,128)S(1)}, f32[24,640]{1,0:T(8,128)S(1)}, u32[]{:S(2)}, u32[]{:S(2)}) collective-permute-start(f32[24,640]{1,0:T(8,128)S(1)} %join.4.token.own), channel_id=1, source_target_pairs={{0,23},{1,18},{2,17},{3,20},{4,19},{5,22},{6,21},{7,16},{8,31},{9,... | collective-permute-start | bytes 184328 | tf_op jit(solution)/shard_map/ppermute | solution.py:416
  15.8 1.9 %core.5.token.refs_0_ = f32[384,64]{1,0:T(8,128)S(1)} custom-call(f32[5,5850,128]{2,1,0:T(8,128)S(1)} %get-tuple-element.13.moved, f32[72,640]{1,0:T(8,128)S(1)} %get-tuple-element.11.wide, f32[24,640]{1,0:T(8,128)S(1)} %join.4.token.own, f32[384,64]{1,0:T(8,128)S(1)} %core.4.token.refs_0_), custom_call_target="tpu_custom_call" | custom-call | flops 4000000000 | bytes 1000000 | tf_op jit(solution)/shard_map/core/pallas_call | solution.py:236
  17.6 0.6 %collective-permute-done.1.other.second_got = f32[24,640]{1,0:T(8,128)S(1)} collective-permute-done((f32[24,640]{1,0:T(8,128)S(1)}, f32[24,640]{1,0:T(8,128)S(1)}, u32[]{:S(2)}, u32[]{:S(2)}) %collective-permute-start.1) | collective-permute-done | bytes 61472 | tf_op jit(solution)/shard_map/ppermute | solution.py:416
  18.2 0.0 copy-start.1
  18.2 1.7 %collective-permute-start.2 = (f32[8,128]{1,0:T(8,128)S(1)}, f32[8,128]{1,0:T(8,128)S(1)}, u32[]{:S(2)}, u32[]{:S(2)}) collective-permute-start(f32[8,128]{1,0:T(8,128)S(1)} %join.5.token.own), channel_id=1, source_target_pairs={{0,48},{1,49},{2,50},{3,51},{4,52},{5,53},{6,54},{7,55},{8,56},{9,... | collective-permute-start | bytes 12296 | tf_op jit(solution)/shard_map/ppermute | solution.py:416
  19.9 1.9 %core.6.token.refs_0_ = f32[384,64]{1,0:T(8,128)S(1)} custom-call(f32[5,5850,128]{2,1,0:T(8,128)S(1)} %get-tuple-element.13.moved, f32[72,640]{1,0:T(8,128)S(1)} %get-tuple-element.11.wide, f32[8,128]{1,0:T(8,128)S(1)} %join.5.token.own, f32[384,64]{1,0:T(8,128)S(1)} %core.5.token.refs_0_), custom_call_target="tpu_custom_call" | custom-call | flops 4000000000 | bytes 1000000 | tf_op jit(solution)/shard_map/core/pallas_call | solution.py:236
  21.8 1.3 %collective-permute-done.2.other = f32[8,128]{1,0:T(8,128)S(1)} collective-permute-done((f32[8,128]{1,0:T(8,128)S(1)}, f32[8,128]{1,0:T(8,128)S(1)}, u32[]{:S(2)}, u32[]{:S(2)}) %collective-permute-start.2) | collective-permute-done | bytes 4128 | tf_op jit(solution)/shard_map/ppermute | solution.py:416
  23.1 3.3 %collective-permute-start.3 = (f32[8,128]{1,0:T(8,128)S(1)}, f32[8,128]{1,0:T(8,128)S(1)}, u32[]{:S(2)}, u32[]{:S(2)}) collective-permute-start(f32[8,128]{1,0:T(8,128)S(1)} %join.6.token.own), channel_id=1, source_target_pairs={{0,64},{1,65},{2,66},{3,67},{4,68},{5,69},{6,70},{7,71},{8,72},{9,... | collective-permute-start | bytes 12296 | tf_op jit(solution)/shard_map/ppermute | solution.py:416
  26.3 1.9 %core.7.token.before = f32[384,64]{1,0:T(8,128)S(1)} custom-call(f32[5,5850,128]{2,1,0:T(8,128)S(1)} %get-tuple-element.13.moved, f32[72,640]{1,0:T(8,128)S(1)} %get-tuple-element.11.wide, f32[8,128]{1,0:T(8,128)S(1)} %join.6.token.own, f32[384,64]{1,0:T(8,128)S(1)} %core.6.token.refs_0_), custom_call_target="tpu_custom_call" | custom-call | flops 4000000000 | bytes 1000000 | tf_op jit(solution)/shard_map/core/pallas_call | solution.py:236
  28.2 0.0 collective-permute-done.3.other
  28.2 5.6 %collective-permute-start.4 = (f32[8,128]{1,0:T(8,128)S(1)}, f32[8,128]{1,0:T(8,128)S(1)}, u32[]{:S(2)}, u32[]{:S(2)}) collective-permute-start(f32[8,128]{1,0:T(8,128)S(1)} %join.7.token.own), channel_id=1, source_target_pairs={{0,192},{1,193},{2,194},{3,195},{4,196},{5,197},{6,198},{7,199},{8... | collective-permute-start | bytes 12296 | tf_op jit(solution)/shard_map/ppermute | solution.py:416
  33.9 0.0 copy-done.1
  33.9 2.6 %edge.1.send = f32[8,40,128]{2,1,0:T(8,128)S(1)} custom-call(f32[5,5850,128]{2,1,0:T(8,128)S(1)} %get-tuple-element.13.moved, f32[24,640]{1,0:T(8,128)S(1)} %collective-permute-done.other.first_got, f32[24,640]{1,0:T(8,128)S(1)} %collective-permute-done.1.other.second_got, f32[8,128]{1,0:T(8,128)S(1)} %join.7.token.own, f32[384,64]{1,0:T(8,128)S(1)} %core.7.token.before, ...), custom_call_target="tpu_custom_call" | custom-call | flops 4000000000 | bytes 1000000 | tf_op jit(solution)/shard_map/edge/pallas_call | solution.py:295
  36.4 0.0 collective-permute-done.4.other
  36.5 11.4 %all_to_all.5.blocks = f32[8,40,128]{2,1,0:T(8,128)S(1)} all-to-all(f32[8,40,128]{2,1,0:T(8,128)S(1)} %put.1), channel_id=1, replica_groups=mesh['scan'=32,'band'=8] {'band'}, dimensions={0} | all-to-all | bytes 327680 | tf_op jit(solution)/shard_map/all_to_all | solution.py:422
  47.9 0.8 %finish.1 = f32[64,64]{1,0:T(8,128)} custom-call(f32[8,40,128]{2,1,0:T(8,128)S(1)} %all_to_all.5.blocks), custom_call_target="tpu_custom_call" | custom-call | tf_op jit(solution)/shard_map/finish/pallas_call | solution.py:364
  (6 shorter events, 0.0 us)
Async XLA Ops:
  0.0 0.9 %copy-start.4 = (s32[72,576]{1,0:T(8,128)S(1)}, s32[72,576]{1,0:T(8,128)}, u32[]{:S(2)}) copy-start(s32[72,576]{1,0:T(8,128)} %labels.1) | copy-start | bytes 497668
  0.0 0.9 %copy-start.5 = (f32[64,72]{1,0:T(8,128)S(1)}, f32[64,72]{1,0:T(8,128)}, u32[]{:S(2)}) copy-start(f32[64,72]{1,0:T(8,128)} %scales.1) | copy-start | bytes 55300
  0.0 2.2 %copy-start.3 = (s32[64]{0:T(128)S(1)}, s32[64]{0:T(128)}, u32[]{:S(2)}) copy-start(s32[64]{0:T(128)} %col_shift.1) | copy-start | bytes 772
  0.0 2.2 %copy-start.2 = (s32[64]{0:T(128)S(1)}, s32[64]{0:T(128)}, u32[]{:S(2)}) copy-start(s32[64]{0:T(128)} %row_shift.1) | copy-start | bytes 772
  0.0 2.8 %copy-start = (bf16[64,72,576]{2,1,0:T(8,128)(2,1)S(1)}, bf16[64,72,576]{2,1,0:T(8,128)(2,1)}, u32[]{:S(2)}) copy-start(bf16[64,72,576]{2,1,0:T(8,128)(2,1)} %codes.1) | copy-start | bytes 15925252
  6.7 4.3 %collective-permute-start = (f32[24,640]{1,0:T(8,128)S(1)}, f32[24,640]{1,0:T(8,128)S(1)}, u32[]{:S(2)}, u32[]{:S(2)}) collective-permute-start(f32[24,640]{1,0:T(8,128)S(1)} %get-tuple-element.14.token.own), channel_id=1, source_target_pairs={{0,9},{1,8},{2,11},{3,10},{4,13},{5,12},{6,15},{7,14},{8,1},{9,0},... | collective-permute-start | bytes 184328 | tf_op jit(solution)/shard_map/ppermute | solution.py:416
  10.9 7.3 %collective-permute-start.1 = (f32[24,640]{1,0:T(8,128)S(1)}, f32[24,640]{1,0:T(8,128)S(1)}, u32[]{:S(2)}, u32[]{:S(2)}) collective-permute-start(f32[24,640]{1,0:T(8,128)S(1)} %join.4.token.own), channel_id=1, source_target_pairs={{0,23},{1,18},{2,17},{3,20},{4,19},{5,22},{6,21},{7,16},{8,31},{9,... | collective-permute-start | bytes 184328 | tf_op jit(solution)/shard_map/ppermute | solution.py:416
  18.2 15.6 %copy-start.1 = (f32[3,128,512]{2,1,0:T(8,128)S(1)}, f32[3,128,512]{2,1,0:T(8,128)}, u32[]{:S(2)}) copy-start(f32[3,128,512]{2,1,0:T(8,128)} %param.11) | copy-start | bytes 2359300
  18.2 4.8 %collective-permute-start.2 = (f32[8,128]{1,0:T(8,128)S(1)}, f32[8,128]{1,0:T(8,128)S(1)}, u32[]{:S(2)}, u32[]{:S(2)}) collective-permute-start(f32[8,128]{1,0:T(8,128)S(1)} %join.5.token.own), channel_id=1, source_target_pairs={{0,48},{1,49},{2,50},{3,51},{4,52},{5,53},{6,54},{7,55},{8,56},{9,... | collective-permute-start | bytes 12296 | tf_op jit(solution)/shard_map/ppermute | solution.py:416
  23.1 5.1 %collective-permute-start.3 = (f32[8,128]{1,0:T(8,128)S(1)}, f32[8,128]{1,0:T(8,128)S(1)}, u32[]{:S(2)}, u32[]{:S(2)}) collective-permute-start(f32[8,128]{1,0:T(8,128)S(1)} %join.6.token.own), channel_id=1, source_target_pairs={{0,64},{1,65},{2,66},{3,67},{4,68},{5,69},{6,70},{7,71},{8,72},{9,... | collective-permute-start | bytes 12296 | tf_op jit(solution)/shard_map/ppermute | solution.py:416
  28.2 8.2 %collective-permute-start.4 = (f32[8,128]{1,0:T(8,128)S(1)}, f32[8,128]{1,0:T(8,128)S(1)}, u32[]{:S(2)}, u32[]{:S(2)}) collective-permute-start(f32[8,128]{1,0:T(8,128)S(1)} %join.7.token.own), channel_id=1, source_target_pairs={{0,192},{1,193},{2,194},{3,195},{4,196},{5,197},{6,198},{7,199},{8... | collective-permute-start | bytes 12296 | tf_op jit(solution)/shard_map/ppermute | solution.py:416

commit v3 on v2

--- a/solution.py
+++ b/solution.py
@@ -26,7 +26,7 @@
         self.width = self.tiles * LANES
         self.pitch = frame_count + 1
         self.tall = -(-band_height // 16) * 16
-        self.packed = 8 + -(-self.reach // 8) * 8
+        self.packed = -(-(self.reach + 3) // 16) * 16
 
 
 def widened(size, labels):
@@ -110,7 +110,24 @@
     )(diagonal, scales, labels)
 
 
-def shift_kernel(size, row_shift, col_shift, spread, codes, wide, cleared, moved, payload, total):
+def pack(size, out, lines, labels, sums):
+    high = sums.astype(jnp.bfloat16).astype(jnp.float32)
+    middle = (sums - high).astype(jnp.bfloat16).astype(jnp.float32)
+    lines[...] = jnp.zeros(lines.shape, jnp.float32)
+    lines[0 : size.reach, :] = labels
+    for k, part in enumerate([high, middle, sums - high - middle]):
+        lines[size.reach + k : size.reach + k + 1, 0:LANES] = part
+    out[...] = lines[...].astype(jnp.bfloat16)
+
+
+def packed_sums(size, message):
+    parts = message[...].astype(jnp.float32)[size.reach : size.reach + 3, 0:LANES]
+    return parts[0:1] + parts[1:2] + parts[2:3]
+
+
+def shift_kernel(
+    size, row_shift, col_shift, spread, codes, wide, cleared, moved, payload, total, lines
+):
     frames, rows, cols, tiles, reach = size.frames, size.rows, size.cols, size.tiles, size.reach
     total[...] = jnp.zeros((rows, LANES), jnp.float32)
     whole_lane = lax.broadcasted_iota(jnp.int32, (rows, LANES), 1)
@@ -151,9 +168,9 @@
         return carry
 
     lax.fori_loop(0, frames, shift_frame, 0, unroll=4)
-    payload[0:8, 0:LANES] = jnp.sum(total[...].reshape(rows // 8, 8, LANES), axis=0)
     top, bottom = wide[0:reach, :], wide[rows - reach : rows, :]
-    payload[8 : 8 + reach, :] = jnp.where(band % 2 == 0, bottom, top)
+    labels = jnp.where(band % 2 == 1, bottom, top)
+    pack(size, payload, lines, labels, jnp.sum(total[...], axis=0, keepdims=True))
 
 
 def shift_frames(size, row_shift, col_shift, spread, codes, wide, cleared):
@@ -161,11 +178,14 @@
         functools.partial(shift_kernel, size),
         out_shape=[
             jax.ShapeDtypeStruct(cleared.shape, jnp.float32),
-            jax.ShapeDtypeStruct((size.packed, size.width), jnp.float32),
+            jax.ShapeDtypeStruct((size.packed, size.width), jnp.bfloat16),
         ],
         in_specs=[SMEM] * 2 + [VMEM] * 4,
         out_specs=[VMEM] * 2,
-        scratch_shapes=[pltpu.VMEM((size.rows, LANES), jnp.float32)],
+        scratch_shapes=[
+            pltpu.VMEM((size.rows, LANES), jnp.float32),
+            pltpu.VMEM((size.packed, size.width), jnp.float32),
+        ],
         input_output_aliases={5: 0},
         compiler_params=pltpu.CompilerParams(vmem_limit_bytes=12 * MIB),
         cost_estimate=pl.CostEstimate(flops=6 * 10**9, bytes_accessed=10**6, transcendentals=0),
@@ -248,10 +268,11 @@
     frames, rows, reach = size.frames, size.rows, size.reach
     moments[...] = before[...]
     band, bands = lax.axis_index("band"), lax.axis_size("band")
-    even = band % 2 == 0
-    first, second = first_got[8 : 8 + reach, :], second_got[8 : 8 + reach, :]
-    wide[0:reach, :] = jnp.where(even, second, first)
-    wide[reach : 2 * reach, :] = jnp.where(even, first, second)
+    odd = band % 2 == 1
+    first = first_got[...].astype(jnp.float32)[0:reach, :]
+    second = second_got[...].astype(jnp.float32)[0:reach, :]
+    wide[0:reach, :] = jnp.where(odd, second, first)
+    wide[reach : 2 * reach, :] = jnp.where(odd, first, second)
     nothing = jnp.full((reach, size.width), -1.0, jnp.float32)
 
     @pl.when(band == 0)
@@ -309,20 +330,31 @@
     )(moved, first_got, second_got, token, before, coeffs)
 
 
-def join_kernel(size, own, other, wide, token, out):
-    out[0:8, 0:LANES] = own[0:8, 0:LANES] + other[0:8, 0:LANES]
-    if out.shape[0] > 8:
-        top, bottom = wide[0 : size.reach, :], wide[size.rows - size.reach : size.rows, :]
-        out[8 : 8 + size.reach, :] = jnp.where(lax.axis_index("band") % 2 == 0, top, bottom)
-
-
-def join(size, own, other, wide, token, with_labels):
-    shape = (size.packed, size.width) if with_labels else (8, LANES)
-    return pl.pallas_call(
-        functools.partial(join_kernel, size),
-        out_shape=jax.ShapeDtypeStruct(shape, jnp.float32),
+def first_join_kernel(size, own, other, wide, token, out, lines):
+    top, bottom = wide[0 : size.reach, :], wide[size.rows - size.reach : size.rows, :]
+    labels = jnp.where(lax.axis_index("band") % 2 == 1, top, bottom)
+    pack(size, out, lines, labels, packed_sums(size, own) + packed_sums(size, other))
+
+
+def second_join_kernel(size, own, other, wide, token, out, lines):
+    out[...] = jnp.zeros(out.shape, jnp.float32)
+    out[0:1, :] = packed_sums(size, own) + packed_sums(size, other)
+
+
+def join_kernel(size, own, other, wide, token, out, lines):
+    out[...] = own[...] + other[...]
+
+
+def join(size, kernel, own, other, wide, token):
+    out = jax.ShapeDtypeStruct((8, LANES), jnp.float32)
+    if kernel is first_join_kernel:
+        out = jax.ShapeDtypeStruct(own.shape, own.dtype)
+    return pl.pallas_call(
+        functools.partial(kernel, size),
+        out_shape=out,
         in_specs=[VMEM, VMEM, VMEM, pl.BlockSpec(memory_space=pl.ANY)],
         out_specs=VMEM,
+        scratch_shapes=[pltpu.VMEM((size.packed, size.width), jnp.float32)],
         compiler_params=pltpu.CompilerParams(vmem_limit_bytes=2 * MIB),
         name="join",
     )(own, other, wide, token)
@@ -331,7 +363,7 @@
 def put_kernel(send, own, other, out):
     bands, height, _ = out.shape
     for b in range(bands):
-        out[b, height - 8 : height, :] = own[0:8, 0:LANES] + other[0:8, 0:LANES]
+        out[b, height - 8 : height, :] = own[...] + other[...]
 
 
 def put_total(send, own, other):
@@ -388,14 +420,14 @@
         return b ^ 1
 
     def lower_pair(b):
-        return (((b + 1) % bands) ^ 1) - 1 if ((b + 1) % bands) ^ 1 else bands - 1
+        return b if b in (0, bands - 1) else ((b + 1) ^ 1) - 1
 
     moves = [
-        (lambda s: s ^ 1, upper_pair),
-        (lambda s: s ^ 2, lower_pair),
-        (x_around, same),
+        (lambda s: s ^ 1, lower_pair),
+        (x_around, upper_pair),
         (lambda s: s ^ 8, same),
         (z_around, same),
+        (lambda s: s ^ 2, same),
     ]
     return [
         [(s * bands + b, move(s) * bands + turn(b)) for s in range(scans) for b in range(bands)]
@@ -411,12 +443,13 @@
     coeffs = mask_coeffs.reshape(3 * SEGS, MASKS)
     steps = partner_steps()
     cuts = [band_height * i // (len(steps) - 1) for i in range(len(steps))]
+    joins = [first_join_kernel, second_join_kernel, join_kernel, join_kernel]
     moments, got = None, []
     for i, pairs in enumerate(steps):
         got.append(lax.ppermute(total, ("scan", "band"), pairs))
         if i < len(steps) - 1:
             moments = core_rows(size, moved, wide, total, moments, cuts[i], cuts[i + 1])
-            total = join(size, total, got[i], wide, moments, i == 0)
+            total = join(size, joins[i], total, got[i], wide, moments)
     send = edge_rows(size, moved, got[0], got[1], total, moments, coeffs)
     send = put_total(send, total, got[-1])
     blocks = lax.all_to_all(send, "band", 0, 0)

time: 48.8 us -> 46.7 us (0.957)
  starting transfers between devices: 16.5 us -> 12.2 us
  blocking collectives: 11.4 us -> 14.5 us
  waiting for transfers between devices: 3.15 us -> 2.15 us
    ppermute x5, starting transfers between devices: 16.5 us -> 12.2 us  [body(): got.append(lax.ppermute(total, ('scan', 'band'), pairs))]
    all_to_all x1, blocking collectives: 11.4 us -> 14.5 us  [body(): blocks = lax.all_to_all(send, 'band', 0, 0)]
    ppermute x5, waiting for transfers between devices: 3.15 us -> 2.15 us  [body(): got.append(lax.ppermute(total, ('scan', 'band'), pairs))]
  transfers between devices with their start and end apart: 5 -> 5, of which waited for: 3 -> 2; matrix products, arithmetic and copies ran while one was open for 0% -> 0% of each run, Pallas kernels for 21% -> 22%
where the time goes in v3:
time: 46.7 us; the launch traced here: 46.4 us
  Pallas kernels  16 us (34%)
  blocking collectives  14.5 us (31%)
  starting transfers between devices  12.2 us (26%)
  waiting for transfers between devices  2.15 us (5%)
  local copies, waits for them, and re-layouts  1.52 us (3%)
    all_to_all x1, blocking collectives, body(): blocks = lax.all_to_all(send, 'band', 0, 0)  14.5 us
    ppermute x5, starting transfers between devices, body(): got.append(lax.ppermute(total, ('scan', 'band'), pairs))  12.2 us
    pallas_call x4, Pallas kernels, core_rows(): pl.pallas_call(functools.partial(core_kernel, size, first, last, before i...  7.45 us
    pallas_call x1, Pallas kernels, shift_frames(): pl.pallas_call(functools.partial(shift_kernel, size), out_shape=[jax.Shap...  3.82 us
    pallas_call x1, Pallas kernels, edge_rows(): pl.pallas_call(functools.partial(edge_kernel, size), out_shape=jax.ShapeD...  2.57 us
    ppermute x5, waiting for transfers between devices, body(): got.append(lax.ppermute(total, ('scan', 'band'), pairs))  2.15 us
    unnamed x12, local copies, waits for them, and re-layouts  1.52 us
    pallas_call x1, Pallas kernels, prepare(): pl.pallas_call(functools.partial(prepare_kernel, size), out_shape=[jax.Sh...  1.25 us
  transfers between devices with their start and end apart: 5, of which 2 were waited for; matrix products, arithmetic and copies ran while one was open for 0% of the time, Pallas kernels for 22%

profile of v3, /device:TPU:6, one launch (start us, length us, event | category | flops | bytes accessed | tf_op | source)
XLA Modules:
  0.0 46.4 jit_solution(3926061780583215599)
XLA Ops:
  0.0 0.0 copy-start.4
  0.0 0.0 copy-start.5
  0.0 0.0 copy-start.3
  0.0 0.0 copy-start.2
  0.0 0.0 copy-start
  0.1 0.9 %copy-done.4 = s32[72,576]{1,0:T(8,128)S(1)} copy-done((s32[72,576]{1,0:T(8,128)S(1)}, s32[72,576]{1,0:T(8,128)}, u32[]{:S(2)}) %copy-start.4) | copy-done | bytes 165912
  0.9 0.0 copy-done.5
  0.9 1.2 %prepare.1 = (f32[5,5850,128]{2,1,0:T(8,128)S(1)}, f32[5120,128]{1,0:T(8,128)S(1)}, f32[72,640]{1,0:T(8,128)S(1)}) custom-call(bf16[80,256]{1,0:T(8,128)(2,1)S(1)} %diagonals.1.diagonal, f32[64,72]{1,0:T(8,128)S(1)} %copy-done.5, s32[72,576]{1,0:T(8,128)S(1)} %copy-done.4), custom_call_target="tpu_custom_call" | custom-call | flops 500000000 | bytes 1000000 | tf_op jit(solution)/shard_map/prepare/pallas_call | solution.py:97
  2.2 0.0 copy-done.3
  2.2 0.0 copy-done.2
  2.2 0.6 %copy-done = bf16[64,72,576]{2,1,0:T(8,128)(2,1)S(1)} copy-done((bf16[64,72,576]{2,1,0:T(8,128)(2,1)S(1)}, bf16[64,72,576]{2,1,0:T(8,128)(2,1)}, u32[]{:S(2)}) %copy-start) | copy-done | bytes 5308440
  2.8 3.8 %shift.1 = (f32[5,5850,128]{2,1,0:T(8,128)S(1)}, bf16[16,640]{1,0:T(8,128)(2,1)S(1)}) custom-call(s32[64]{0:T(128)S(1)} %copy-done.2, s32[64]{0:T(128)S(1)} %copy-done.3, f32[5120,128]{1,0:T(8,128)S(1)} %get-tuple-element.10.spread, bf16[64,72,576]{2,1,0:T(8,128)(2,1)S(1)} %copy-done, ...), custom_call_target="tpu_custom_call", output_to_operand_aliasing={{0}: (5, {})} | custom-call | flops 6000000000 | bytes 1000000 | tf_op jit(solution)/shard_map/shift/pallas_call | solution.py:177
  6.7 0.1 collective-permute-start
  6.7 1.9 %core.4.token.refs_0_ = f32[384,64]{1,0:T(8,128)S(1)} custom-call(f32[5,5850,128]{2,1,0:T(8,128)S(1)} %get-tuple-element.13.moved, f32[72,640]{1,0:T(8,128)S(1)} %get-tuple-element.11.wide, bf16[16,640]{1,0:T(8,128)(2,1)S(1)} %get-tuple-element.14.token.own), custom_call_target="tpu_custom_call" | custom-call | flops 4000000000 | bytes 1000000 | tf_op jit(solution)/shard_map/core/pallas_call | solution.py:256
  8.6 0.0 collective-permute-done.other.first_got
  8.7 3.0 %collective-permute-start.1 = (bf16[16,640]{1,0:T(8,128)(2,1)S(1)}, bf16[16,640]{1,0:T(8,128)(2,1)S(1)}, u32[]{:S(2)}, u32[]{:S(2)}) collective-permute-start(bf16[16,640]{1,0:T(8,128)(2,1)S(1)} %join.4.token.own), channel_id=1, source_target_pairs={{0,49},{1,48},{2,51},{3,50},{4,53},{5,52},{6,55},{7,54},{8,57},{9,... | collective-permute-start | bytes 61448 | tf_op jit(solution)/shard_map/ppermute | solution.py:449
  11.6 1.9 %core.5.token.refs_0_ = f32[384,64]{1,0:T(8,128)S(1)} custom-call(f32[5,5850,128]{2,1,0:T(8,128)S(1)} %get-tuple-element.13.moved, f32[72,640]{1,0:T(8,128)S(1)} %get-tuple-element.11.wide, bf16[16,640]{1,0:T(8,128)(2,1)S(1)} %join.4.token.own, f32[384,64]{1,0:T(8,128)S(1)} %core.4.token.refs_0_), custom_call_target="tpu_custom_call" | custom-call | flops 4000000000 | bytes 1000000 | tf_op jit(solution)/shard_map/core/pallas_call | solution.py:256
  13.5 1.1 %collective-permute-done.1.other.second_got = bf16[16,640]{1,0:T(8,128)(2,1)S(1)} collective-permute-done((bf16[16,640]{1,0:T(8,128)(2,1)S(1)}, bf16[16,640]{1,0:T(8,128)(2,1)S(1)}, u32[]{:S(2)}, u32[]{:S(2)}) %collective-permute-start.1) | collective-permute-done | bytes 20512 | tf_op jit(solution)/shard_map/ppermute | solution.py:449
  14.6 0.0 copy-start.1
  14.7 3.4 %collective-permute-start.2 = (f32[8,128]{1,0:T(8,128)S(1)}, f32[8,128]{1,0:T(8,128)S(1)}, u32[]{:S(2)}, u32[]{:S(2)}) collective-permute-start(f32[8,128]{1,0:T(8,128)S(1)} %join.5.token.own), channel_id=1, source_target_pairs={{0,64},{1,65},{2,66},{3,67},{4,68},{5,69},{6,70},{7,71},{8,72},{9,... | collective-permute-start | bytes 12296 | tf_op jit(solution)/shard_map/ppermute | solution.py:449
  18.0 1.9 %core.6.token.refs_0_ = f32[384,64]{1,0:T(8,128)S(1)} custom-call(f32[5,5850,128]{2,1,0:T(8,128)S(1)} %get-tuple-element.13.moved, f32[72,640]{1,0:T(8,128)S(1)} %get-tuple-element.11.wide, f32[8,128]{1,0:T(8,128)S(1)} %join.5.token.own, f32[384,64]{1,0:T(8,128)S(1)} %core.5.token.refs_0_), custom_call_target="tpu_custom_call" | custom-call | flops 4000000000 | bytes 1000000 | tf_op jit(solution)/shard_map/core/pallas_call | solution.py:256
  19.9 0.0 collective-permute-done.2.other
  19.9 5.6 %collective-permute-start.3 = (f32[8,128]{1,0:T(8,128)S(1)}, f32[8,128]{1,0:T(8,128)S(1)}, u32[]{:S(2)}, u32[]{:S(2)}) collective-permute-start(f32[8,128]{1,0:T(8,128)S(1)} %join.6.token.own), channel_id=1, source_target_pairs={{0,192},{1,193},{2,194},{3,195},{4,196},{5,197},{6,198},{7,199},{8... | collective-permute-start | bytes 12296 | tf_op jit(solution)/shard_map/ppermute | solution.py:449
  25.6 1.9 %core.7.token.before = f32[384,64]{1,0:T(8,128)S(1)} custom-call(f32[5,5850,128]{2,1,0:T(8,128)S(1)} %get-tuple-element.13.moved, f32[72,640]{1,0:T(8,128)S(1)} %get-tuple-element.11.wide, f32[8,128]{1,0:T(8,128)S(1)} %join.6.token.own, f32[384,64]{1,0:T(8,128)S(1)} %core.6.token.refs_0_), custom_call_target="tpu_custom_call" | custom-call | flops 4000000000 | bytes 1000000 | tf_op jit(solution)/shard_map/core/pallas_call | solution.py:256
  27.4 0.0 collective-permute-done.3.other
  27.4 0.1 collective-permute-start.4
  27.5 0.0 copy-done.1
  27.6 2.6 %edge.1.send = f32[8,40,128]{2,1,0:T(8,128)S(1)} custom-call(f32[5,5850,128]{2,1,0:T(8,128)S(1)} %get-tuple-element.13.moved, bf16[16,640]{1,0:T(8,128)(2,1)S(1)} %collective-permute-done.other.first_got, bf16[16,640]{1,0:T(8,128)(2,1)S(1)} %collective-permute-done.1.other.second_got, f32[8,128]{1,0:T(8,128)S(1)} %join.7.token.own, ...), custom_call_target="tpu_custom_call" | custom-call | flops 4000000000 | bytes 1000000 | tf_op jit(solution)/shard_map/edge/pallas_call | solution.py:316
  30.1 1.0 %collective-permute-done.4.other = f32[8,128]{1,0:T(8,128)S(1)} collective-permute-done((f32[8,128]{1,0:T(8,128)S(1)}, f32[8,128]{1,0:T(8,128)S(1)}, u32[]{:S(2)}, u32[]{:S(2)}) %collective-permute-start.4) | collective-permute-done | bytes 4128 | tf_op jit(solution)/shard_map/ppermute | solution.py:449
  31.1 14.5 %all_to_all.5.blocks = f32[8,40,128]{2,1,0:T(8,128)S(1)} all-to-all(f32[8,40,128]{2,1,0:T(8,128)S(1)} %put.1), channel_id=1, replica_groups=mesh['scan'=32,'band'=8] {'band'}, dimensions={0} | all-to-all | bytes 327680 | tf_op jit(solution)/shard_map/all_to_all | solution.py:455
  45.6 0.8 %finish.1 = f32[64,64]{1,0:T(8,128)} custom-call(f32[8,40,128]{2,1,0:T(8,128)S(1)} %all_to_all.5.blocks), custom_call_target="tpu_custom_call" | custom-call | tf_op jit(solution)/shard_map/finish/pallas_call | solution.py:396
  (6 shorter events, 0.1 us)
Async XLA Ops:
  0.0 0.9 %copy-start.4 = (s32[72,576]{1,0:T(8,128)S(1)}, s32[72,576]{1,0:T(8,128)}, u32[]{:S(2)}) copy-start(s32[72,576]{1,0:T(8,128)} %labels.1) | copy-start | bytes 497668
  0.0 0.9 %copy-start.5 = (f32[64,72]{1,0:T(8,128)S(1)}, f32[64,72]{1,0:T(8,128)}, u32[]{:S(2)}) copy-start(f32[64,72]{1,0:T(8,128)} %scales.1) | copy-start | bytes 55300
  0.0 2.2 %copy-start.3 = (s32[64]{0:T(128)S(1)}, s32[64]{0:T(128)}, u32[]{:S(2)}) copy-start(s32[64]{0:T(128)} %col_shift.1) | copy-start | bytes 772
  0.0 2.2 %copy-start.2 = (s32[64]{0:T(128)S(1)}, s32[64]{0:T(128)}, u32[]{:S(2)}) copy-start(s32[64]{0:T(128)} %row_shift.1) | copy-start | bytes 772
  0.0 2.8 %copy-start = (bf16[64,72,576]{2,1,0:T(8,128)(2,1)S(1)}, bf16[64,72,576]{2,1,0:T(8,128)(2,1)}, u32[]{:S(2)}) copy-start(bf16[64,72,576]{2,1,0:T(8,128)(2,1)} %codes.1) | copy-start | bytes 15925252
  6.7 2.0 %collective-permute-start = (bf16[16,640]{1,0:T(8,128)(2,1)S(1)}, bf16[16,640]{1,0:T(8,128)(2,1)S(1)}, u32[]{:S(2)}, u32[]{:S(2)}) collective-permute-start(bf16[16,640]{1,0:T(8,128)(2,1)S(1)} %get-tuple-element.14.token.own), channel_id=1, source_target_pairs={{0,8},{1,10},{2,9},{3,12},{4,11},{5,14},{6,13},{7,15},{8,0},{9,2},... | collective-permute-start | bytes 61448 | tf_op jit(solution)/shard_map/ppermute | solution.py:449
  8.7 6.0 %collective-permute-start.1 = (bf16[16,640]{1,0:T(8,128)(2,1)S(1)}, bf16[16,640]{1,0:T(8,128)(2,1)S(1)}, u32[]{:S(2)}, u32[]{:S(2)}) collective-permute-start(bf16[16,640]{1,0:T(8,128)(2,1)S(1)} %join.4.token.own), channel_id=1, source_target_pairs={{0,49},{1,48},{2,51},{3,50},{4,53},{5,52},{6,55},{7,54},{8,57},{9,... | collective-permute-start | bytes 61448 | tf_op jit(solution)/shard_map/ppermute | solution.py:449
  14.6 12.9 %copy-start.1 = (f32[3,128,512]{2,1,0:T(8,128)S(1)}, f32[3,128,512]{2,1,0:T(8,128)}, u32[]{:S(2)}) copy-start(f32[3,128,512]{2,1,0:T(8,128)} %param.11) | copy-start | bytes 2359300
  14.7 5.2 %collective-permute-start.2 = (f32[8,128]{1,0:T(8,128)S(1)}, f32[8,128]{1,0:T(8,128)S(1)}, u32[]{:S(2)}, u32[]{:S(2)}) collective-permute-start(f32[8,128]{1,0:T(8,128)S(1)} %join.5.token.own), channel_id=1, source_target_pairs={{0,64},{1,65},{2,66},{3,67},{4,68},{5,69},{6,70},{7,71},{8,72},{9,... | collective-permute-start | bytes 12296 | tf_op jit(solution)/shard_map/ppermute | solution.py:449
  19.9 7.5 %collective-permute-start.3 = (f32[8,128]{1,0:T(8,128)S(1)}, f32[8,128]{1,0:T(8,128)S(1)}, u32[]{:S(2)}, u32[]{:S(2)}) collective-permute-start(f32[8,128]{1,0:T(8,128)S(1)} %join.6.token.own), channel_id=1, source_target_pairs={{0,192},{1,193},{2,194},{3,195},{4,196},{5,197},{6,198},{7,199},{8... | collective-permute-start | bytes 12296 | tf_op jit(solution)/shard_map/ppermute | solution.py:449
  27.4 3.7 %collective-permute-start.4 = (f32[8,128]{1,0:T(8,128)S(1)}, f32[8,128]{1,0:T(8,128)S(1)}, u32[]{:S(2)}, u32[]{:S(2)}) collective-permute-start(f32[8,128]{1,0:T(8,128)S(1)} %join.7.token.own), channel_id=1, source_target_pairs={{0,16},{1,17},{2,18},{3,19},{4,20},{5,21},{6,22},{7,23},{8,24},{9,... | collective-permute-start | bytes 12296 | tf_op jit(solution)/shard_map/ppermute | solution.py:449

commit v4 on v3

--- a/solution.py
+++ b/solution.py
@@ -126,7 +126,7 @@
 
 
 def shift_kernel(
-    size, row_shift, col_shift, spread, codes, wide, cleared, moved, payload, total, lines
+    size, row_shift, col_shift, spread, codes, wide, cleared, moved, payload, labels_only, total, lines
 ):
     frames, rows, cols, tiles, reach = size.frames, size.rows, size.cols, size.tiles, size.reach
     total[...] = jnp.zeros((rows, LANES), jnp.float32)
@@ -169,8 +169,9 @@
 
     lax.fori_loop(0, frames, shift_frame, 0, unroll=4)
     top, bottom = wide[0:reach, :], wide[rows - reach : rows, :]
-    labels = jnp.where(band % 2 == 1, bottom, top)
-    pack(size, payload, lines, labels, jnp.sum(total[...], axis=0, keepdims=True))
+    pack(size, labels_only, lines, jnp.where(band % 2 == 1, top, bottom), jnp.zeros((1, LANES)))
+    sums = jnp.sum(total[...], axis=0, keepdims=True)
+    pack(size, payload, lines, jnp.where(band % 2 == 1, bottom, top), sums)
 
 
 def shift_frames(size, row_shift, col_shift, spread, codes, wide, cleared):
@@ -179,9 +180,10 @@
         out_shape=[
             jax.ShapeDtypeStruct(cleared.shape, jnp.float32),
             jax.ShapeDtypeStruct((size.packed, size.width), jnp.bfloat16),
+            jax.ShapeDtypeStruct((size.packed, size.width), jnp.bfloat16),
         ],
         in_specs=[SMEM] * 2 + [VMEM] * 4,
-        out_specs=[VMEM] * 2,
+        out_specs=[VMEM] * 3,
         scratch_shapes=[
             pltpu.VMEM((size.rows, LANES), jnp.float32),
             pltpu.VMEM((size.packed, size.width), jnp.float32),
@@ -330,34 +332,27 @@
     )(moved, first_got, second_got, token, before, coeffs)
 
 
-def first_join_kernel(size, own, other, wide, token, out, lines):
-    top, bottom = wide[0 : size.reach, :], wide[size.rows - size.reach : size.rows, :]
-    labels = jnp.where(lax.axis_index("band") % 2 == 1, top, bottom)
-    pack(size, out, lines, labels, packed_sums(size, own) + packed_sums(size, other))
-
-
-def second_join_kernel(size, own, other, wide, token, out, lines):
+def first_join_kernel(size, own, other, token, out):
     out[...] = jnp.zeros(out.shape, jnp.float32)
     out[0:1, :] = packed_sums(size, own) + packed_sums(size, other)
 
 
-def join_kernel(size, own, other, wide, token, out, lines):
-    out[...] = own[...] + other[...]
-
-
-def join(size, kernel, own, other, wide, token):
-    out = jax.ShapeDtypeStruct((8, LANES), jnp.float32)
-    if kernel is first_join_kernel:
-        out = jax.ShapeDtypeStruct(own.shape, own.dtype)
+def join_kernel(size, *refs):
+    total = refs[0][...]
+    for part in refs[1:-2]:
+        total = total + part[...]
+    refs[-1][...] = total
+
+
+def join(size, kernel, parts, token):
     return pl.pallas_call(
         functools.partial(kernel, size),
-        out_shape=out,
-        in_specs=[VMEM, VMEM, VMEM, pl.BlockSpec(memory_space=pl.ANY)],
-        out_specs=VMEM,
-        scratch_shapes=[pltpu.VMEM((size.packed, size.width), jnp.float32)],
+        out_shape=jax.ShapeDtypeStruct((8, LANES), jnp.float32),
+        in_specs=[VMEM] * len(parts) + [pl.BlockSpec(memory_space=pl.ANY)],
+        out_specs=VMEM,
         compiler_params=pltpu.CompilerParams(vmem_limit_bytes=2 * MIB),
         name="join",
-    )(own, other, wide, token)
+    )(*parts, token)
 
 
 def put_kernel(send, own, other, out):
@@ -403,6 +398,14 @@
     )(blocks)
 
 
+def upper_pair(b):
+    return b ^ 1
+
+
+def lower_pair(b):
+    return b if b in (0, lax.axis_size("band") - 1) else ((b + 1) ^ 1) - 1
+
+
 def partner_steps():
     scans, bands = lax.axis_size("scan"), lax.axis_size("band")
     around = {0: 3, 1: 2, 2: 1, 3: 0}
@@ -416,22 +419,18 @@
     def same(b):
         return b
 
-    def upper_pair(b):
-        return b ^ 1
-
-    def lower_pair(b):
-        return b if b in (0, bands - 1) else ((b + 1) ^ 1) - 1
-
     moves = [
-        (lambda s: s ^ 1, lower_pair),
-        (x_around, upper_pair),
-        (lambda s: s ^ 8, same),
-        (z_around, same),
-        (lambda s: s ^ 2, same),
+        [(lambda s: s ^ 1, lower_pair)],
+        [(x_around, same), (lambda s: s ^ 2, same), (lambda s: s ^ 4, same)],
+        [(lambda s: s ^ 8, same)],
+        [(z_around, same)],
     ]
     return [
-        [(s * bands + b, move(s) * bands + turn(b)) for s in range(scans) for b in range(bands)]
-        for move, turn in moves
+        [
+            [(s * bands + b, move(s) * bands + turn(b)) for s in range(scans) for b in range(bands)]
+            for move, turn in step
+        ]
+        for step in moves
     ]
 
 
@@ -439,19 +438,23 @@
     frame_count, band_height, det_cols = frame_codes.shape
     size = Sizes(frame_count, band_height, det_cols)
     cleared, spread, wide = prepare(size, diagonals(size), row_scales, segment_labels)
-    moved, total = shift_frames(size, row_shift, col_shift, spread, frame_codes, wide, cleared)
+    moved, total, labels_only = shift_frames(
+        size, row_shift, col_shift, spread, frame_codes, wide, cleared
+    )
     coeffs = mask_coeffs.reshape(3 * SEGS, MASKS)
+    pairs = [(b, upper_pair(b)) for b in range(lax.axis_size("band"))]
+    second_got = lax.ppermute(labels_only, "band", pairs)
     steps = partner_steps()
-    cuts = [band_height * i // (len(steps) - 1) for i in range(len(steps))]
-    joins = [first_join_kernel, second_join_kernel, join_kernel, join_kernel]
+    cuts = [0, band_height // 4, band_height * 5 // 8, band_height]
     moments, got = None, []
-    for i, pairs in enumerate(steps):
-        got.append(lax.ppermute(total, ("scan", "band"), pairs))
+    for i, step in enumerate(steps):
+        got.append([lax.ppermute(total, ("scan", "band"), pairs) for pairs in step])
         if i < len(steps) - 1:
             moments = core_rows(size, moved, wide, total, moments, cuts[i], cuts[i + 1])
-            total = join(size, joins[i], total, got[i], wide, moments)
-    send = edge_rows(size, moved, got[0], got[1], total, moments, coeffs)
-    send = put_total(send, total, got[-1])
+            kernel = first_join_kernel if i == 0 else join_kernel
+            total = join(size, kernel, [total] + got[i], moments)
+    send = edge_rows(size, moved, got[0][0], second_got, total, moments, coeffs)
+    send = put_total(send, total, got[-1][0])
     blocks = lax.all_to_all(send, "band", 0, 0)
     return finish(blocks, frame_count)
 

time: 46.7 us -> 45.4 us (0.972)
  waiting for transfers between devices: 2.15 us -> 0.02 us
  starting transfers between devices: 12.2 us -> 13.9 us
  blocking collectives: 14.5 us -> 13.4 us
    ppermute x5 -> x7, waiting for transfers between devices: 2.15 us -> 0.02 us  [the longest x6 0.02 us: body(): got.append([lax.ppermute(total, ('scan', 'band'), pairs) for pairs in step])]
    ppermute x5 -> x7, starting transfers between devices: 12.2 us -> 13.9 us  [the longest x6 12.3 us: body(): got.append([lax.ppermute(total, ('scan', 'band'), pairs) for pairs in step])]
    all_to_all x1, blocking collectives: 14.5 us -> 13.4 us  [body(): blocks = lax.all_to_all(send, 'band', 0, 0)]
    pallas_call x4 -> x3, Pallas kernels: 7.45 us -> 7.45 us  [core_rows(): pl.pallas_call(functools.partial(core_kernel, size, first, last, before i...]
  transfers between devices with their start and end apart: 5 -> 7, of which waited for: 2 -> 0; matrix products, arithmetic and copies ran while one was open for 0% -> 0% of each run, Pallas kernels for 22% -> 22%
where the time goes in v4:
time: 45.4 us; the launch traced here: 45 us
  Pallas kernels  15.9 us (35%)
  starting transfers between devices  13.9 us (31%)
  blocking collectives  13.4 us (30%)
  local copies, waits for them, and re-layouts  1.52 us (3%)
    all_to_all x1, blocking collectives, body(): blocks = lax.all_to_all(send, 'band', 0, 0)  13.4 us
    ppermute x6, starting transfers between devices, body(): got.append([lax.ppermute(total, ('scan', 'band'), pairs) for pairs in step])  12.3 us
    pallas_call x3, Pallas kernels, core_rows(): pl.pallas_call(functools.partial(core_kernel, size, first, last, before i...  7.45 us
    pallas_call x1, Pallas kernels, shift_frames(): pl.pallas_call(functools.partial(shift_kernel, size), out_shape=[jax.Shap...  3.82 us
    pallas_call x1, Pallas kernels, edge_rows(): pl.pallas_call(functools.partial(edge_kernel, size), out_shape=jax.ShapeD...  2.56 us
    ppermute x1, starting transfers between devices, body(): second_got = lax.ppermute(labels_only, 'band', pairs)  1.66 us
    unnamed x12, local copies, waits for them, and re-layouts  1.52 us
    pallas_call x1, Pallas kernels, prepare(): pl.pallas_call(functools.partial(prepare_kernel, size), out_shape=[jax.Sh...  1.25 us
  transfers between devices with their start and end apart: 7, of which 0 were waited for; matrix products, arithmetic and copies ran while one was open for 0% of the time, Pallas kernels for 22%

profile of v4, /device:TPU:6, one launch (start us, length us, event | category | flops | bytes accessed | tf_op | source)
XLA Modules:
  0.0 45.0 jit_solution(12793344593896053595)
XLA Ops:
  0.0 0.0 copy-start.4
  0.0 0.0 copy-start.5
  0.0 0.0 copy-start.3
  0.0 0.0 copy-start.2
  0.0 0.0 copy-start
  0.1 0.9 %copy-done.4 = s32[72,576]{1,0:T(8,128)S(1)} copy-done((s32[72,576]{1,0:T(8,128)S(1)}, s32[72,576]{1,0:T(8,128)}, u32[]{:S(2)}) %copy-start.4) | copy-done | bytes 165912
  0.9 0.0 copy-done.5
  0.9 1.2 %prepare.1 = (f32[5,5850,128]{2,1,0:T(8,128)S(1)}, f32[5120,128]{1,0:T(8,128)S(1)}, f32[72,640]{1,0:T(8,128)S(1)}) custom-call(bf16[80,256]{1,0:T(8,128)(2,1)S(1)} %diagonals.1.diagonal, f32[64,72]{1,0:T(8,128)S(1)} %copy-done.5, s32[72,576]{1,0:T(8,128)S(1)} %copy-done.4), custom_call_target="tpu_custom_call" | custom-call | flops 500000000 | bytes 1000000 | tf_op jit(solution)/shard_map/prepare/pallas_call | solution.py:97
  2.2 0.0 copy-done.3
  2.2 0.0 copy-done.2
  2.2 0.6 %copy-done = bf16[64,72,576]{2,1,0:T(8,128)(2,1)S(1)} copy-done((bf16[64,72,576]{2,1,0:T(8,128)(2,1)S(1)}, bf16[64,72,576]{2,1,0:T(8,128)(2,1)}, u32[]{:S(2)}) %copy-start) | copy-done | bytes 5308440
  2.8 3.8 %shift.1 = (f32[5,5850,128]{2,1,0:T(8,128)S(1)}, bf16[16,640]{1,0:T(8,128)(2,1)S(1)}, bf16[16,640]{1,0:T(8,128)(2,1)S(1)}) custom-call(s32[64]{0:T(128)S(1)} %copy-done.2, s32[64]{0:T(128)S(1)} %copy-done.3, f32[5120,128]{1,0:T(8,128)S(1)} %get-tuple-element.11.spread, bf16[64,72,576]{2,1,0:T(8,128)(2,1)S(1)} %copy-done, ...), custom_call_target="tpu_custom_call", output_to_operand_aliasing={{0}: (5, {})} | custom-call | flops 6000000000 | bytes 1000000 | tf_op jit(solution)/shard_map/shift/pallas_call | solution.py:178
  6.7 1.7 %collective-permute-start.1 = (bf16[16,640]{1,0:T(8,128)(2,1)S(1)}, bf16[16,640]{1,0:T(8,128)(2,1)S(1)}, u32[]{:S(2)}, u32[]{:S(2)}) collective-permute-start(bf16[16,640]{1,0:T(8,128)(2,1)S(1)} %get-tuple-element.16), channel_id=1, source_target_pairs={{0,1},{1,0},{2,3},{3,2},{4,5},{5,4},{6,7},{7,6},{8,9},{9,8},{10,11... | collective-permute-start | bytes 61448 | tf_op jit(solution)/shard_map/ppermute | solution.py:446
  8.3 0.0 collective-permute-start
  8.3 1.9 %core.3.token.refs_0_ = f32[384,64]{1,0:T(8,128)S(1)} custom-call(f32[5,5850,128]{2,1,0:T(8,128)S(1)} %get-tuple-element.14.moved, f32[72,640]{1,0:T(8,128)S(1)} %get-tuple-element.12.wide, bf16[16,640]{1,0:T(8,128)(2,1)S(1)} %get-tuple-element.15.token.own), custom_call_target="tpu_custom_call" | custom-call | flops 4000000000 | bytes 1000000 | tf_op jit(solution)/shard_map/core/pallas_call | solution.py:258
  10.2 0.0 collective-permute-done.other.first_got
  10.2 0.0 copy-start.1
  10.2 1.5 %collective-permute-start.4 = (f32[8,128]{1,0:T(8,128)S(1)}, f32[8,128]{1,0:T(8,128)S(1)}, u32[]{:S(2)}, u32[]{:S(2)}) collective-permute-start(f32[8,128]{1,0:T(8,128)S(1)} %join.3.token.refs_0_), channel_id=1, source_target_pairs={{0,32},{1,33},{2,34},{3,35},{4,36},{5,37},{6,38},{7,39},{8,40},{9,... | collective-permute-start | bytes 12296 | tf_op jit(solution)/shard_map/ppermute | solution.py:451
  11.7 0.2 collective-permute-start.3
  11.9 2.5 %collective-permute-start.2 = (f32[8,128]{1,0:T(8,128)S(1)}, f32[8,128]{1,0:T(8,128)S(1)}, u32[]{:S(2)}, u32[]{:S(2)}) collective-permute-start(f32[8,128]{1,0:T(8,128)S(1)} %join.3.token.refs_0_), channel_id=1, source_target_pairs={{0,48},{1,49},{2,50},{3,51},{4,52},{5,53},{6,54},{7,55},{8,56},{9,... | collective-permute-start | bytes 12296 | tf_op jit(solution)/shard_map/ppermute | solution.py:451
  14.4 2.8 %core.4.refs_4_.refs_0_ = f32[384,64]{1,0:T(8,128)S(1)} custom-call(f32[5,5850,128]{2,1,0:T(8,128)S(1)} %get-tuple-element.14.moved, f32[72,640]{1,0:T(8,128)S(1)} %get-tuple-element.12.wide, f32[8,128]{1,0:T(8,128)S(1)} %join.3.token.refs_0_, f32[384,64]{1,0:T(8,128)S(1)} %core.3.token.refs_0_), custom_call_target="tpu_custom_call" | custom-call | flops 4000000000 | bytes 1000000 | tf_op jit(solution)/shard_map/core/pallas_call | solution.py:258
  17.2 0.0 collective-permute-done.4.refs_3_
  17.2 0.0 collective-permute-done.3.refs_2_
  17.2 0.0 collective-permute-done.2.refs_1_
  17.3 3.4 %collective-permute-start.5 = (f32[8,128]{1,0:T(8,128)S(1)}, f32[8,128]{1,0:T(8,128)S(1)}, u32[]{:S(2)}, u32[]{:S(2)}) collective-permute-start(f32[8,128]{1,0:T(8,128)S(1)} %join.4.token.refs_0_), channel_id=1, source_target_pairs={{0,64},{1,65},{2,66},{3,67},{4,68},{5,69},{6,70},{7,71},{8,72},{9,... | collective-permute-start | bytes 12296 | tf_op jit(solution)/shard_map/ppermute | solution.py:451
  20.6 2.8 %core.5.refs_2_.before = f32[384,64]{1,0:T(8,128)S(1)} custom-call(f32[5,5850,128]{2,1,0:T(8,128)S(1)} %get-tuple-element.14.moved, f32[72,640]{1,0:T(8,128)S(1)} %get-tuple-element.12.wide, f32[8,128]{1,0:T(8,128)S(1)} %join.4.token.refs_0_, f32[384,64]{1,0:T(8,128)S(1)} %core.4.refs_4_.refs_0_), custom_call_target="tpu_custom_call" | custom-call | flops 4000000000 | bytes 1000000 | tf_op jit(solution)/shard_map/core/pallas_call | solution.py:258
  23.4 0.0 collective-permute-done.5.refs_1_
  23.5 4.7 %collective-permute-start.6 = (f32[8,128]{1,0:T(8,128)S(1)}, f32[8,128]{1,0:T(8,128)S(1)}, u32[]{:S(2)}, u32[]{:S(2)}) collective-permute-start(f32[8,128]{1,0:T(8,128)S(1)} %join.5.token.own), channel_id=1, source_target_pairs={{0,192},{1,193},{2,194},{3,195},{4,196},{5,197},{6,198},{7,199},{8... | collective-permute-start | bytes 12296 | tf_op jit(solution)/shard_map/ppermute | solution.py:451
  28.2 0.0 collective-permute-done.1.second_got
  28.2 0.0 copy-done.1
  28.2 2.6 %edge.1.send = f32[8,40,128]{2,1,0:T(8,128)S(1)} custom-call(f32[5,5850,128]{2,1,0:T(8,128)S(1)} %get-tuple-element.14.moved, bf16[16,640]{1,0:T(8,128)(2,1)S(1)} %collective-permute-done.other.first_got, bf16[16,640]{1,0:T(8,128)(2,1)S(1)} %collective-permute-done.1.second_got, f32[8,128]{1,0:T(8,128)S(1)} %join.5.token.own, ...), custom_call_target="tpu_custom_call" | custom-call | flops 4000000000 | bytes 1000000 | tf_op jit(solution)/shard_map/edge/pallas_call | solution.py:318
  30.7 0.0 collective-permute-done.6.other
  30.8 13.4 %all_to_all.5.blocks = f32[8,40,128]{2,1,0:T(8,128)S(1)} all-to-all(f32[8,40,128]{2,1,0:T(8,128)S(1)} %put.1), channel_id=1, replica_groups=mesh['scan'=32,'band'=8] {'band'}, dimensions={0} | all-to-all | bytes 327680 | tf_op jit(solution)/shard_map/all_to_all | solution.py:458
  44.2 0.8 %finish.1 = f32[64,64]{1,0:T(8,128)} custom-call(f32[8,40,128]{2,1,0:T(8,128)S(1)} %all_to_all.5.blocks), custom_call_target="tpu_custom_call" | custom-call | tf_op jit(solution)/shard_map/finish/pallas_call | solution.py:391
  (5 shorter events, 0.0 us)
Async XLA Ops:
  0.0 0.9 %copy-start.4 = (s32[72,576]{1,0:T(8,128)S(1)}, s32[72,576]{1,0:T(8,128)}, u32[]{:S(2)}) copy-start(s32[72,576]{1,0:T(8,128)} %labels.1) | copy-start | bytes 497668
  0.0 0.9 %copy-start.5 = (f32[64,72]{1,0:T(8,128)S(1)}, f32[64,72]{1,0:T(8,128)}, u32[]{:S(2)}) copy-start(f32[64,72]{1,0:T(8,128)} %scales.1) | copy-start | bytes 55300
  0.0 2.2 %copy-start.3 = (s32[64]{0:T(128)S(1)}, s32[64]{0:T(128)}, u32[]{:S(2)}) copy-start(s32[64]{0:T(128)} %col_shift.1) | copy-start | bytes 772
  0.0 2.2 %copy-start.2 = (s32[64]{0:T(128)S(1)}, s32[64]{0:T(128)}, u32[]{:S(2)}) copy-start(s32[64]{0:T(128)} %row_shift.1) | copy-start | bytes 772
  0.0 2.8 %copy-start = (bf16[64,72,576]{2,1,0:T(8,128)(2,1)S(1)}, bf16[64,72,576]{2,1,0:T(8,128)(2,1)}, u32[]{:S(2)}) copy-start(bf16[64,72,576]{2,1,0:T(8,128)(2,1)} %codes.1) | copy-start | bytes 15925252
  6.7 21.5 %collective-permute-start.1 = (bf16[16,640]{1,0:T(8,128)(2,1)S(1)}, bf16[16,640]{1,0:T(8,128)(2,1)S(1)}, u32[]{:S(2)}, u32[]{:S(2)}) collective-permute-start(bf16[16,640]{1,0:T(8,128)(2,1)S(1)} %get-tuple-element.16), channel_id=1, source_target_pairs={{0,1},{1,0},{2,3},{3,2},{4,5},{5,4},{6,7},{7,6},{8,9},{9,8},{10,11... | collective-permute-start | bytes 61448 | tf_op jit(solution)/shard_map/ppermute | solution.py:446
  8.3 1.9 %collective-permute-start = (bf16[16,640]{1,0:T(8,128)(2,1)S(1)}, bf16[16,640]{1,0:T(8,128)(2,1)S(1)}, u32[]{:S(2)}, u32[]{:S(2)}) collective-permute-start(bf16[16,640]{1,0:T(8,128)(2,1)S(1)} %get-tuple-element.15.token.own), channel_id=1, source_target_pairs={{0,8},{1,10},{2,9},{3,12},{4,11},{5,14},{6,13},{7,15},{8,0},{9,2},... | collective-permute-start | bytes 61448 | tf_op jit(solution)/shard_map/ppermute | solution.py:451
  10.2 17.9 %copy-start.1 = (f32[3,128,512]{2,1,0:T(8,128)S(1)}, f32[3,128,512]{2,1,0:T(8,128)}, u32[]{:S(2)}) copy-start(f32[3,128,512]{2,1,0:T(8,128)} %param.11) | copy-start | bytes 2359300
  10.2 7.0 %collective-permute-start.4 = (f32[8,128]{1,0:T(8,128)S(1)}, f32[8,128]{1,0:T(8,128)S(1)}, u32[]{:S(2)}, u32[]{:S(2)}) collective-permute-start(f32[8,128]{1,0:T(8,128)S(1)} %join.3.token.refs_0_), channel_id=1, source_target_pairs={{0,32},{1,33},{2,34},{3,35},{4,36},{5,37},{6,38},{7,39},{8,40},{9,... | collective-permute-start | bytes 12296 | tf_op jit(solution)/shard_map/ppermute | solution.py:451
  11.7 5.5 %collective-permute-start.3 = (f32[8,128]{1,0:T(8,128)S(1)}, f32[8,128]{1,0:T(8,128)S(1)}, u32[]{:S(2)}, u32[]{:S(2)}) collective-permute-start(f32[8,128]{1,0:T(8,128)S(1)} %join.3.token.refs_0_), channel_id=1, source_target_pairs={{0,16},{1,17},{2,18},{3,19},{4,20},{5,21},{6,22},{7,23},{8,24},{9,... | collective-permute-start | bytes 12296 | tf_op jit(solution)/shard_map/ppermute | solution.py:451
  11.9 5.3 %collective-permute-start.2 = (f32[8,128]{1,0:T(8,128)S(1)}, f32[8,128]{1,0:T(8,128)S(1)}, u32[]{:S(2)}, u32[]{:S(2)}) collective-permute-start(f32[8,128]{1,0:T(8,128)S(1)} %join.3.token.refs_0_), channel_id=1, source_target_pairs={{0,48},{1,49},{2,50},{3,51},{4,52},{5,53},{6,54},{7,55},{8,56},{9,... | collective-permute-start | bytes 12296 | tf_op jit(solution)/shard_map/ppermute | solution.py:451
  17.3 6.2 %collective-permute-start.5 = (f32[8,128]{1,0:T(8,128)S(1)}, f32[8,128]{1,0:T(8,128)S(1)}, u32[]{:S(2)}, u32[]{:S(2)}) collective-permute-start(f32[8,128]{1,0:T(8,128)S(1)} %join.4.token.refs_0_), channel_id=1, source_target_pairs={{0,64},{1,65},{2,66},{3,67},{4,68},{5,69},{6,70},{7,71},{8,72},{9,... | collective-permute-start | bytes 12296 | tf_op jit(solution)/shard_map/ppermute | solution.py:451
  23.5 7.3 %collective-permute-start.6 = (f32[8,128]{1,0:T(8,128)S(1)}, f32[8,128]{1,0:T(8,128)S(1)}, u32[]{:S(2)}, u32[]{:S(2)}) collective-permute-start(f32[8,128]{1,0:T(8,128)S(1)} %join.5.token.own), channel_id=1, source_target_pairs={{0,192},{1,193},{2,194},{3,195},{4,196},{5,197},{6,198},{7,199},{8... | collective-permute-start | bytes 12296 | tf_op jit(solution)/shard_map/ppermute | solution.py:451

commit v5 on v4

--- a/solution.py
+++ b/solution.py
@@ -34,6 +34,21 @@
     return jnp.concatenate([labels.astype(jnp.float32), fill], axis=1)
 
 
+def pack(size, out, lines, labels, sums):
+    high = sums.astype(jnp.bfloat16).astype(jnp.float32)
+    middle = (sums - high).astype(jnp.bfloat16).astype(jnp.float32)
+    lines[...] = jnp.zeros(lines.shape, jnp.float32)
+    lines[0 : size.reach, :] = labels
+    for k, part in enumerate([high, middle, sums - high - middle]):
+        lines[size.reach + k : size.reach + k + 1, 0:LANES] = part
+    out[...] = lines[...].astype(jnp.bfloat16)
+
+
+def packed_sums(size, message):
+    parts = message[...].astype(jnp.float32)[size.reach : size.reach + 3, 0:LANES]
+    return parts[0:1] + parts[1:2] + parts[2:3]
+
+
 def diagonal_kernel(size, out):
     place = lax.broadcasted_iota(jnp.int32, out.shape, 1)
     row = lax.broadcasted_iota(jnp.int32, out.shape, 0)
@@ -52,7 +67,9 @@
     )()
 
 
-def prepare_kernel(size, diagonal, scales, labels, moved, spread, wide, split):
+def prepare_kernel(
+    size, diagonal, scales, labels, moved, spread, wide, labels_only, split, lines
+):
     frames, rows = size.frames, size.rows
     empty = jnp.zeros((frames, LANES), jnp.float32)
 
@@ -91,6 +108,9 @@
 
     lax.fori_loop(0, frames // group, spread_group, 0, unroll=8)
     wide[...] = widened(size, labels[...])
+    top, bottom = wide[0 : size.reach, :], wide[rows - size.reach : rows, :]
+    wanted = jnp.where(lax.axis_index("band") % 2 == 1, top, bottom)
+    pack(size, labels_only, lines, wanted, jnp.zeros((1, LANES), jnp.float32))
 
 
 def prepare(size, diagonal, scales, labels):
@@ -100,33 +120,22 @@
             jax.ShapeDtypeStruct((size.tiles, size.ext * size.pitch, LANES), jnp.float32),
             jax.ShapeDtypeStruct((size.frames * size.tall, LANES), jnp.float32),
             jax.ShapeDtypeStruct((size.rows, size.width), jnp.float32),
+            jax.ShapeDtypeStruct((size.packed, size.width), jnp.bfloat16),
         ],
         in_specs=[VMEM] * 3,
-        out_specs=[VMEM] * 3,
-        scratch_shapes=[pltpu.VMEM((size.frames, 2 * LANES), jnp.float32)],
+        out_specs=[VMEM] * 4,
+        scratch_shapes=[
+            pltpu.VMEM((size.frames, 2 * LANES), jnp.float32),
+            pltpu.VMEM((size.packed, size.width), jnp.float32),
+        ],
         compiler_params=pltpu.CompilerParams(vmem_limit_bytes=8 * MIB),
         cost_estimate=pl.CostEstimate(flops=5 * 10**8, bytes_accessed=10**6, transcendentals=0),
         name="prepare",
     )(diagonal, scales, labels)
 
 
-def pack(size, out, lines, labels, sums):
-    high = sums.astype(jnp.bfloat16).astype(jnp.float32)
-    middle = (sums - high).astype(jnp.bfloat16).astype(jnp.float32)
-    lines[...] = jnp.zeros(lines.shape, jnp.float32)
-    lines[0 : size.reach, :] = labels
-    for k, part in enumerate([high, middle, sums - high - middle]):
-        lines[size.reach + k : size.reach + k + 1, 0:LANES] = part
-    out[...] = lines[...].astype(jnp.bfloat16)
-
-
-def packed_sums(size, message):
-    parts = message[...].astype(jnp.float32)[size.reach : size.reach + 3, 0:LANES]
-    return parts[0:1] + parts[1:2] + parts[2:3]
-
-
 def shift_kernel(
-    size, row_shift, col_shift, spread, codes, wide, cleared, moved, payload, labels_only, total, lines
+    size, row_shift, col_shift, spread, codes, wide, cleared, moved, payload, total, lines
 ):
     frames, rows, cols, tiles, reach = size.frames, size.rows, size.cols, size.tiles, size.reach
     total[...] = jnp.zeros((rows, LANES), jnp.float32)
@@ -167,9 +176,8 @@
         total[...] += jnp.where((target >= 0) & (target < cols), row_sum, 0.0)
         return carry
 
-    lax.fori_loop(0, frames, shift_frame, 0, unroll=4)
+    lax.fori_loop(0, frames, shift_frame, 0, unroll=8)
     top, bottom = wide[0:reach, :], wide[rows - reach : rows, :]
-    pack(size, labels_only, lines, jnp.where(band % 2 == 1, top, bottom), jnp.zeros((1, LANES)))
     sums = jnp.sum(total[...], axis=0, keepdims=True)
     pack(size, payload, lines, jnp.where(band % 2 == 1, bottom, top), sums)
 
@@ -180,10 +188,9 @@
         out_shape=[
             jax.ShapeDtypeStruct(cleared.shape, jnp.float32),
             jax.ShapeDtypeStruct((size.packed, size.width), jnp.bfloat16),
-            jax.ShapeDtypeStruct((size.packed, size.width), jnp.bfloat16),
         ],
         in_specs=[SMEM] * 2 + [VMEM] * 4,
-        out_specs=[VMEM] * 3,
+        out_specs=[VMEM] * 2,
         scratch_shapes=[
             pltpu.VMEM((size.rows, LANES), jnp.float32),
             pltpu.VMEM((size.packed, size.width), jnp.float32),
@@ -437,10 +444,10 @@
 def body(frame_codes, row_scales, row_shift, col_shift, segment_labels, mask_coeffs):
     frame_count, band_height, det_cols = frame_codes.shape
     size = Sizes(frame_count, band_height, det_cols)
-    cleared, spread, wide = prepare(size, diagonals(size), row_scales, segment_labels)
-    moved, total, labels_only = shift_frames(
-        size, row_shift, col_shift, spread, frame_codes, wide, cleared
+    cleared, spread, wide, labels_only = prepare(
+        size, diagonals(size), row_scales, segment_labels
     )
+    moved, total = shift_frames(size, row_shift, col_shift, spread, frame_codes, wide, cleared)
     coeffs = mask_coeffs.reshape(3 * SEGS, MASKS)
     pairs = [(b, upper_pair(b)) for b in range(lax.axis_size("band"))]
     second_got = lax.ppermute(labels_only, "band", pairs)

time: 45.4 us -> 44.7 us (0.985)
  blocking collectives: 13.4 us -> 11.8 us
  starting transfers between devices: 13.9 us -> 15 us
    all_to_all x1, blocking collectives: 13.4 us -> 11.8 us  [body(): blocks = lax.all_to_all(send, 'band', 0, 0)]
    ppermute x1, starting transfers between devices: 1.66 us -> 2.58 us  [body(): second_got = lax.ppermute(labels_only, 'band', pairs)]
  transfers between devices with their start and end apart: 7 -> 7, of which waited for: 0 -> 0; matrix products, arithmetic and copies ran while one was open for 0% -> 0% of each run, Pallas kernels for 22% -> 23%
where the time goes in v5:
time: 44.7 us; the launch traced here: 44.3 us
  Pallas kernels  15.8 us (35%)
  starting transfers between devices  15 us (34%)
  blocking collectives  11.8 us (26%)
  local copies, waits for them, and re-layouts  1.49 us (3%)
    ppermute x6, starting transfers between devices, body(): got.append([lax.ppermute(total, ('scan', 'band'), pairs) for pairs in step])  12.4 us
    all_to_all x1, blocking collectives, body(): blocks = lax.all_to_all(send, 'band', 0, 0)  11.8 us
    pallas_call x3, Pallas kernels, core_rows(): pl.pallas_call(functools.partial(core_kernel, size, first, last, before i...  7.44 us
    pallas_call x1, Pallas kernels, shift_frames(): pl.pallas_call(functools.partial(shift_kernel, size), out_shape=[jax.Shap...  3.66 us
    ppermute x1, starting transfers between devices, body(): second_got = lax.ppermute(labels_only, 'band', pairs)  2.58 us
    pallas_call x1, Pallas kernels, edge_rows(): pl.pallas_call(functools.partial(edge_kernel, size), out_shape=jax.ShapeD...  2.55 us
    unnamed x12, local copies, waits for them, and re-layouts  1.49 us
    pallas_call x1, Pallas kernels, prepare(): pl.pallas_call(functools.partial(prepare_kernel, size), out_shape=[jax.Sh...  1.29 us
  transfers between devices with their start and end apart: 7, of which 0 were waited for; matrix products, arithmetic and copies ran while one was open for 0% of the time, Pallas kernels for 23%

profile of v5, /device:TPU:6, one launch (start us, length us, event | category | flops | bytes accessed | tf_op | source)
XLA Modules:
  0.0 44.3 jit_solution(8602524047824100530)
XLA Ops:
  0.0 0.0 copy-start.4
  0.0 0.0 copy-start.5
  0.0 0.0 copy-start.3
  0.0 0.0 copy-start.2
  0.0 0.0 copy-start
  0.1 0.9 %copy-done.4 = s32[72,576]{1,0:T(8,128)S(1)} copy-done((s32[72,576]{1,0:T(8,128)S(1)}, s32[72,576]{1,0:T(8,128)}, u32[]{:S(2)}) %copy-start.4) | copy-done | bytes 165912
  0.9 0.0 copy-done.5
  0.9 1.3 %prepare.1 = (f32[5,5850,128]{2,1,0:T(8,128)S(1)}, f32[5120,128]{1,0:T(8,128)S(1)}, f32[72,640]{1,0:T(8,128)S(1)}, bf16[16,640]{1,0:T(8,128)(2,1)S(1)}) custom-call(bf16[80,256]{1,0:T(8,128)(2,1)S(1)} %diagonals.1.diagonal, f32[64,72]{1,0:T(8,128)S(1)} %copy-done.5, s32[72,576]{1,0:T(8,128)S(1)} %copy-done.4), custom_call_target="tpu_custom_call" | custom-call | flops 500000000 | bytes 1000000 | tf_op jit(solution)/shard_map/prepare/pallas_call | solution.py:117
  2.2 0.0 copy-done.3
  2.2 0.0 copy-done.2
  2.2 0.6 %copy-done = bf16[64,72,576]{2,1,0:T(8,128)(2,1)S(1)} copy-done((bf16[64,72,576]{2,1,0:T(8,128)(2,1)S(1)}, bf16[64,72,576]{2,1,0:T(8,128)(2,1)}, u32[]{:S(2)}) %copy-start) | copy-done | bytes 5308440
  2.8 3.7 %shift.1 = (f32[5,5850,128]{2,1,0:T(8,128)S(1)}, bf16[16,640]{1,0:T(8,128)(2,1)S(1)}) custom-call(s32[64]{0:T(128)S(1)} %copy-done.2, s32[64]{0:T(128)S(1)} %copy-done.3, f32[5120,128]{1,0:T(8,128)S(1)} %get-tuple-element.11.spread, bf16[64,72,576]{2,1,0:T(8,128)(2,1)S(1)} %copy-done, ...), custom_call_target="tpu_custom_call", output_to_operand_aliasing={{0}: (5, {})} | custom-call | flops 6000000000 | bytes 1000000 | tf_op jit(solution)/shard_map/shift/pallas_call | solution.py:186
  6.5 0.1 collective-permute-start
  6.6 2.6 %collective-permute-start.1 = (bf16[16,640]{1,0:T(8,128)(2,1)S(1)}, bf16[16,640]{1,0:T(8,128)(2,1)S(1)}, u32[]{:S(2)}, u32[]{:S(2)}) collective-permute-start(bf16[16,640]{1,0:T(8,128)(2,1)S(1)} %get-tuple-element.16), channel_id=1, source_target_pairs={{0,1},{1,0},{2,3},{3,2},{4,5},{5,4},{6,7},{7,6},{8,9},{9,8},{10,11... | collective-permute-start | bytes 61448 | tf_op jit(solution)/shard_map/ppermute | solution.py:453
  9.2 1.9 %core.3.token.refs_0_ = f32[384,64]{1,0:T(8,128)S(1)} custom-call(f32[5,5850,128]{2,1,0:T(8,128)S(1)} %get-tuple-element.14.moved, f32[72,640]{1,0:T(8,128)S(1)} %get-tuple-element.12.wide, bf16[16,640]{1,0:T(8,128)(2,1)S(1)} %get-tuple-element.15.token.own), custom_call_target="tpu_custom_call" | custom-call | flops 4000000000 | bytes 1000000 | tf_op jit(solution)/shard_map/core/pallas_call | solution.py:265
  11.0 0.0 collective-permute-done.other.first_got
  11.1 0.0 copy-start.1
  11.1 1.5 %collective-permute-start.4 = (f32[8,128]{1,0:T(8,128)S(1)}, f32[8,128]{1,0:T(8,128)S(1)}, u32[]{:S(2)}, u32[]{:S(2)}) collective-permute-start(f32[8,128]{1,0:T(8,128)S(1)} %join.3.token.refs_0_), channel_id=1, source_target_pairs={{0,32},{1,33},{2,34},{3,35},{4,36},{5,37},{6,38},{7,39},{8,40},{9,... | collective-permute-start | bytes 12296 | tf_op jit(solution)/shard_map/ppermute | solution.py:458
  12.6 0.0 collective-permute-start.3
  12.6 2.7 %collective-permute-start.2 = (f32[8,128]{1,0:T(8,128)S(1)}, f32[8,128]{1,0:T(8,128)S(1)}, u32[]{:S(2)}, u32[]{:S(2)}) collective-permute-start(f32[8,128]{1,0:T(8,128)S(1)} %join.3.token.refs_0_), channel_id=1, source_target_pairs={{0,48},{1,49},{2,50},{3,51},{4,52},{5,53},{6,54},{7,55},{8,56},{9,... | collective-permute-start | bytes 12296 | tf_op jit(solution)/shard_map/ppermute | solution.py:458
  15.3 2.8 %core.4.refs_4_.refs_0_ = f32[384,64]{1,0:T(8,128)S(1)} custom-call(f32[5,5850,128]{2,1,0:T(8,128)S(1)} %get-tuple-element.14.moved, f32[72,640]{1,0:T(8,128)S(1)} %get-tuple-element.12.wide, f32[8,128]{1,0:T(8,128)S(1)} %join.3.token.refs_0_, f32[384,64]{1,0:T(8,128)S(1)} %core.3.token.refs_0_), custom_call_target="tpu_custom_call" | custom-call | flops 4000000000 | bytes 1000000 | tf_op jit(solution)/shard_map/core/pallas_call | solution.py:265
  18.1 0.0 collective-permute-done.4.refs_3_
  18.1 0.0 collective-permute-done.3.refs_2_
  18.1 0.0 collective-permute-done.2.refs_1_
  18.1 3.4 %collective-permute-start.5 = (f32[8,128]{1,0:T(8,128)S(1)}, f32[8,128]{1,0:T(8,128)S(1)}, u32[]{:S(2)}, u32[]{:S(2)}) collective-permute-start(f32[8,128]{1,0:T(8,128)S(1)} %join.4.token.refs_0_), channel_id=1, source_target_pairs={{0,64},{1,65},{2,66},{3,67},{4,68},{5,69},{6,70},{7,71},{8,72},{9,... | collective-permute-start | bytes 12296 | tf_op jit(solution)/shard_map/ppermute | solution.py:458
  21.5 2.8 %core.5.refs_2_.before = f32[384,64]{1,0:T(8,128)S(1)} custom-call(f32[5,5850,128]{2,1,0:T(8,128)S(1)} %get-tuple-element.14.moved, f32[72,640]{1,0:T(8,128)S(1)} %get-tuple-element.12.wide, f32[8,128]{1,0:T(8,128)S(1)} %join.4.token.refs_0_, f32[384,64]{1,0:T(8,128)S(1)} %core.4.refs_4_.refs_0_), custom_call_target="tpu_custom_call" | custom-call | flops 4000000000 | bytes 1000000 | tf_op jit(solution)/shard_map/core/pallas_call | solution.py:265
  24.3 0.0 collective-permute-done.5.refs_1_
  24.3 4.7 %collective-permute-start.6 = (f32[8,128]{1,0:T(8,128)S(1)}, f32[8,128]{1,0:T(8,128)S(1)}, u32[]{:S(2)}, u32[]{:S(2)}) collective-permute-start(f32[8,128]{1,0:T(8,128)S(1)} %join.5.token.own), channel_id=1, source_target_pairs={{0,192},{1,193},{2,194},{3,195},{4,196},{5,197},{6,198},{7,199},{8... | collective-permute-start | bytes 12296 | tf_op jit(solution)/shard_map/ppermute | solution.py:458
  29.0 0.0 collective-permute-done.1.second_got
  29.0 0.0 copy-done.1
  29.0 2.6 %edge.1.send = f32[8,40,128]{2,1,0:T(8,128)S(1)} custom-call(f32[5,5850,128]{2,1,0:T(8,128)S(1)} %get-tuple-element.14.moved, bf16[16,640]{1,0:T(8,128)(2,1)S(1)} %collective-permute-done.other.first_got, bf16[16,640]{1,0:T(8,128)(2,1)S(1)} %collective-permute-done.1.second_got, f32[8,128]{1,0:T(8,128)S(1)} %join.5.token.own, ...), custom_call_target="tpu_custom_call" | custom-call | flops 4000000000 | bytes 1000000 | tf_op jit(solution)/shard_map/edge/pallas_call | solution.py:325
  31.6 0.0 collective-permute-done.6.other
  31.6 11.8 %all_to_all.5.blocks = f32[8,40,128]{2,1,0:T(8,128)S(1)} all-to-all(f32[8,40,128]{2,1,0:T(8,128)S(1)} %put.1), channel_id=1, replica_groups=mesh['scan'=32,'band'=8] {'band'}, dimensions={0} | all-to-all | bytes 327680 | tf_op jit(solution)/shard_map/all_to_all | solution.py:465
  43.5 0.8 %finish.1 = f32[64,64]{1,0:T(8,128)} custom-call(f32[8,40,128]{2,1,0:T(8,128)S(1)} %all_to_all.5.blocks), custom_call_target="tpu_custom_call" | custom-call | tf_op jit(solution)/shard_map/finish/pallas_call | solution.py:398
  (5 shorter events, 0.0 us)
Async XLA Ops:
  0.0 0.9 %copy-start.4 = (s32[72,576]{1,0:T(8,128)S(1)}, s32[72,576]{1,0:T(8,128)}, u32[]{:S(2)}) copy-start(s32[72,576]{1,0:T(8,128)} %labels.1) | copy-start | bytes 497668
  0.0 0.9 %copy-start.5 = (f32[64,72]{1,0:T(8,128)S(1)}, f32[64,72]{1,0:T(8,128)}, u32[]{:S(2)}) copy-start(f32[64,72]{1,0:T(8,128)} %scales.1) | copy-start | bytes 55300
  0.0 2.2 %copy-start.3 = (s32[64]{0:T(128)S(1)}, s32[64]{0:T(128)}, u32[]{:S(2)}) copy-start(s32[64]{0:T(128)} %col_shift.1) | copy-start | bytes 772
  0.0 2.2 %copy-start.2 = (s32[64]{0:T(128)S(1)}, s32[64]{0:T(128)}, u32[]{:S(2)}) copy-start(s32[64]{0:T(128)} %row_shift.1) | copy-start | bytes 772
  0.0 2.8 %copy-start = (bf16[64,72,576]{2,1,0:T(8,128)(2,1)S(1)}, bf16[64,72,576]{2,1,0:T(8,128)(2,1)}, u32[]{:S(2)}) copy-start(bf16[64,72,576]{2,1,0:T(8,128)(2,1)} %codes.1) | copy-start | bytes 15925252
  6.5 4.6 %collective-permute-start = (bf16[16,640]{1,0:T(8,128)(2,1)S(1)}, bf16[16,640]{1,0:T(8,128)(2,1)S(1)}, u32[]{:S(2)}, u32[]{:S(2)}) collective-permute-start(bf16[16,640]{1,0:T(8,128)(2,1)S(1)} %get-tuple-element.15.token.own), channel_id=1, source_target_pairs={{0,8},{1,10},{2,9},{3,12},{4,11},{5,14},{6,13},{7,15},{8,0},{9,2},... | collective-permute-start | bytes 61448 | tf_op jit(solution)/shard_map/ppermute | solution.py:458
  6.6 22.5 %collective-permute-start.1 = (bf16[16,640]{1,0:T(8,128)(2,1)S(1)}, bf16[16,640]{1,0:T(8,128)(2,1)S(1)}, u32[]{:S(2)}, u32[]{:S(2)}) collective-permute-start(bf16[16,640]{1,0:T(8,128)(2,1)S(1)} %get-tuple-element.16), channel_id=1, source_target_pairs={{0,1},{1,0},{2,3},{3,2},{4,5},{5,4},{6,7},{7,6},{8,9},{9,8},{10,11... | collective-permute-start | bytes 61448 | tf_op jit(solution)/shard_map/ppermute | solution.py:453
  11.1 18.0 %copy-start.1 = (f32[3,128,512]{2,1,0:T(8,128)S(1)}, f32[3,128,512]{2,1,0:T(8,128)}, u32[]{:S(2)}) copy-start(f32[3,128,512]{2,1,0:T(8,128)} %param.11) | copy-start | bytes 2359300
  11.1 7.0 %collective-permute-start.4 = (f32[8,128]{1,0:T(8,128)S(1)}, f32[8,128]{1,0:T(8,128)S(1)}, u32[]{:S(2)}, u32[]{:S(2)}) collective-permute-start(f32[8,128]{1,0:T(8,128)S(1)} %join.3.token.refs_0_), channel_id=1, source_target_pairs={{0,32},{1,33},{2,34},{3,35},{4,36},{5,37},{6,38},{7,39},{8,40},{9,... | collective-permute-start | bytes 12296 | tf_op jit(solution)/shard_map/ppermute | solution.py:458
  12.6 5.5 %collective-permute-start.3 = (f32[8,128]{1,0:T(8,128)S(1)}, f32[8,128]{1,0:T(8,128)S(1)}, u32[]{:S(2)}, u32[]{:S(2)}) collective-permute-start(f32[8,128]{1,0:T(8,128)S(1)} %join.3.token.refs_0_), channel_id=1, source_target_pairs={{0,16},{1,17},{2,18},{3,19},{4,20},{5,21},{6,22},{7,23},{8,24},{9,... | collective-permute-start | bytes 12296 | tf_op jit(solution)/shard_map/ppermute | solution.py:458
  12.6 5.5 %collective-permute-start.2 = (f32[8,128]{1,0:T(8,128)S(1)}, f32[8,128]{1,0:T(8,128)S(1)}, u32[]{:S(2)}, u32[]{:S(2)}) collective-permute-start(f32[8,128]{1,0:T(8,128)S(1)} %join.3.token.refs_0_), channel_id=1, source_target_pairs={{0,48},{1,49},{2,50},{3,51},{4,52},{5,53},{6,54},{7,55},{8,56},{9,... | collective-permute-start | bytes 12296 | tf_op jit(solution)/shard_map/ppermute | solution.py:458
  18.1 6.2 %collective-permute-start.5 = (f32[8,128]{1,0:T(8,128)S(1)}, f32[8,128]{1,0:T(8,128)S(1)}, u32[]{:S(2)}, u32[]{:S(2)}) collective-permute-start(f32[8,128]{1,0:T(8,128)S(1)} %join.4.token.refs_0_), channel_id=1, source_target_pairs={{0,64},{1,65},{2,66},{3,67},{4,68},{5,69},{6,70},{7,71},{8,72},{9,... | collective-permute-start | bytes 12296 | tf_op jit(solution)/shard_map/ppermute | solution.py:458
  24.3 7.3 %collective-permute-start.6 = (f32[8,128]{1,0:T(8,128)S(1)}, f32[8,128]{1,0:T(8,128)S(1)}, u32[]{:S(2)}, u32[]{:S(2)}) collective-permute-start(f32[8,128]{1,0:T(8,128)S(1)} %join.5.token.own), channel_id=1, source_target_pairs={{0,192},{1,193},{2,194},{3,195},{4,196},{5,197},{6,198},{7,199},{8... | collective-permute-start | bytes 12296 | tf_op jit(solution)/shard_map/ppermute | solution.py:458

commit v6 on v5

--- a/solution.py
+++ b/solution.py
@@ -25,6 +25,7 @@
         self.tiles = -(-det_cols // LANES)
         self.width = self.tiles * LANES
         self.pitch = frame_count + 1
+        self.lines = -(-(self.ext + 1) * self.pitch // 8) * 8
         self.tall = -(-band_height // 16) * 16
         self.packed = -(-(self.reach + 3) // 16) * 16
 
@@ -117,7 +118,7 @@
     return pl.pallas_call(
         functools.partial(prepare_kernel, size),
         out_shape=[
-            jax.ShapeDtypeStruct((size.tiles, size.ext * size.pitch, LANES), jnp.float32),
+            jax.ShapeDtypeStruct((size.tiles, size.lines, LANES), jnp.float32),
             jax.ShapeDtypeStruct((size.frames * size.tall, LANES), jnp.float32),
             jax.ShapeDtypeStruct((size.rows, size.width), jnp.float32),
             jax.ShapeDtypeStruct((size.packed, size.width), jnp.bfloat16),

time: 44.7 us -> 44.7 us (level)
  no operation moved by 1% of the time
where the time goes in v6:
time: 44.7 us; the launch traced here: 44.3 us
  Pallas kernels  15.8 us (35%)
  starting transfers between devices  15 us (34%)
  blocking collectives  11.8 us (26%)
  local copies, waits for them, and re-layouts  1.49 us (3%)
    ppermute x6, starting transfers between devices, body(): got.append([lax.ppermute(total, ('scan', 'band'), pairs) for pairs in step])  12.4 us
    all_to_all x1, blocking collectives, body(): blocks = lax.all_to_all(send, 'band', 0, 0)  11.8 us
    pallas_call x3, Pallas kernels, core_rows(): pl.pallas_call(functools.partial(core_kernel, size, first, last, before i...  7.44 us
    pallas_call x1, Pallas kernels, shift_frames(): pl.pallas_call(functools.partial(shift_kernel, size), out_shape=[jax.Shap...  3.66 us
    ppermute x1, starting transfers between devices, body(): second_got = lax.ppermute(labels_only, 'band', pairs)  2.58 us
    pallas_call x1, Pallas kernels, edge_rows(): pl.pallas_call(functools.partial(edge_kernel, size), out_shape=jax.ShapeD...  2.55 us
    unnamed x12, local copies, waits for them, and re-layouts  1.49 us
    pallas_call x1, Pallas kernels, prepare(): pl.pallas_call(functools.partial(prepare_kernel, size), out_shape=[jax.Sh...  1.29 us
  transfers between devices with their start and end apart: 7, of which 0 were waited for; matrix products, arithmetic and copies ran while one was open for 0% of the time, Pallas kernels for 23%

profile of v6, /device:TPU:6, one launch (start us, length us, event | category | flops | bytes accessed | tf_op | source)
XLA Modules:
  0.0 44.3 jit_solution(17235943437776530260)
XLA Ops:
  0.0 0.0 copy-start.4
  0.0 0.0 copy-start.5
  0.0 0.0 copy-start.3
  0.0 0.0 copy-start.2
  0.0 0.0 copy-start
  0.1 0.9 %copy-done.4 = s32[72,576]{1,0:T(8,128)S(1)} copy-done((s32[72,576]{1,0:T(8,128)S(1)}, s32[72,576]{1,0:T(8,128)}, u32[]{:S(2)}) %copy-start.4) | copy-done | bytes 165912
  0.9 0.0 copy-done.5
  0.9 1.3 %prepare.1 = (f32[5,5920,128]{2,1,0:T(8,128)S(1)}, f32[5120,128]{1,0:T(8,128)S(1)}, f32[72,640]{1,0:T(8,128)S(1)}, bf16[16,640]{1,0:T(8,128)(2,1)S(1)}) custom-call(bf16[80,256]{1,0:T(8,128)(2,1)S(1)} %diagonals.1.diagonal, f32[64,72]{1,0:T(8,128)S(1)} %copy-done.5, s32[72,576]{1,0:T(8,128)S(1)} %copy-done.4), custom_call_target="tpu_custom_call" | custom-call | flops 500000000 | bytes 1000000 | tf_op jit(solution)/shard_map/prepare/pallas_call | solution.py:118
  2.2 0.0 copy-done.3
  2.2 0.0 copy-done.2
  2.2 0.6 %copy-done = bf16[64,72,576]{2,1,0:T(8,128)(2,1)S(1)} copy-done((bf16[64,72,576]{2,1,0:T(8,128)(2,1)S(1)}, bf16[64,72,576]{2,1,0:T(8,128)(2,1)}, u32[]{:S(2)}) %copy-start) | copy-done | bytes 5308440
  2.8 3.7 %shift.1 = (f32[5,5920,128]{2,1,0:T(8,128)S(1)}, bf16[16,640]{1,0:T(8,128)(2,1)S(1)}) custom-call(s32[64]{0:T(128)S(1)} %copy-done.2, s32[64]{0:T(128)S(1)} %copy-done.3, f32[5120,128]{1,0:T(8,128)S(1)} %get-tuple-element.11.spread, bf16[64,72,576]{2,1,0:T(8,128)(2,1)S(1)} %copy-done, ...), custom_call_target="tpu_custom_call", output_to_operand_aliasing={{0}: (5, {})} | custom-call | flops 6000000000 | bytes 1000000 | tf_op jit(solution)/shard_map/shift/pallas_call | solution.py:187
  6.5 0.1 collective-permute-start
  6.6 2.6 %collective-permute-start.1 = (bf16[16,640]{1,0:T(8,128)(2,1)S(1)}, bf16[16,640]{1,0:T(8,128)(2,1)S(1)}, u32[]{:S(2)}, u32[]{:S(2)}) collective-permute-start(bf16[16,640]{1,0:T(8,128)(2,1)S(1)} %get-tuple-element.16), channel_id=1, source_target_pairs={{0,1},{1,0},{2,3},{3,2},{4,5},{5,4},{6,7},{7,6},{8,9},{9,8},{10,11... | collective-permute-start | bytes 61448 | tf_op jit(solution)/shard_map/ppermute | solution.py:454
  9.2 1.9 %core.3.token.refs_0_ = f32[384,64]{1,0:T(8,128)S(1)} custom-call(f32[5,5920,128]{2,1,0:T(8,128)S(1)} %get-tuple-element.14.moved, f32[72,640]{1,0:T(8,128)S(1)} %get-tuple-element.12.wide, bf16[16,640]{1,0:T(8,128)(2,1)S(1)} %get-tuple-element.15.token.own), custom_call_target="tpu_custom_call" | custom-call | flops 4000000000 | bytes 1000000 | tf_op jit(solution)/shard_map/core/pallas_call | solution.py:266
  11.0 0.0 collective-permute-done.other.first_got
  11.1 0.0 copy-start.1
  11.1 1.5 %collective-permute-start.4 = (f32[8,128]{1,0:T(8,128)S(1)}, f32[8,128]{1,0:T(8,128)S(1)}, u32[]{:S(2)}, u32[]{:S(2)}) collective-permute-start(f32[8,128]{1,0:T(8,128)S(1)} %join.3.token.refs_0_), channel_id=1, source_target_pairs={{0,32},{1,33},{2,34},{3,35},{4,36},{5,37},{6,38},{7,39},{8,40},{9,... | collective-permute-start | bytes 12296 | tf_op jit(solution)/shard_map/ppermute | solution.py:459
  12.6 0.0 collective-permute-start.3
  12.6 2.7 %collective-permute-start.2 = (f32[8,128]{1,0:T(8,128)S(1)}, f32[8,128]{1,0:T(8,128)S(1)}, u32[]{:S(2)}, u32[]{:S(2)}) collective-permute-start(f32[8,128]{1,0:T(8,128)S(1)} %join.3.token.refs_0_), channel_id=1, source_target_pairs={{0,48},{1,49},{2,50},{3,51},{4,52},{5,53},{6,54},{7,55},{8,56},{9,... | collective-permute-start | bytes 12296 | tf_op jit(solution)/shard_map/ppermute | solution.py:459
  15.3 2.8 %core.4.refs_4_.refs_0_ = f32[384,64]{1,0:T(8,128)S(1)} custom-call(f32[5,5920,128]{2,1,0:T(8,128)S(1)} %get-tuple-element.14.moved, f32[72,640]{1,0:T(8,128)S(1)} %get-tuple-element.12.wide, f32[8,128]{1,0:T(8,128)S(1)} %join.3.token.refs_0_, f32[384,64]{1,0:T(8,128)S(1)} %core.3.token.refs_0_), custom_call_target="tpu_custom_call" | custom-call | flops 4000000000 | bytes 1000000 | tf_op jit(solution)/shard_map/core/pallas_call | solution.py:266
  18.1 0.0 collective-permute-done.4.refs_3_
  18.1 0.0 collective-permute-done.3.refs_2_
  18.1 0.0 collective-permute-done.2.refs_1_
  18.1 3.4 %collective-permute-start.5 = (f32[8,128]{1,0:T(8,128)S(1)}, f32[8,128]{1,0:T(8,128)S(1)}, u32[]{:S(2)}, u32[]{:S(2)}) collective-permute-start(f32[8,128]{1,0:T(8,128)S(1)} %join.4.token.refs_0_), channel_id=1, source_target_pairs={{0,64},{1,65},{2,66},{3,67},{4,68},{5,69},{6,70},{7,71},{8,72},{9,... | collective-permute-start | bytes 12296 | tf_op jit(solution)/shard_map/ppermute | solution.py:459
  21.5 2.8 %core.5.refs_2_.before = f32[384,64]{1,0:T(8,128)S(1)} custom-call(f32[5,5920,128]{2,1,0:T(8,128)S(1)} %get-tuple-element.14.moved, f32[72,640]{1,0:T(8,128)S(1)} %get-tuple-element.12.wide, f32[8,128]{1,0:T(8,128)S(1)} %join.4.token.refs_0_, f32[384,64]{1,0:T(8,128)S(1)} %core.4.refs_4_.refs_0_), custom_call_target="tpu_custom_call" | custom-call | flops 4000000000 | bytes 1000000 | tf_op jit(solution)/shard_map/core/pallas_call | solution.py:266
  24.3 0.0 collective-permute-done.5.refs_1_
  24.3 4.7 %collective-permute-start.6 = (f32[8,128]{1,0:T(8,128)S(1)}, f32[8,128]{1,0:T(8,128)S(1)}, u32[]{:S(2)}, u32[]{:S(2)}) collective-permute-start(f32[8,128]{1,0:T(8,128)S(1)} %join.5.token.own), channel_id=1, source_target_pairs={{0,192},{1,193},{2,194},{3,195},{4,196},{5,197},{6,198},{7,199},{8... | collective-permute-start | bytes 12296 | tf_op jit(solution)/shard_map/ppermute | solution.py:459
  29.0 0.0 collective-permute-done.1.second_got
  29.0 0.0 copy-done.1
  29.0 2.6 %edge.1.send = f32[8,40,128]{2,1,0:T(8,128)S(1)} custom-call(f32[5,5920,128]{2,1,0:T(8,128)S(1)} %get-tuple-element.14.moved, bf16[16,640]{1,0:T(8,128)(2,1)S(1)} %collective-permute-done.other.first_got, bf16[16,640]{1,0:T(8,128)(2,1)S(1)} %collective-permute-done.1.second_got, f32[8,128]{1,0:T(8,128)S(1)} %join.5.token.own, ...), custom_call_target="tpu_custom_call" | custom-call | flops 4000000000 | bytes 1000000 | tf_op jit(solution)/shard_map/edge/pallas_call | solution.py:326
  31.6 0.0 collective-permute-done.6.other
  31.6 11.8 %all_to_all.5.blocks = f32[8,40,128]{2,1,0:T(8,128)S(1)} all-to-all(f32[8,40,128]{2,1,0:T(8,128)S(1)} %put.1), channel_id=1, replica_groups=mesh['scan'=32,'band'=8] {'band'}, dimensions={0} | all-to-all | bytes 327680 | tf_op jit(solution)/shard_map/all_to_all | solution.py:466
  43.5 0.8 %finish.1 = f32[64,64]{1,0:T(8,128)} custom-call(f32[8,40,128]{2,1,0:T(8,128)S(1)} %all_to_all.5.blocks), custom_call_target="tpu_custom_call" | custom-call | tf_op jit(solution)/shard_map/finish/pallas_call | solution.py:399
  (5 shorter events, 0.0 us)
Async XLA Ops:
  0.0 0.9 %copy-start.4 = (s32[72,576]{1,0:T(8,128)S(1)}, s32[72,576]{1,0:T(8,128)}, u32[]{:S(2)}) copy-start(s32[72,576]{1,0:T(8,128)} %labels.1) | copy-start | bytes 497668
  0.0 0.9 %copy-start.5 = (f32[64,72]{1,0:T(8,128)S(1)}, f32[64,72]{1,0:T(8,128)}, u32[]{:S(2)}) copy-start(f32[64,72]{1,0:T(8,128)} %scales.1) | copy-start | bytes 55300
  0.0 2.2 %copy-start.3 = (s32[64]{0:T(128)S(1)}, s32[64]{0:T(128)}, u32[]{:S(2)}) copy-start(s32[64]{0:T(128)} %col_shift.1) | copy-start | bytes 772
  0.0 2.2 %copy-start.2 = (s32[64]{0:T(128)S(1)}, s32[64]{0:T(128)}, u32[]{:S(2)}) copy-start(s32[64]{0:T(128)} %row_shift.1) | copy-start | bytes 772
  0.0 2.8 %copy-start = (bf16[64,72,576]{2,1,0:T(8,128)(2,1)S(1)}, bf16[64,72,576]{2,1,0:T(8,128)(2,1)}, u32[]{:S(2)}) copy-start(bf16[64,72,576]{2,1,0:T(8,128)(2,1)} %codes.1) | copy-start | bytes 15925252
  6.5 4.6 %collective-permute-start = (bf16[16,640]{1,0:T(8,128)(2,1)S(1)}, bf16[16,640]{1,0:T(8,128)(2,1)S(1)}, u32[]{:S(2)}, u32[]{:S(2)}) collective-permute-start(bf16[16,640]{1,0:T(8,128)(2,1)S(1)} %get-tuple-element.15.token.own), channel_id=1, source_target_pairs={{0,8},{1,10},{2,9},{3,12},{4,11},{5,14},{6,13},{7,15},{8,0},{9,2},... | collective-permute-start | bytes 61448 | tf_op jit(solution)/shard_map/ppermute | solution.py:459
  6.6 22.5 %collective-permute-start.1 = (bf16[16,640]{1,0:T(8,128)(2,1)S(1)}, bf16[16,640]{1,0:T(8,128)(2,1)S(1)}, u32[]{:S(2)}, u32[]{:S(2)}) collective-permute-start(bf16[16,640]{1,0:T(8,128)(2,1)S(1)} %get-tuple-element.16), channel_id=1, source_target_pairs={{0,1},{1,0},{2,3},{3,2},{4,5},{5,4},{6,7},{7,6},{8,9},{9,8},{10,11... | collective-permute-start | bytes 61448 | tf_op jit(solution)/shard_map/ppermute | solution.py:454
  11.1 18.0 %copy-start.1 = (f32[3,128,512]{2,1,0:T(8,128)S(1)}, f32[3,128,512]{2,1,0:T(8,128)}, u32[]{:S(2)}) copy-start(f32[3,128,512]{2,1,0:T(8,128)} %param.11) | copy-start | bytes 2359300
  11.1 7.0 %collective-permute-start.4 = (f32[8,128]{1,0:T(8,128)S(1)}, f32[8,128]{1,0:T(8,128)S(1)}, u32[]{:S(2)}, u32[]{:S(2)}) collective-permute-start(f32[8,128]{1,0:T(8,128)S(1)} %join.3.token.refs_0_), channel_id=1, source_target_pairs={{0,32},{1,33},{2,34},{3,35},{4,36},{5,37},{6,38},{7,39},{8,40},{9,... | collective-permute-start | bytes 12296 | tf_op jit(solution)/shard_map/ppermute | solution.py:459
  12.6 5.5 %collective-permute-start.3 = (f32[8,128]{1,0:T(8,128)S(1)}, f32[8,128]{1,0:T(8,128)S(1)}, u32[]{:S(2)}, u32[]{:S(2)}) collective-permute-start(f32[8,128]{1,0:T(8,128)S(1)} %join.3.token.refs_0_), channel_id=1, source_target_pairs={{0,16},{1,17},{2,18},{3,19},{4,20},{5,21},{6,22},{7,23},{8,24},{9,... | collective-permute-start | bytes 12296 | tf_op jit(solution)/shard_map/ppermute | solution.py:459
  12.6 5.5 %collective-permute-start.2 = (f32[8,128]{1,0:T(8,128)S(1)}, f32[8,128]{1,0:T(8,128)S(1)}, u32[]{:S(2)}, u32[]{:S(2)}) collective-permute-start(f32[8,128]{1,0:T(8,128)S(1)} %join.3.token.refs_0_), channel_id=1, source_target_pairs={{0,48},{1,49},{2,50},{3,51},{4,52},{5,53},{6,54},{7,55},{8,56},{9,... | collective-permute-start | bytes 12296 | tf_op jit(solution)/shard_map/ppermute | solution.py:459
  18.1 6.2 %collective-permute-start.5 = (f32[8,128]{1,0:T(8,128)S(1)}, f32[8,128]{1,0:T(8,128)S(1)}, u32[]{:S(2)}, u32[]{:S(2)}) collective-permute-start(f32[8,128]{1,0:T(8,128)S(1)} %join.4.token.refs_0_), channel_id=1, source_target_pairs={{0,64},{1,65},{2,66},{3,67},{4,68},{5,69},{6,70},{7,71},{8,72},{9,... | collective-permute-start | bytes 12296 | tf_op jit(solution)/shard_map/ppermute | solution.py:459
  24.3 7.3 %collective-permute-start.6 = (f32[8,128]{1,0:T(8,128)S(1)}, f32[8,128]{1,0:T(8,128)S(1)}, u32[]{:S(2)}, u32[]{:S(2)}) collective-permute-start(f32[8,128]{1,0:T(8,128)S(1)} %join.5.token.own), channel_id=1, source_target_pairs={{0,192},{1,193},{2,194},{3,195},{4,196},{5,197},{6,198},{7,199},{8... | collective-permute-start | bytes 12296 | tf_op jit(solution)/shard_map/ppermute | solution.py:459

commit v7 on v6

--- a/solution.py
+++ b/solution.py
@@ -429,7 +429,7 @@
 
     moves = [
         [(lambda s: s ^ 1, lower_pair)],
-        [(x_around, same), (lambda s: s ^ 2, same), (lambda s: s ^ 4, same)],
+        [(lambda s: s ^ 4, same), (lambda s: s ^ 2, same), (x_around, same)],
         [(lambda s: s ^ 8, same)],
         [(z_around, same)],
     ]

time: 44.7 us -> 45.8 us (1.025); the launches traced: 44.3 us -> 44.9 us
  starting transfers between devices: 15 us -> 15.6 us
    ppermute x6, starting transfers between devices: 12.4 us -> 13 us  [body(): got.append([lax.ppermute(total, ('scan', 'band'), pairs) for pairs in step])]
  transfers between devices with their start and end apart: 7 -> 7, of which waited for: 0 -> 0; matrix products, arithmetic and copies ran while one was open for 0% -> 0% of each run, Pallas kernels for 23% -> 22%
where the time goes in v7:
time: 45.8 us; the launch traced here: 44.9 us
  Pallas kernels  15.8 us (34%)
  starting transfers between devices  15.6 us (34%)
  blocking collectives  11.8 us (26%)
  local copies, waits for them, and re-layouts  1.49 us (3%)
    ppermute x6, starting transfers between devices, body(): got.append([lax.ppermute(total, ('scan', 'band'), pairs) for pairs in step])  13 us
    all_to_all x1, blocking collectives, body(): blocks = lax.all_to_all(send, 'band', 0, 0)  11.8 us
    pallas_call x3, Pallas kernels, core_rows(): pl.pallas_call(functools.partial(core_kernel, size, first, last, before i...  7.45 us
    pallas_call x1, Pallas kernels, shift_frames(): pl.pallas_call(functools.partial(shift_kernel, size), out_shape=[jax.Shap...  3.66 us
    ppermute x1, starting transfers between devices, body(): second_got = lax.ppermute(labels_only, 'band', pairs)  2.58 us
    pallas_call x1, Pallas kernels, edge_rows(): pl.pallas_call(functools.partial(edge_kernel, size), out_shape=jax.ShapeD...  2.55 us
    unnamed x12, local copies, waits for them, and re-layouts  1.49 us
    pallas_call x1, Pallas kernels, prepare(): pl.pallas_call(functools.partial(prepare_kernel, size), out_shape=[jax.Sh...  1.29 us
  transfers between devices with their start and end apart: 7, of which 0 were waited for; matrix products, arithmetic and copies ran while one was open for 0% of the time, Pallas kernels for 22%

profile of v7, /device:TPU:6, one launch (start us, length us, event | category | flops | bytes accessed | tf_op | source)
XLA Modules:
  0.0 44.9 jit_solution(296275915042574696)
XLA Ops:
  0.0 0.0 copy-start.4
  0.0 0.0 copy-start.5
  0.0 0.0 copy-start.3
  0.0 0.0 copy-start.2
  0.0 0.0 copy-start
  0.1 0.9 %copy-done.4 = s32[72,576]{1,0:T(8,128)S(1)} copy-done((s32[72,576]{1,0:T(8,128)S(1)}, s32[72,576]{1,0:T(8,128)}, u32[]{:S(2)}) %copy-start.4) | copy-done | bytes 165912
  0.9 0.0 copy-done.5
  0.9 1.3 %prepare.1 = (f32[5,5920,128]{2,1,0:T(8,128)S(1)}, f32[5120,128]{1,0:T(8,128)S(1)}, f32[72,640]{1,0:T(8,128)S(1)}, bf16[16,640]{1,0:T(8,128)(2,1)S(1)}) custom-call(bf16[80,256]{1,0:T(8,128)(2,1)S(1)} %diagonals.1.diagonal, f32[64,72]{1,0:T(8,128)S(1)} %copy-done.5, s32[72,576]{1,0:T(8,128)S(1)} %copy-done.4), custom_call_target="tpu_custom_call" | custom-call | flops 500000000 | bytes 1000000 | tf_op jit(solution)/shard_map/prepare/pallas_call | solution.py:118
  2.2 0.0 copy-done.3
  2.2 0.0 copy-done.2
  2.2 0.6 %copy-done = bf16[64,72,576]{2,1,0:T(8,128)(2,1)S(1)} copy-done((bf16[64,72,576]{2,1,0:T(8,128)(2,1)S(1)}, bf16[64,72,576]{2,1,0:T(8,128)(2,1)}, u32[]{:S(2)}) %copy-start) | copy-done | bytes 5308440
  2.8 3.7 %shift.1 = (f32[5,5920,128]{2,1,0:T(8,128)S(1)}, bf16[16,640]{1,0:T(8,128)(2,1)S(1)}) custom-call(s32[64]{0:T(128)S(1)} %copy-done.2, s32[64]{0:T(128)S(1)} %copy-done.3, f32[5120,128]{1,0:T(8,128)S(1)} %get-tuple-element.11.spread, bf16[64,72,576]{2,1,0:T(8,128)(2,1)S(1)} %copy-done, ...), custom_call_target="tpu_custom_call", output_to_operand_aliasing={{0}: (5, {})} | custom-call | flops 6000000000 | bytes 1000000 | tf_op jit(solution)/shard_map/shift/pallas_call | solution.py:187
  6.5 0.1 collective-permute-start
  6.6 2.6 %collective-permute-start.1 = (bf16[16,640]{1,0:T(8,128)(2,1)S(1)}, bf16[16,640]{1,0:T(8,128)(2,1)S(1)}, u32[]{:S(2)}, u32[]{:S(2)}) collective-permute-start(bf16[16,640]{1,0:T(8,128)(2,1)S(1)} %get-tuple-element.16), channel_id=1, source_target_pairs={{0,1},{1,0},{2,3},{3,2},{4,5},{5,4},{6,7},{7,6},{8,9},{9,8},{10,11... | collective-permute-start | bytes 61448 | tf_op jit(solution)/shard_map/ppermute | solution.py:454
  9.2 1.9 %core.3.token.refs_0_ = f32[384,64]{1,0:T(8,128)S(1)} custom-call(f32[5,5920,128]{2,1,0:T(8,128)S(1)} %get-tuple-element.14.moved, f32[72,640]{1,0:T(8,128)S(1)} %get-tuple-element.12.wide, bf16[16,640]{1,0:T(8,128)(2,1)S(1)} %get-tuple-element.15.token.own), custom_call_target="tpu_custom_call" | custom-call | flops 4000000000 | bytes 1000000 | tf_op jit(solution)/shard_map/core/pallas_call | solution.py:266
  11.0 0.0 collective-permute-done.other.first_got
  11.1 0.0 copy-start.1
  11.1 0.6 %collective-permute-start.4 = (f32[8,128]{1,0:T(8,128)S(1)}, f32[8,128]{1,0:T(8,128)S(1)}, u32[]{:S(2)}, u32[]{:S(2)}) collective-permute-start(f32[8,128]{1,0:T(8,128)S(1)} %join.3.token.refs_0_), channel_id=1, source_target_pairs={{0,48},{1,49},{2,50},{3,51},{4,52},{5,53},{6,54},{7,55},{8,56},{9,... | collective-permute-start | bytes 12296 | tf_op jit(solution)/shard_map/ppermute | solution.py:459
  11.7 0.9 %collective-permute-start.3 = (f32[8,128]{1,0:T(8,128)S(1)}, f32[8,128]{1,0:T(8,128)S(1)}, u32[]{:S(2)}, u32[]{:S(2)}) collective-permute-start(f32[8,128]{1,0:T(8,128)S(1)} %join.3.token.refs_0_), channel_id=1, source_target_pairs={{0,16},{1,17},{2,18},{3,19},{4,20},{5,21},{6,22},{7,23},{8,24},{9,... | collective-permute-start | bytes 12296 | tf_op jit(solution)/shard_map/ppermute | solution.py:459
  12.5 3.4 %collective-permute-start.2 = (f32[8,128]{1,0:T(8,128)S(1)}, f32[8,128]{1,0:T(8,128)S(1)}, u32[]{:S(2)}, u32[]{:S(2)}) collective-permute-start(f32[8,128]{1,0:T(8,128)S(1)} %join.3.token.refs_0_), channel_id=1, source_target_pairs={{0,32},{1,33},{2,34},{3,35},{4,36},{5,37},{6,38},{7,39},{8,40},{9,... | collective-permute-start | bytes 12296 | tf_op jit(solution)/shard_map/ppermute | solution.py:459
  15.9 2.8 %core.4.refs_4_.refs_0_ = f32[384,64]{1,0:T(8,128)S(1)} custom-call(f32[5,5920,128]{2,1,0:T(8,128)S(1)} %get-tuple-element.14.moved, f32[72,640]{1,0:T(8,128)S(1)} %get-tuple-element.12.wide, f32[8,128]{1,0:T(8,128)S(1)} %join.3.token.refs_0_, f32[384,64]{1,0:T(8,128)S(1)} %core.3.token.refs_0_), custom_call_target="tpu_custom_call" | custom-call | flops 4000000000 | bytes 1000000 | tf_op jit(solution)/shard_map/core/pallas_call | solution.py:266
  18.7 0.0 collective-permute-done.4.refs_3_
  18.7 0.0 collective-permute-done.3.refs_2_
  18.7 0.0 collective-permute-done.2.refs_1_
  18.8 3.4 %collective-permute-start.5 = (f32[8,128]{1,0:T(8,128)S(1)}, f32[8,128]{1,0:T(8,128)S(1)}, u32[]{:S(2)}, u32[]{:S(2)}) collective-permute-start(f32[8,128]{1,0:T(8,128)S(1)} %join.4.token.refs_0_), channel_id=1, source_target_pairs={{0,64},{1,65},{2,66},{3,67},{4,68},{5,69},{6,70},{7,71},{8,72},{9,... | collective-permute-start | bytes 12296 | tf_op jit(solution)/shard_map/ppermute | solution.py:459
  22.1 2.8 %core.5.refs_2_.before = f32[384,64]{1,0:T(8,128)S(1)} custom-call(f32[5,5920,128]{2,1,0:T(8,128)S(1)} %get-tuple-element.14.moved, f32[72,640]{1,0:T(8,128)S(1)} %get-tuple-element.12.wide, f32[8,128]{1,0:T(8,128)S(1)} %join.4.token.refs_0_, f32[384,64]{1,0:T(8,128)S(1)} %core.4.refs_4_.refs_0_), custom_call_target="tpu_custom_call" | custom-call | flops 4000000000 | bytes 1000000 | tf_op jit(solution)/shard_map/core/pallas_call | solution.py:266
  24.9 0.0 collective-permute-done.5.refs_1_
  24.9 4.7 %collective-permute-start.6 = (f32[8,128]{1,0:T(8,128)S(1)}, f32[8,128]{1,0:T(8,128)S(1)}, u32[]{:S(2)}, u32[]{:S(2)}) collective-permute-start(f32[8,128]{1,0:T(8,128)S(1)} %join.5.token.own), channel_id=1, source_target_pairs={{0,192},{1,193},{2,194},{3,195},{4,196},{5,197},{6,198},{7,199},{8... | collective-permute-start | bytes 12296 | tf_op jit(solution)/shard_map/ppermute | solution.py:459
  29.7 0.0 collective-permute-done.1.second_got
  29.7 0.0 copy-done.1
  29.7 2.6 %edge.1.send = f32[8,40,128]{2,1,0:T(8,128)S(1)} custom-call(f32[5,5920,128]{2,1,0:T(8,128)S(1)} %get-tuple-element.14.moved, bf16[16,640]{1,0:T(8,128)(2,1)S(1)} %collective-permute-done.other.first_got, bf16[16,640]{1,0:T(8,128)(2,1)S(1)} %collective-permute-done.1.second_got, f32[8,128]{1,0:T(8,128)S(1)} %join.5.token.own, ...), custom_call_target="tpu_custom_call" | custom-call | flops 4000000000 | bytes 1000000 | tf_op jit(solution)/shard_map/edge/pallas_call | solution.py:326
  32.2 0.0 collective-permute-done.6.other
  32.2 11.8 %all_to_all.5.blocks = f32[8,40,128]{2,1,0:T(8,128)S(1)} all-to-all(f32[8,40,128]{2,1,0:T(8,128)S(1)} %put.1), channel_id=1, replica_groups=mesh['scan'=32,'band'=8] {'band'}, dimensions={0} | all-to-all | bytes 327680 | tf_op jit(solution)/shard_map/all_to_all | solution.py:466
  44.1 0.8 %finish.1 = f32[64,64]{1,0:T(8,128)} custom-call(f32[8,40,128]{2,1,0:T(8,128)S(1)} %all_to_all.5.blocks), custom_call_target="tpu_custom_call" | custom-call | tf_op jit(solution)/shard_map/finish/pallas_call | solution.py:399
  (5 shorter events, 0.0 us)
Async XLA Ops:
  0.0 0.9 %copy-start.4 = (s32[72,576]{1,0:T(8,128)S(1)}, s32[72,576]{1,0:T(8,128)}, u32[]{:S(2)}) copy-start(s32[72,576]{1,0:T(8,128)} %labels.1) | copy-start | bytes 497668
  0.0 0.9 %copy-start.5 = (f32[64,72]{1,0:T(8,128)S(1)}, f32[64,72]{1,0:T(8,128)}, u32[]{:S(2)}) copy-start(f32[64,72]{1,0:T(8,128)} %scales.1) | copy-start | bytes 55300
  0.0 2.2 %copy-start.3 = (s32[64]{0:T(128)S(1)}, s32[64]{0:T(128)}, u32[]{:S(2)}) copy-start(s32[64]{0:T(128)} %col_shift.1) | copy-start | bytes 772
  0.0 2.2 %copy-start.2 = (s32[64]{0:T(128)S(1)}, s32[64]{0:T(128)}, u32[]{:S(2)}) copy-start(s32[64]{0:T(128)} %row_shift.1) | copy-start | bytes 772
  0.0 2.8 %copy-start = (bf16[64,72,576]{2,1,0:T(8,128)(2,1)S(1)}, bf16[64,72,576]{2,1,0:T(8,128)(2,1)}, u32[]{:S(2)}) copy-start(bf16[64,72,576]{2,1,0:T(8,128)(2,1)} %codes.1) | copy-start | bytes 15925252
  6.5 4.6 %collective-permute-start = (bf16[16,640]{1,0:T(8,128)(2,1)S(1)}, bf16[16,640]{1,0:T(8,128)(2,1)S(1)}, u32[]{:S(2)}, u32[]{:S(2)}) collective-permute-start(bf16[16,640]{1,0:T(8,128)(2,1)S(1)} %get-tuple-element.15.token.own), channel_id=1, source_target_pairs={{0,8},{1,10},{2,9},{3,12},{4,11},{5,14},{6,13},{7,15},{8,0},{9,2},... | collective-permute-start | bytes 61448 | tf_op jit(solution)/shard_map/ppermute | solution.py:459
  6.6 23.1 %collective-permute-start.1 = (bf16[16,640]{1,0:T(8,128)(2,1)S(1)}, bf16[16,640]{1,0:T(8,128)(2,1)S(1)}, u32[]{:S(2)}, u32[]{:S(2)}) collective-permute-start(bf16[16,640]{1,0:T(8,128)(2,1)S(1)} %get-tuple-element.16), channel_id=1, source_target_pairs={{0,1},{1,0},{2,3},{3,2},{4,5},{5,4},{6,7},{7,6},{8,9},{9,8},{10,11... | collective-permute-start | bytes 61448 | tf_op jit(solution)/shard_map/ppermute | solution.py:454
  11.1 18.6 %copy-start.1 = (f32[3,128,512]{2,1,0:T(8,128)S(1)}, f32[3,128,512]{2,1,0:T(8,128)}, u32[]{:S(2)}) copy-start(f32[3,128,512]{2,1,0:T(8,128)} %param.11) | copy-start | bytes 2359300
  11.1 7.6 %collective-permute-start.4 = (f32[8,128]{1,0:T(8,128)S(1)}, f32[8,128]{1,0:T(8,128)S(1)}, u32[]{:S(2)}, u32[]{:S(2)}) collective-permute-start(f32[8,128]{1,0:T(8,128)S(1)} %join.3.token.refs_0_), channel_id=1, source_target_pairs={{0,48},{1,49},{2,50},{3,51},{4,52},{5,53},{6,54},{7,55},{8,56},{9,... | collective-permute-start | bytes 12296 | tf_op jit(solution)/shard_map/ppermute | solution.py:459
  11.7 7.1 %collective-permute-start.3 = (f32[8,128]{1,0:T(8,128)S(1)}, f32[8,128]{1,0:T(8,128)S(1)}, u32[]{:S(2)}, u32[]{:S(2)}) collective-permute-start(f32[8,128]{1,0:T(8,128)S(1)} %join.3.token.refs_0_), channel_id=1, source_target_pairs={{0,16},{1,17},{2,18},{3,19},{4,20},{5,21},{6,22},{7,23},{8,24},{9,... | collective-permute-start | bytes 12296 | tf_op jit(solution)/shard_map/ppermute | solution.py:459
  12.5 6.2 %collective-permute-start.2 = (f32[8,128]{1,0:T(8,128)S(1)}, f32[8,128]{1,0:T(8,128)S(1)}, u32[]{:S(2)}, u32[]{:S(2)}) collective-permute-start(f32[8,128]{1,0:T(8,128)S(1)} %join.3.token.refs_0_), channel_id=1, source_target_pairs={{0,32},{1,33},{2,34},{3,35},{4,36},{5,37},{6,38},{7,39},{8,40},{9,... | collective-permute-start | bytes 12296 | tf_op jit(solution)/shard_map/ppermute | solution.py:459
  18.8 6.2 %collective-permute-start.5 = (f32[8,128]{1,0:T(8,128)S(1)}, f32[8,128]{1,0:T(8,128)S(1)}, u32[]{:S(2)}, u32[]{:S(2)}) collective-permute-start(f32[8,128]{1,0:T(8,128)S(1)} %join.4.token.refs_0_), channel_id=1, source_target_pairs={{0,64},{1,65},{2,66},{3,67},{4,68},{5,69},{6,70},{7,71},{8,72},{9,... | collective-permute-start | bytes 12296 | tf_op jit(solution)/shard_map/ppermute | solution.py:459
  24.9 7.3 %collective-permute-start.6 = (f32[8,128]{1,0:T(8,128)S(1)}, f32[8,128]{1,0:T(8,128)S(1)}, u32[]{:S(2)}, u32[]{:S(2)}) collective-permute-start(f32[8,128]{1,0:T(8,128)S(1)} %join.5.token.own), channel_id=1, source_target_pairs={{0,192},{1,193},{2,194},{3,195},{4,196},{5,197},{6,198},{7,199},{8... | collective-permute-start | bytes 12296 | tf_op jit(solution)/shard_map/ppermute | solution.py:459
